TPU v7x, 1024 devices: a whole 4x8x16 slice. The times are simulated.
1024 devices in a mesh: band: 256 (over z, y, core), lon: 4 (over x).
Axes of the slice: x: 4, y: 8, z: 16, core: 2. Of those that a mesh axis runs over, the one named last changes fastest.
Arguments:
- grid_state: bfloat16 [131072, 512], P(('band', 'lon')), may hold values from -6 to 6
- mesh_state: bfloat16 [16384, 512], P(('band', 'lon')), may hold values from -6 to 6
- edge_weights: bfloat16 [3, 3, 512, 512], replicated, may hold values from -0.25 to 0.25
- node_weights: bfloat16 [3, 3, 512, 512], replicated, may hold values from -0.25 to 0.25
- enc_recv: int32 [131072, 2], P(('band', 'lon')), may hold values from 0 to 16383, as said below
- proc_send: int32 [16384, 6], P(('band', 'lon')), may hold values from 0 to 16383, as said below
- long_send: int32 [1024, 6], P(('band', 'lon')), may hold values from 0 to 1023, as said below
- dec_send: int32 [131072, 3], P(('band', 'lon')), may hold values from 0 to 16383, as said below
Outputs:
- grid_out: bfloat16 [131072, 512], P(('band', 'lon'))
- mesh_two: bfloat16 [16384, 512], P(('band', 'lon'))
Inputs may be any that keep to these rules, and one draw needn't show every extreme that they name: enc_recv[g, k] is a mesh node of band g // 512 or of a band beside it, the band of node m being m // 64. proc_send[m, k] is a node of band m // 64 or of a band beside it. long_send[c, j] is a coarse node of band c // 4 or of a band beside it, the band of coarse node c being c // 4. dec_send[g, k] is a mesh node of band g // 512 or of a band beside it.
All inputs are finite; a program needn't handle non-finite values.
Results may differ from a plain program's by a relative error of at most 0.019.
Values may be sent and summed in bfloat16 or wider, within the bound.
No kernel may reach another device: no remote copies, remote signals or barrier semaphores. Data moves between devices by JAX's collectives and lax.ppermute only.
A program may use at most 32 MiB of HBM per device.

v0:
```python
import jax
import jax.numpy as jnp
from jax import lax
from jax.sharding import PartitionSpec as P


def extended(block, sides, width):
    for axis, dim in sides:
        count = lax.axis_size(axis)
        forward = [(i, i + 1) for i in range(count - 1)]
        backward = [(target, source) for source, target in forward]
        low = lax.ppermute(
            lax.slice_in_dim(block, block.shape[dim] - width, None, axis=dim), axis, forward
        )
        high = lax.ppermute(lax.slice_in_dim(block, 0, width, axis=dim), axis, backward)
        block = jnp.concatenate([low, block, high], axis=dim)
    return block


def from_behind(x, axis, by):
    count = lax.axis_size(axis)
    pairs = [(i, i + by) for i in range(count) if 0 <= i + by < count]
    return lax.ppermute(x, axis, pairs)


def layer_norm(values):
    average = jnp.mean(values, axis=-1, keepdims=True)
    centred = values - average
    spread = jnp.mean(centred * centred, axis=-1, keepdims=True)
    return centred * lax.rsqrt(spread + 1e-05)


def edge_messages(before, out_weights):
    hidden = jax.nn.silu(before).astype(jnp.bfloat16)
    shaped = hidden.reshape(-1, hidden.shape[-1])
    result = layer_norm(jnp.dot(shaped, out_weights, preferred_element_type=jnp.float32))
    return result.reshape(before.shape)


def node_update(state, aggregate, weights):
    inner = jnp.dot(state, weights[0], preferred_element_type=jnp.float32)
    inner = inner + jnp.dot(
        aggregate.astype(jnp.bfloat16), weights[1], preferred_element_type=jnp.float32
    )
    hidden = jax.nn.silu(inner).astype(jnp.bfloat16)
    outer = layer_norm(jnp.dot(hidden, weights[2], preferred_element_type=jnp.float32))
    return (state.astype(jnp.float32) + outer).astype(jnp.bfloat16)


def collect(state):
    lon_rows = lax.all_gather(state, "lon", axis=0, tiled=True)
    return extended(lon_rows, (("band", 0),), lon_rows.shape[0])


def per_device(
    grid_state, mesh_state, edge_weights, node_weights, enc_recv, proc_send, long_send, dec_send
):
    width = grid_state.shape[1]
    mesh_rows = mesh_state.shape[0]
    band_rows = mesh_rows * lax.axis_size("lon")
    table_start = (lax.axis_index("band") - 1) * band_rows
    table_zero = collect(mesh_state)
    recv_table = jnp.dot(table_zero, edge_weights[0, 1], preferred_element_type=jnp.float32)
    sent_proj = jnp.dot(grid_state, edge_weights[0, 0], preferred_element_type=jnp.float32)
    local_recv = enc_recv - table_start
    messages = edge_messages(sent_proj[:, None, :] + recv_table[local_recv], edge_weights[0, 2])
    partial_value = jax.ops.segment_sum(
        messages.reshape(-1, width), local_recv.reshape(-1), num_segments=3 * band_rows
    )
    pieces = partial_value.reshape(3, band_rows, width)
    running = pieces[1]
    for offset, source in ((1, 2), (-1, 0)):
        running = running + from_behind(pieces[source].astype(jnp.bfloat16), "band", offset).astype(
            jnp.float32
        )
    enc_sum = lax.psum_scatter(
        running.astype(jnp.bfloat16), "lon", scatter_dimension=0, tiled=True
    ).astype(jnp.float32)
    mesh_one = node_update(mesh_state, enc_sum, node_weights[0])
    table_one = collect(mesh_one)
    send_table = jnp.dot(table_one, edge_weights[1, 0], preferred_element_type=jnp.float32)
    recv_mesh = jnp.dot(mesh_one, edge_weights[1, 1], preferred_element_type=jnp.float32)
    proc_sum = jnp.sum(
        edge_messages(
            send_table[proc_send - table_start] + recv_mesh[:, None, :], edge_weights[1, 2]
        ),
        axis=1,
    )
    far_before = send_table[long_send * mesh_rows - table_start] + recv_mesh[:1][:, None, :]
    far_sum = jnp.sum(edge_messages(far_before, edge_weights[1, 2]), axis=1)
    proc_sum = proc_sum.at[0:1].add(far_sum)
    mesh_two = node_update(mesh_one, proc_sum, node_weights[1])
    table_two = collect(mesh_two)
    send_two = jnp.dot(table_two, edge_weights[2, 0], preferred_element_type=jnp.float32)
    recv_grid = jnp.dot(grid_state, edge_weights[2, 1], preferred_element_type=jnp.float32)
    dec_before = send_two[dec_send - table_start] + recv_grid[:, None, :]
    dec_sum = jnp.sum(edge_messages(dec_before, edge_weights[2, 2]), axis=1)
    grid_out = node_update(grid_state, dec_sum, node_weights[2])
    return (grid_out, mesh_two)


def solution(mesh):
    in_specs = (
        P(("band", "lon"), None),
        P(("band", "lon"), None),
        P(),
        P(),
        P(("band", "lon"), None),
        P(("band", "lon"), None),
        P(("band", "lon"), None),
        P(("band", "lon"), None),
    )
    out_specs = (P(("band", "lon"), None), P(("band", "lon"), None))
    return jax.shard_map(
        per_device, mesh=mesh, in_specs=in_specs, out_specs=out_specs, check_vma=False
    )
```

profile of v0, /device:TPU:249, one launch (start us, length us, event | category | flops | bytes accessed | tf_op | source)
XLA Modules:
  0.0 164.7 jit_solution(11368866744413187530)
XLA Ops:
  7.2 9.5 %all_gather.9 = bf16[64,512]{1,0:T(8,128)(2,1)S(1)} all-gather(bf16[16,512]{1,0:T(8,128)(2,1)} %param.11), channel_id=1, replica_groups=mesh['band'=256,'lon'=4] {'lon'}, dimensions={0}, use_global_device_ids=true | all-gather | bytes 81920 | tf_op jit(solution)/shard_map/all_gather | solution.py:51
  16.7 7.9 %collective-permute-start = (bf16[64,512]{1,0:T(8,128)(2,1)S(1)}, bf16[64,512]{1,0:T(8,128)(2,1)S(1)}, u32[]{:S(2)}, u32[]{:S(2)}) collective-permute-start(bf16[64,512]{1,0:T(8,128)(2,1)S(1)} %all_gather.9), channel_id=1, source_target_pairs={{0,4},{4,8},{8,12},{12,16},{16,20},{20,24},{24,28},{28,32},{32,36}... | collective-permute-start | bytes 196616 | tf_op jit(solution)/shard_map/ppermute | solution.py:12
  24.6 1.9 %collective-permute-start.1 = (bf16[64,512]{1,0:T(8,128)(2,1)S(1)}, bf16[64,512]{1,0:T(8,128)(2,1)S(1)}, u32[]{:S(2)}, u32[]{:S(2)}) collective-permute-start(bf16[64,512]{1,0:T(8,128)(2,1)S(1)} %all_gather.9), channel_id=1, source_target_pairs={{4,0},{8,4},{12,8},{16,12},{20,16},{24,20},{28,24},{32,28},{36,32}... | collective-permute-start | bytes 196616 | tf_op jit(solution)/shard_map/ppermute | solution.py:15
  30.5 1.4 fusion.34
  37.8 1.4 fusion.109
  39.4 2.3 %scatter_custom_fusion = f32[192,512]{1,0:T(8,128)S(1)} fusion(s32[256]{0:T(256)S(1)} %reshape.329, f32[256,512]{1,0:T(8,128)S(1)} %get-tuple-element.19, f32[256]{0:T(256)S(1)} %add_rsqrt_fusion.1, f32[256]{0:T(256)S(1)} %broadcast_multiply_fusion.1, f32[]{:T(128)} %constant.84.clone.1), kind=kCustom, calls=%fused_computation.60 | custom fusion | flops 393216 | bytes 919556 | tf_op jit(solution)/shard_map/scatter-add | solution.py:67
  41.8 7.0 %collective-permute-start.2 = (bf16[64,512]{1,0:T(8,128)(2,1)S(1)}, bf16[64,512]{1,0:T(8,128)(2,1)S(1)}, u32[]{:S(2)}, u32[]{:S(2)}) collective-permute-start(bf16[64,512]{1,0:T(8,128)(2,1)S(1)} %get-tuple-element.16), channel_id=1, source_target_pairs={{0,4},{4,8},{8,12},{12,16},{16,20},{20,24},{24,28},{28,32},{32,36}... | collective-permute-start | bytes 196616 | tf_op jit(solution)/shard_map/ppermute | solution.py:23
  48.8 1.9 %collective-permute-start.3 = (bf16[64,512]{1,0:T(8,128)(2,1)S(1)}, bf16[64,512]{1,0:T(8,128)(2,1)S(1)}, u32[]{:S(2)}, u32[]{:S(2)}) collective-permute-start(bf16[64,512]{1,0:T(8,128)(2,1)S(1)} %get-tuple-element.17), channel_id=1, source_target_pairs={{4,0},{8,4},{12,8},{16,12},{20,16},{24,20},{28,24},{32,28},{36,32}... | collective-permute-start | bytes 196616 | tf_op jit(solution)/shard_map/ppermute | solution.py:23
  50.7 6.9 %collective-permute-done.3 = bf16[64,512]{1,0:T(8,128)(2,1)S(1)} collective-permute-done((bf16[64,512]{1,0:T(8,128)(2,1)S(1)}, bf16[64,512]{1,0:T(8,128)(2,1)S(1)}, u32[]{:S(2)}, u32[]{:S(2)}) %collective-permute-start.3) | collective-permute-done | bytes 65568 | tf_op jit(solution)/shard_map/ppermute | solution.py:23
  58.9 27.7 %reduce-scatter.2.cloned.1.call-done = bf16[16,512]{1,0:T(8,128)(2,1)} async-done(((bf16[64,512]{1,0:T(8,128)(2,1)}), bf16[16,512]{1,0:T(8,128)(2,1)}) %reduce-scatter.2.cloned.1.call-update) | async-done | bytes 16400 | tf_op jit(solution)/shard_map/reduce_scatter | solution.py:76
  86.6 1.7 %fusion.110 = (f32[16]{0:T(128)S(1)}, f32[16,512]{1,0:T(8,128)S(1)}) fusion(bf16[3,3,512,512]{3,2,1,0:T(8,128)(2,1)} %param.13, f32[16,512]{1,0:T(8,128)S(1)} %fusion.32, bf16[16,512]{1,0:T(8,128)(2,1)} %reduce-scatter.2.cloned.1.call-done), kind=kOutput, calls=%fused_computation.150 | convolution fusion | flops 16834544 | bytes 1130560 | tf_op jit(solution)/shard_map/dot_general | solution.py:46
  88.6 9.0 %all_gather.10 = bf16[64,512]{1,0:T(8,128)(2,1)S(1)} all-gather(bf16[16,512]{1,0:T(8,128)(2,1)S(1)} %add_convert_fusion.2), channel_id=1, replica_groups=mesh['band'=256,'lon'=4] {'lon'}, dimensions={0}, use_global_device_ids=true | all-gather | bytes 81920 | tf_op jit(solution)/shard_map/all_gather | solution.py:51
  97.6 10.0 %collective-permute-start.4 = (bf16[64,512]{1,0:T(8,128)(2,1)S(1)}, bf16[64,512]{1,0:T(8,128)(2,1)S(1)}, u32[]{:S(2)}, u32[]{:S(2)}) collective-permute-start(bf16[64,512]{1,0:T(8,128)(2,1)S(1)} %all_gather.10), channel_id=1, source_target_pairs={{0,4},{4,8},{8,12},{12,16},{16,20},{20,24},{24,28},{28,32},{32,36}... | collective-permute-start | bytes 196616 | tf_op jit(solution)/shard_map/ppermute | solution.py:12
  107.5 1.9 %collective-permute-start.5 = (bf16[64,512]{1,0:T(8,128)(2,1)S(1)}, bf16[64,512]{1,0:T(8,128)(2,1)S(1)}, u32[]{:S(2)}, u32[]{:S(2)}) collective-permute-start(bf16[64,512]{1,0:T(8,128)(2,1)S(1)} %all_gather.10), channel_id=1, source_target_pairs={{4,0},{8,4},{12,8},{16,12},{20,16},{24,20},{28,24},{32,28},{36,32}... | collective-permute-start | bytes 196616 | tf_op jit(solution)/shard_map/ppermute | solution.py:15
  111.9 4.5 %collective-permute-done.5 = bf16[64,512]{1,0:T(8,128)(2,1)S(1)} collective-permute-done((bf16[64,512]{1,0:T(8,128)(2,1)S(1)}, bf16[64,512]{1,0:T(8,128)(2,1)S(1)}, u32[]{:S(2)}, u32[]{:S(2)}) %collective-permute-start.5) | collective-permute-done | bytes 65568 | tf_op jit(solution)/shard_map/ppermute | solution.py:15
  120.8 1.4 fusion.113
  122.8 1.7 %fusion.115 = (f32[16]{0:T(128)S(1)}, f32[16,512]{1,0:T(8,128)S(1)}) fusion(bf16[3,3,512,512]{3,2,1,0:T(8,128)(2,1)} %param.13, f32[16,512]{1,0:T(8,128)S(1)} %fusion.21, f32[16,512]{1,0:T(8,128)S(1)} %scatter-add.13), kind=kOutput, calls=%fused_computation.153 | convolution fusion | flops 16842736 | bytes 1146944 | tf_op jit(solution)/shard_map/dot_general | solution.py:46
  124.7 9.0 %all_gather.11 = bf16[64,512]{1,0:T(8,128)(2,1)S(1)} all-gather(bf16[16,512]{1,0:T(8,128)(2,1)S(1)} %add_convert_fusion.1), channel_id=1, replica_groups=mesh['band'=256,'lon'=4] {'lon'}, dimensions={0}, use_global_device_ids=true | all-gather | bytes 81920 | tf_op jit(solution)/shard_map/all_gather | solution.py:51
  133.7 5.3 %collective-permute-start.6 = (bf16[64,512]{1,0:T(8,128)(2,1)S(1)}, bf16[64,512]{1,0:T(8,128)(2,1)S(1)}, u32[]{:S(2)}, u32[]{:S(2)}) collective-permute-start(bf16[64,512]{1,0:T(8,128)(2,1)S(1)} %all_gather.11), channel_id=1, source_target_pairs={{0,4},{4,8},{8,12},{12,16},{16,20},{20,24},{24,28},{28,32},{32,36}... | collective-permute-start | bytes 196616 | tf_op jit(solution)/shard_map/ppermute | solution.py:12
  139.0 1.9 %collective-permute-start.7 = (bf16[64,512]{1,0:T(8,128)(2,1)S(1)}, bf16[64,512]{1,0:T(8,128)(2,1)S(1)}, u32[]{:S(2)}, u32[]{:S(2)}) collective-permute-start(bf16[64,512]{1,0:T(8,128)(2,1)S(1)} %all_gather.11), channel_id=1, source_target_pairs={{4,0},{8,4},{12,8},{16,12},{20,16},{24,20},{28,24},{32,28},{36,32}... | collective-permute-start | bytes 196616 | tf_op jit(solution)/shard_map/ppermute | solution.py:15
  141.0 7.0 %collective-permute-done.7 = bf16[64,512]{1,0:T(8,128)(2,1)S(1)} collective-permute-done((bf16[64,512]{1,0:T(8,128)(2,1)S(1)}, bf16[64,512]{1,0:T(8,128)(2,1)S(1)}, u32[]{:S(2)}, u32[]{:S(2)}) %collective-permute-start.7) | collective-permute-done | bytes 65568 | tf_op jit(solution)/shard_map/ppermute | solution.py:15
  149.2 1.6 gather_fusion.3
  152.2 1.5 fusion.120
  155.2 1.7 %fusion.121 = (f32[128]{0:T(128)S(1)}, f32[128,512]{1,0:T(8,128)S(1)}) fusion(bf16[3,3,512,512]{3,2,1,0:T(8,128)(2,1)} %param.13, f32[128,512]{1,0:T(8,128)S(1)} %fusion.34, bf16[128,512]{1,0:T(8,128)(2,1)S(1)} %reduce_sum.167), kind=kOutput, calls=%fused_computation.155 | convolution fusion | flops 134676352 | bytes 1704448 | tf_op jit(solution)/shard_map/dot_general | solution.py:46
  (89 shorter events, 24.1 us)
Async XLA Ops:
  7.2 79.5 %reduce-scatter.2.cloned.1.call-start = ((), (), s32[]{:S(2)}) async-start(), calls=%async_computation.1 | async-start | bytes 81920 | tf_op jit(solution)/shard_map/reduce_scatter | solution.py:76
  16.7 17.7 %collective-permute-start = (bf16[64,512]{1,0:T(8,128)(2,1)S(1)}, bf16[64,512]{1,0:T(8,128)(2,1)S(1)}, u32[]{:S(2)}, u32[]{:S(2)}) collective-permute-start(bf16[64,512]{1,0:T(8,128)(2,1)S(1)} %all_gather.9), channel_id=1, source_target_pairs={{0,4},{4,8},{8,12},{12,16},{16,20},{20,24},{24,28},{28,32},{32,36}... | collective-permute-start | bytes 196616 | tf_op jit(solution)/shard_map/ppermute | solution.py:12
  24.6 9.8 %collective-permute-start.1 = (bf16[64,512]{1,0:T(8,128)(2,1)S(1)}, bf16[64,512]{1,0:T(8,128)(2,1)S(1)}, u32[]{:S(2)}, u32[]{:S(2)}) collective-permute-start(bf16[64,512]{1,0:T(8,128)(2,1)S(1)} %all_gather.9), channel_id=1, source_target_pairs={{4,0},{8,4},{12,8},{16,12},{20,16},{24,20},{28,24},{32,28},{36,32}... | collective-permute-start | bytes 196616 | tf_op jit(solution)/shard_map/ppermute | solution.py:15
  35.7 15.0 %copy-start.3 = (s32[1,6]{1,0:T(1,128)S(1)}, s32[1,6]{1,0:T(1,128)}, u32[]{:S(2)}) copy-start(s32[1,6]{1,0:T(1,128)} %param.16) | copy-start | bytes 76
  36.7 51.8 %copy-start.1 = (bf16[16,512]{1,0:T(8,128)(2,1)S(1)}, bf16[16,512]{1,0:T(8,128)(2,1)}, u32[]{:S(2)}) copy-start(bf16[16,512]{1,0:T(8,128)(2,1)} %param.11) | copy-start | bytes 49156
  41.8 8.9 %collective-permute-start.2 = (bf16[64,512]{1,0:T(8,128)(2,1)S(1)}, bf16[64,512]{1,0:T(8,128)(2,1)S(1)}, u32[]{:S(2)}, u32[]{:S(2)}) collective-permute-start(bf16[64,512]{1,0:T(8,128)(2,1)S(1)} %get-tuple-element.16), channel_id=1, source_target_pairs={{0,4},{4,8},{8,12},{12,16},{16,20},{20,24},{24,28},{28,32},{32,36}... | collective-permute-start | bytes 196616 | tf_op jit(solution)/shard_map/ppermute | solution.py:23
  48.8 8.9 %collective-permute-start.3 = (bf16[64,512]{1,0:T(8,128)(2,1)S(1)}, bf16[64,512]{1,0:T(8,128)(2,1)S(1)}, u32[]{:S(2)}, u32[]{:S(2)}) collective-permute-start(bf16[64,512]{1,0:T(8,128)(2,1)S(1)} %get-tuple-element.17), channel_id=1, source_target_pairs={{4,0},{8,4},{12,8},{16,12},{20,16},{24,20},{28,24},{32,28},{36,32}... | collective-permute-start | bytes 196616 | tf_op jit(solution)/shard_map/ppermute | solution.py:23
  97.6 14.4 %collective-permute-start.4 = (bf16[64,512]{1,0:T(8,128)(2,1)S(1)}, bf16[64,512]{1,0:T(8,128)(2,1)S(1)}, u32[]{:S(2)}, u32[]{:S(2)}) collective-permute-start(bf16[64,512]{1,0:T(8,128)(2,1)S(1)} %all_gather.10), channel_id=1, source_target_pairs={{0,4},{4,8},{8,12},{12,16},{16,20},{20,24},{24,28},{28,32},{32,36}... | collective-permute-start | bytes 196616 | tf_op jit(solution)/shard_map/ppermute | solution.py:12
  107.5 8.9 %collective-permute-start.5 = (bf16[64,512]{1,0:T(8,128)(2,1)S(1)}, bf16[64,512]{1,0:T(8,128)(2,1)S(1)}, u32[]{:S(2)}, u32[]{:S(2)}) collective-permute-start(bf16[64,512]{1,0:T(8,128)(2,1)S(1)} %all_gather.10), channel_id=1, source_target_pairs={{4,0},{8,4},{12,8},{16,12},{20,16},{24,20},{28,24},{32,28},{36,32}... | collective-permute-start | bytes 196616 | tf_op jit(solution)/shard_map/ppermute | solution.py:15
  124.7 26.2 %copy-start.2 = (bf16[16,512]{1,0:T(8,128)(2,1)}, bf16[16,512]{1,0:T(8,128)(2,1)S(1)}, u32[]{:S(2)}) copy-start(bf16[16,512]{1,0:T(8,128)(2,1)S(1)} %add_convert_fusion.1) | copy-start | bytes 49156
  133.7 7.3 %collective-permute-start.6 = (bf16[64,512]{1,0:T(8,128)(2,1)S(1)}, bf16[64,512]{1,0:T(8,128)(2,1)S(1)}, u32[]{:S(2)}, u32[]{:S(2)}) collective-permute-start(bf16[64,512]{1,0:T(8,128)(2,1)S(1)} %all_gather.11), channel_id=1, source_target_pairs={{0,4},{4,8},{8,12},{12,16},{16,20},{20,24},{24,28},{28,32},{32,36}... | collective-permute-start | bytes 196616 | tf_op jit(solution)/shard_map/ppermute | solution.py:12
  139.0 8.9 %collective-permute-start.7 = (bf16[64,512]{1,0:T(8,128)(2,1)S(1)}, bf16[64,512]{1,0:T(8,128)(2,1)S(1)}, u32[]{:S(2)}, u32[]{:S(2)}) collective-permute-start(bf16[64,512]{1,0:T(8,128)(2,1)S(1)} %all_gather.11), channel_id=1, source_target_pairs={{4,0},{8,4},{12,8},{16,12},{20,16},{24,20},{28,24},{32,28},{36,32}... | collective-permute-start | bytes 196616 | tf_op jit(solution)/shard_map/ppermute | solution.py:15
  152.2 4.9 %copy-start = (bf16[128,512]{1,0:T(8,128)(2,1)S(1)}, bf16[128,512]{1,0:T(8,128)(2,1)}, u32[]{:S(2)}) copy-start(bf16[128,512]{1,0:T(8,128)(2,1)} %param.10) | copy-start | bytes 393220
Sparse Core Ops, SparseCore 0:
  58.5 28.0 reduce-scatter.1
where the time goes:
time: 166 us; the launch traced here: 165 us
  waiting for transfers between devices  46.2 us (28%)
  starting transfers between devices  37.8 us (23%)
  blocking collectives  27.5 us (17%)
  matrix products  22.3 us (13%)
  between operations  14.6 us (9%)
  other arithmetic  9.88 us (6%)
  local copies, waits for them, and re-layouts  6.48 us (4%)
    reduce_scatter x1, waiting for transfers between devices, per_device(): lax.psum_scatter(running.astype(jnp.bfloat16), 'lon', scatter_dimension=0...  27.7 us
    all_gather x3, blocking collectives, collect(): lon_rows = lax.all_gather(state, 'lon', axis=0, tiled=True)  27.5 us
    ppermute x3, starting transfers between devices, extended(): lax.ppermute(lax.slice_in_dim(block, block.shape[dim] - width, None, axis...  23.2 us
    ppermute x3, waiting for transfers between devices, extended(): lax.ppermute(lax.slice_in_dim(block, 0, width, axis=dim), axis, backward)  11.5 us
    ppermute x2, starting transfers between devices, from_behind(): return lax.ppermute(x, axis, pairs)  8.88 us
    ppermute x2, waiting for transfers between devices, from_behind(): return lax.ppermute(x, axis, pairs)  6.95 us
    ppermute x3, starting transfers between devices, extended(): lax.ppermute(lax.slice_in_dim(block, 0, width, axis=dim), axis, backward)  5.76 us
    dot_general x4, matrix products, edge_messages(): jnp.dot(shaped, out_weights, preferred_element_type=jnp.float32)  5.65 us
  transfers between devices with their start and end apart: 9, of which 4 were waited for; matrix products, arithmetic and copies ran while one was open for 7% of the time, Pallas kernels for 0%

commit v1 on v0

v1 whole, which is shorter than its diff:
```python
import jax
import jax.numpy as jnp
from jax import lax
from jax.experimental import pallas as pl
from jax.experimental.pallas import tpu as pltpu
from jax.sharding import PartitionSpec as P

BF = jnp.bfloat16
F32 = jnp.float32
NONE = 384


def mm(a, b):
    return jnp.dot(a, b, preferred_element_type=F32)


def silu(x):
    half = 0.5 * x
    return half + half * jnp.tanh(half)


def layer_norm(values):
    average = jnp.mean(values, axis=-1, keepdims=True)
    centred = values - average
    spread = jnp.mean(centred * centred, axis=-1, keepdims=True)
    return centred * lax.rsqrt(spread + 1e-05)


def update(state, aggregate, w0, w1, w2):
    inner = mm(state, w0) + mm(aggregate.astype(BF), w1)
    outer = layer_norm(mm(silu(inner).astype(BF), w2))
    return (state.astype(F32) + outer).astype(BF)


def slot_of(target_band, band):
    step = jnp.where(band % 2 == 0, target_band - band, band - target_band)
    return jnp.where(step < 0, 2, step)


def one_hot(index, rows, dtype=BF):
    lanes = lax.broadcasted_iota(jnp.int32, (index.shape[0], rows), 1)
    return jnp.where(lanes == index, 1.0, 0.0).astype(dtype)


def pack_kernel(where_ref, grid_ref, mesh_ref, enc_ref, proc_ref, far_ref, out_ref, enc_buf, proc_buf, far_buf, rows, sems):
    small = [
        pltpu.make_async_copy(src, dst, sems.at[n])
        for n, (src, dst) in enumerate(((enc_ref, enc_buf), (proc_ref, proc_buf), (far_ref, far_buf)))
    ]
    large = []
    for d in range(4):
        large.append(pltpu.make_async_copy(grid_ref, out_ref.at[d, 0:128], sems.at[3 + d]))
        large.append(pltpu.make_async_copy(mesh_ref, out_ref.at[d, 128:144], sems.at[7 + d]))
    for copy in small + large:
        copy.start()
    band = where_ref[0]
    rows[...] = jnp.full(rows.shape, float(NONE), F32)
    for copy in small:
        copy.wait()
    enc = enc_buf[...]
    rows[0:2, :] = (slot_of(enc >> 6, band) * 64 + (enc & 63)).astype(F32)
    proc = proc_buf[...]
    rows[2:8, 0:16] = (slot_of(proc >> 6, band) * 64 + (proc & 63)).astype(F32)
    far = far_buf[...]
    rows[8:9, 0:6] = (slot_of(far >> 2, band) * 64 + (far & 3) * 16).astype(F32)
    index = rows[...].astype(BF)
    for d in range(4):
        out_ref[d, 144:160, 0:128] = index
        out_ref[d, 144:160, 128:512] = jnp.zeros((16, 384), BF)
    for copy in large:
        copy.wait()


def encode_kernel(where_ref, all_ref, pair_ref, cross_ref, ew_ref, acc_ref, p1_ref, p2_ref, up_ref, down_ref, ohs, msgs):
    own = [all_ref[l, 128:144] for l in range(4)]
    table = jnp.concatenate([*own, pair_ref[...], cross_ref[...]], axis=0)
    rows_id = lax.broadcasted_iota(jnp.int32, (192, 128), 0)
    recv = mm(table, ew_ref[0, 1]).astype(BF)
    w_send, w_out = ew_ref[0, 0], ew_ref[0, 2]
    for l in range(4):
        index = all_ref[l, 144:160, 0:128].astype(F32)
        cols = index.T.astype(jnp.int32)
        flat = index.astype(jnp.int32)
        for k in range(2):
            start = l * 256 + k * 128
            ohs[:, start : start + 128] = jnp.where(rows_id == flat[k : k + 1, :], 1.0, 0.0).astype(BF)
        hot = jnp.concatenate([one_hot(cols[:, k : k + 1], 192) for k in range(2)], axis=0)
        sent = mm(all_ref[l, 0:128], w_send)
        before = mm(hot, recv) + jnp.concatenate([sent, sent], axis=0)
        result = layer_norm(mm(silu(before).astype(BF), w_out))
        msgs[l * 256 : (l + 1) * 256] = result.astype(BF)
    total = mm(ohs[...], msgs[...])
    acc_ref[...] = total
    own, pair, cross = (total[64 * n : 64 * n + 64].astype(BF) for n in range(3))
    p1_ref[0:64] = own
    p1_ref[64:128] = pair
    p2_ref[0:64] = own
    p2_ref[64:128] = cross
    even = where_ref[0] % 2 == 0

    @pl.when(even)
    def _():
        up_ref[...] = pair
        down_ref[...] = cross

    @pl.when(jnp.logical_not(even))
    def _():
        up_ref[...] = cross
        down_ref[...] = pair


def process_kernel(
    where_ref, acc_ref, r1_ref, r2_ref, up_ref, down_ref, part_ref, pair_ref, cross_ref, ew_ref, nw_ref, band_ref, own_ref, hots
):
    near_id = lax.broadcasted_iota(jnp.int32, (16, 1), 0)
    far_id = lax.broadcasted_iota(jnp.int32, (8, 1), 0)
    lanes = lax.broadcasted_iota(jnp.int32, (16, 256), 1)
    for l in range(4):
        cols = part_ref[l, 144:160, 0:128].astype(F32).T.astype(jnp.int32)
        for k in range(6):
            hit = jnp.logical_or(lanes == cols[0:16, 2 + k : 3 + k], lanes == near_id + (192 + 16 * l))
            hots[l * 128 + 16 * k : l * 128 + 16 * k + 16] = jnp.where(hit, 1.0, 0.0).astype(BF)
        hit = jnp.logical_or(lanes == cols[0:16, 8:9], lanes == 192 + 16 * l)
        hots[l * 128 + 96 : l * 128 + 112] = jnp.where(hit, 1.0, 0.0).astype(BF)
        hots[l * 128 + 112 : l * 128 + 128] = jnp.zeros((16, 256), BF)
    table = jnp.concatenate([*[part_ref[l, 128:144] for l in range(4)], pair_ref[...], cross_ref[...]], axis=0)
    even = where_ref[0] % 2 == 0
    above, below = up_ref[...].astype(F32), down_ref[...].astype(F32)
    far_pair = jnp.where(even, below, above)
    far_cross = jnp.where(even, above, below)
    own = acc_ref[0:64] + r1_ref[64:128].astype(F32) + r2_ref[64:128].astype(F32)
    pair = acc_ref[64:128] + r1_ref[0:64].astype(F32) + far_pair
    cross = acc_ref[128:192] + r2_ref[0:64].astype(F32) + far_cross
    sums = jnp.concatenate([own, pair, cross], axis=0)
    one = update(table, sums, nw_ref[0, 0], nw_ref[0, 1], nw_ref[0, 2])
    send = mm(one, ew_ref[1, 0]).astype(BF)
    recv = mm(one[0:64], ew_ref[1, 1]).astype(BF)
    both = jnp.concatenate([send, recv], axis=0)
    w_out = ew_ref[1, 2]
    parts = []
    for l in range(0, 4, 2):
        before = mm(hots[l * 128 : (l + 2) * 128], both)
        messages = layer_norm(mm(silu(before).astype(BF), w_out))
        for m in range(2):
            base = 128 * m
            near = messages[base : base + 16]
            for k in range(1, 6):
                near = near + messages[base + 16 * k : base + 16 * k + 16]
            far = jnp.where(far_id < 6, messages[base + 96 : base + 104], 0.0)
            far = jnp.sum(far, axis=0, keepdims=True)
            parts.append(near + jnp.where(near_id == 0, far, 0.0))
    sums = jnp.concatenate(parts, axis=0)
    two = update(one[0:64], sums, nw_ref[1, 0], nw_ref[1, 1], nw_ref[1, 2])
    band_ref[...] = two
    lon = where_ref[1]
    for l in range(4):

        @pl.when(lon == l)
        def _():
            own_ref[...] = two[16 * l : 16 * l + 16]


def decode_kernel(where_ref, grid_ref, dec_ref, own_ref, pair_ref, cross_ref, ew_ref, nw_ref, out_ref, rows):
    index = dec_ref[...]
    rows[...] = jnp.zeros(rows.shape, F32)
    rows[0:3, :] = (slot_of(index >> 6, where_ref[0]) * 64 + (index & 63)).astype(F32)
    index = rows[...].T.astype(jnp.int32)
    state = grid_ref[...]
    table = jnp.concatenate([own_ref[...], pair_ref[...], cross_ref[...]], axis=0)
    send = mm(table, ew_ref[2, 0]).astype(BF)
    recv = mm(state, ew_ref[2, 1])
    w_out = ew_ref[2, 2]
    sums = None
    for k in range(3):
        before = mm(one_hot(index[:, k : k + 1], 192), send) + recv
        messages = layer_norm(mm(silu(before).astype(BF), w_out))
        sums = messages if sums is None else sums + messages
    out_ref[...] = update(state, sums, nw_ref[2, 0], nw_ref[2, 1], nw_ref[2, 2])


SMEM = pl.BlockSpec(memory_space=pltpu.SMEM)
VMEM = pl.BlockSpec(memory_space=pltpu.VMEM)
HBM = pl.BlockSpec(memory_space=pltpu.HBM)
MIB = 1024 * 1024


def params(limit=16):
    return pltpu.CompilerParams(vmem_limit_bytes=limit * MIB)


def cost(products):
    return pl.CostEstimate(flops=2 * products * 512 * 512, bytes_accessed=8 * MIB, transcendentals=0)


def per_device(
    grid_state, mesh_state, edge_weights, node_weights, enc_recv, proc_send, long_send, dec_send
):
    width = grid_state.shape[1]
    bands = lax.axis_size("band")
    where = jnp.stack([lax.axis_index("band"), lax.axis_index("lon")]).astype(jnp.int32)
    across = [(i, i + 1 if i % 2 else i - 1) for i in range(1, bands - 1)]
    within = [(i, i ^ 1) for i in range(bands)]
    upward = [(i, i + 2) for i in range(bands - 2)]
    downward = [(i + 2, i) for i in range(bands - 2)]

    def sides(pair_block, cross_block):
        cross = lax.ppermute(cross_block, "band", across)
        pair = lax.ppermute(pair_block, "band", within)
        return pair, cross

    shape = jax.ShapeDtypeStruct
    packed = pl.pallas_call(
        pack_kernel,
        in_specs=[SMEM] + [HBM] * 5,
        out_specs=VMEM,
        out_shape=shape((4, 160, width), BF),
        scratch_shapes=[
            pltpu.VMEM((2, 128), jnp.int32),
            pltpu.VMEM((6, 16), jnp.int32),
            pltpu.VMEM((1, 6), jnp.int32),
            pltpu.VMEM((16, 128), F32),
            pltpu.SemaphoreType.DMA((11,)),
        ],
        compiler_params=params(16),
        cost_estimate=cost(8000),
        name="pack",
    )(where, *(pltpu.with_memory_space_constraint(x, pltpu.HBM) for x in (grid_state, mesh_state, enc_recv.T, proc_send.T, long_send)))
    with jax.named_scope("gather_lon"):
        packed = lax.all_to_all(packed, "lon", 0, 0)
    with jax.named_scope("mesh_sides"):
        band_state = packed[:, 128:144].reshape(64, width)
        pair_state, cross_state = sides(band_state, band_state)
    acc, p1, p2, up, down = pl.pallas_call(
        encode_kernel,
        in_specs=[SMEM] + [VMEM] * 4,
        out_specs=[VMEM] * 5,
        out_shape=[
            shape((192, width), F32),
            shape((128, width), BF),
            shape((128, width), BF),
            shape((64, width), BF),
            shape((64, width), BF),
        ],
        scratch_shapes=[pltpu.VMEM((192, 1024), BF), pltpu.VMEM((1024, width), BF)],
        compiler_params=params(),
        cost_estimate=cost(8000),
        name="encode",
    )(where, packed, pair_state, cross_state, edge_weights)
    with jax.named_scope("sum_sides"):
        r_up = lax.ppermute(up, "band", upward)
        r_down = lax.ppermute(down, "band", downward)
        r1, r2 = sides(p1, p2)
    band_two, mesh_two = pl.pallas_call(
        process_kernel,
        in_specs=[SMEM] + [VMEM] * 10,
        out_specs=[VMEM, VMEM],
        out_shape=[shape((64, width), BF), shape((16, width), BF)],
        scratch_shapes=[pltpu.VMEM((512, 256), BF)],
        compiler_params=params(),
        cost_estimate=cost(8000),
        name="process",
    )(where, acc, r1, r2, r_up, r_down, packed, pair_state, cross_state, edge_weights, node_weights)
    with jax.named_scope("two_sides"):
        pair_two, cross_two = sides(band_two, band_two)
    grid_out = pl.pallas_call(
        decode_kernel,
        in_specs=[SMEM] + [VMEM] * 7,
        out_specs=VMEM,
        out_shape=shape(grid_state.shape, BF),
        scratch_shapes=[pltpu.VMEM((8, 128), F32)],
        compiler_params=params(),
        cost_estimate=cost(8000),
        name="decode",
    )(where, grid_state, dec_send.T, band_two, pair_two, cross_two, edge_weights, node_weights)
    return (grid_out, mesh_two)


def solution(mesh):
    rows = P(("band", "lon"), None)
    in_specs = (rows, rows, P(), P(), rows, rows, rows, rows)
    return jax.shard_map(
        per_device, mesh=mesh, in_specs=in_specs, out_specs=(rows, rows), check_vma=False
    )
```

time: 166 us -> 64.1 us (0.39)
  the two profiles are of different devices: /device:TPU:249 before, /device:TPU:768 now
where the time goes in v1:
time: 64.1 us; the launch traced here: 63.8 us
  starting transfers between devices  28.2 us (44%)
  blocking collectives  15 us (23%)
  Pallas kernels  12.1 us (19%)
  waiting for transfers between devices  7.65 us (12%)
  between operations  0.77 us (1%)
    all_to_all x1, blocking collectives, per_device(): packed = lax.all_to_all(packed, 'lon', 0, 0)  15 us
    ppermute x3, starting transfers between devices, sides(): cross = lax.ppermute(cross_block, 'band', across)  13.3 us
    ppermute x1, starting transfers between devices, per_device(): r_down = lax.ppermute(down, 'band', downward)  7.24 us
    ppermute x3, starting transfers between devices, sides(): pair = lax.ppermute(pair_block, 'band', within)  5.76 us
    ppermute x3, waiting for transfers between devices, sides(): cross = lax.ppermute(cross_block, 'band', across)  5.76 us
    pallas_call x1, Pallas kernels, per_device(): pl.pallas_call(process_kernel, in_specs=[SMEM] + [VMEM] * 10, out_specs=[...  3.79 us
    pallas_call x1, Pallas kernels, per_device(): pl.pallas_call(decode_kernel, in_specs=[SMEM] + [VMEM] * 7, out_specs=VME...  3.15 us
    pallas_call x1, Pallas kernels, per_device(): pl.pallas_call(encode_kernel, in_specs=[SMEM] + [VMEM] * 4, out_specs=[VM...  3.08 us
  transfers between devices with their start and end apart: 8, of which 4 were waited for; matrix products, arithmetic and copies ran while one was open for 0% of the time, Pallas kernels for 0%

profile of v1, /device:TPU:768, one launch (start us, length us, event | category | flops | bytes accessed | tf_op | source)
XLA Modules:
  0.0 63.8 jit_solution(10494743269988615900)
XLA Ops:
  0.6 0.1 pad_add_fusion.where_ref
  0.7 2.1 %pack.1 = bf16[4,160,512]{2,1,0:T(8,128)(2,1)S(1)} custom-call(s32[2]{0:T(128)S(1)} %pad_add_fusion.where_ref, bf16[128,512]{1,0:T(8,128)(2,1)} %grid_ref.3, bf16[16,512]{1,0:T(8,128)(2,1)} %mesh_ref.1, s32[2,128]{1,0:T(2,128)} %bitcast.12, s32[6,16]{1,0:T(8,128)} %bitcast.11, s32[1,6]{1,0:T(1,128)} %far_ref.1), custom_call_target="tpu_custom_call" | custom-call | flops 4194304000 | bytes 8388608 | tf_op jit(solution)/shard_map/pack/pallas_call | solution.py:212
  2.8 15.0 %all_to_all.5.all_ref.part_ref = bf16[4,160,512]{2,1,0:T(8,128)(2,1)S(1)} all-to-all(bf16[4,160,512]{2,1,0:T(8,128)(2,1)S(1)} %pack.1), channel_id=1, replica_groups=mesh['band'=256,'lon'=4] {'lon'}, dimensions={0} | all-to-all | bytes 1310720 | tf_op jit(solution)/shard_map/gather_lon/all_to_all | solution.py:229
  17.8 0.0 slice-start.1
  17.8 5.1 %collective-permute-start.1 = (bf16[64,512]{1,0:T(8,128)(2,1)S(1)}, bf16[64,512]{1,0:T(8,128)(2,1)S(1)}, u32[]{:S(2)}, u32[]{:S(2)}) collective-permute-start(bf16[64,512]{1,0:T(8,128)(2,1)S(1)} %bitcast.9), channel_id=1, source_target_pairs={{4,8},{8,4},{12,16},{16,12},{20,24},{24,20},{28,32},{32,28},{36,40... | collective-permute-start | bytes 196616 | tf_op jit(solution)/shard_map/mesh_sides/ppermute | solution.py:207
  22.9 1.9 %collective-permute-start = (bf16[64,512]{1,0:T(8,128)(2,1)S(1)}, bf16[64,512]{1,0:T(8,128)(2,1)S(1)}, u32[]{:S(2)}, u32[]{:S(2)}) collective-permute-start(bf16[64,512]{1,0:T(8,128)(2,1)S(1)} %bitcast.10), channel_id=1, source_target_pairs={{0,4},{4,0},{8,12},{12,8},{16,20},{20,16},{24,28},{28,24},{32,36},... | collective-permute-start | bytes 196616 | tf_op jit(solution)/shard_map/mesh_sides/ppermute | solution.py:208
  24.8 2.1 %collective-permute-done.1.cross_ref = bf16[64,512]{1,0:T(8,128)(2,1)S(1)} collective-permute-done((bf16[64,512]{1,0:T(8,128)(2,1)S(1)}, bf16[64,512]{1,0:T(8,128)(2,1)S(1)}, u32[]{:S(2)}, u32[]{:S(2)}) %collective-permute-start.1) | collective-permute-done | bytes 65568 | tf_op jit(solution)/shard_map/mesh_sides/ppermute | solution.py:207
  27.0 0.0 collective-permute-done.pair_ref
  27.0 3.1 %encode.1 = (f32[192,512]{1,0:T(8,128)S(1)}, bf16[128,512]{1,0:T(8,128)(2,1)S(1)}, bf16[128,512]{1,0:T(8,128)(2,1)S(1)}, bf16[64,512]{1,0:T(8,128)(2,1)S(1)}, bf16[64,512]{1,0:T(8,128)(2,1)S(1)}) custom-call(s32[2]{0:T(128)S(1)} %pad_add_fusion.where_ref, bf16[4,160,512]{2,1,0:T(8,128)(2,1)S(1)} %all_to_all.5.all_ref.part_ref, ...), custom_call_target="tpu_custom_call" | custom-call | flops 4194304000 | bytes 8388608 | tf_op jit(solution)/shard_map/encode/pallas_call | solution.py:233
  30.1 1.9 %collective-permute-start.2 = (bf16[128,512]{1,0:T(8,128)(2,1)S(1)}, bf16[128,512]{1,0:T(8,128)(2,1)S(1)}, u32[]{:S(2)}, u32[]{:S(2)}) collective-permute-start(bf16[128,512]{1,0:T(8,128)(2,1)S(1)} %get-tuple-element.10), channel_id=1, source_target_pairs={{0,4},{4,0},{8,12},{12,8},{16,20},{20,16},{24,28},{28,24},{32,36},... | collective-permute-start | bytes 393224 | tf_op jit(solution)/shard_map/sum_sides/ppermute | solution.py:208
  32.0 4.8 %collective-permute-start.3 = (bf16[128,512]{1,0:T(8,128)(2,1)S(1)}, bf16[128,512]{1,0:T(8,128)(2,1)S(1)}, u32[]{:S(2)}, u32[]{:S(2)}) collective-permute-start(bf16[128,512]{1,0:T(8,128)(2,1)S(1)} %get-tuple-element.11), channel_id=1, source_target_pairs={{4,8},{8,4},{12,16},{16,12},{20,24},{24,20},{28,32},{32,28},{36,40... | collective-permute-start | bytes 393224 | tf_op jit(solution)/shard_map/sum_sides/ppermute | solution.py:207
  36.8 1.9 %collective-permute-start.4 = (bf16[64,512]{1,0:T(8,128)(2,1)S(1)}, bf16[64,512]{1,0:T(8,128)(2,1)S(1)}, u32[]{:S(2)}, u32[]{:S(2)}) collective-permute-start(bf16[64,512]{1,0:T(8,128)(2,1)S(1)} %get-tuple-element.12), channel_id=1, source_target_pairs={{0,8},{4,12},{8,16},{12,20},{16,24},{20,28},{24,32},{28,36},{32,40... | collective-permute-start | bytes 196616 | tf_op jit(solution)/shard_map/sum_sides/ppermute | solution.py:250
  38.8 7.2 %collective-permute-start.5 = (bf16[64,512]{1,0:T(8,128)(2,1)S(1)}, bf16[64,512]{1,0:T(8,128)(2,1)S(1)}, u32[]{:S(2)}, u32[]{:S(2)}) collective-permute-start(bf16[64,512]{1,0:T(8,128)(2,1)S(1)} %get-tuple-element.13), channel_id=1, source_target_pairs={{8,0},{12,4},{16,8},{20,12},{24,16},{28,20},{32,24},{36,28},{40,32... | collective-permute-start | bytes 196616 | tf_op jit(solution)/shard_map/sum_sides/ppermute | solution.py:251
  46.0 0.3 collective-permute-done.4.up_ref
  46.3 1.6 %collective-permute-done.5.down_ref = bf16[64,512]{1,0:T(8,128)(2,1)S(1)} collective-permute-done((bf16[64,512]{1,0:T(8,128)(2,1)S(1)}, bf16[64,512]{1,0:T(8,128)(2,1)S(1)}, u32[]{:S(2)}, u32[]{:S(2)}) %collective-permute-start.5) | collective-permute-done | bytes 65568 | tf_op jit(solution)/shard_map/sum_sides/ppermute | solution.py:251
  47.9 0.0 collective-permute-done.2.r1_ref
  47.9 0.0 copy-start.1
  47.9 0.0 copy-start.2
  47.9 3.8 %process.1 = (bf16[64,512]{1,0:T(8,128)(2,1)S(1)}, bf16[16,512]{1,0:T(8,128)(2,1)}) custom-call(s32[2]{0:T(128)S(1)} %pad_add_fusion.where_ref, f32[192,512]{1,0:T(8,128)S(1)} %get-tuple-element.9.acc_ref, bf16[128,512]{1,0:T(8,128)(2,1)S(1)} %collective-permute-done.2.r1_ref, bf16[128,512]{1,0:T(8,128)(2,1)S(1)} %collective-permute-done.3.r2_ref, ...), custom_call_target="tpu_custom_call" | custom-call | flops 4194304000 | bytes 8388608 | tf_op jit(solution)/shard_map/process/pallas_call | solution.py:253
  51.7 3.3 %collective-permute-start.7 = (bf16[64,512]{1,0:T(8,128)(2,1)S(1)}, bf16[64,512]{1,0:T(8,128)(2,1)S(1)}, u32[]{:S(2)}, u32[]{:S(2)}) collective-permute-start(bf16[64,512]{1,0:T(8,128)(2,1)S(1)} %get-tuple-element.14.own_ref), channel_id=1, source_target_pairs={{4,8},{8,4},{12,16},{16,12},{20,24},{24,20},{28,32},{32,28},{36,40... | collective-permute-start | bytes 196616 | tf_op jit(solution)/shard_map/two_sides/ppermute | solution.py:207
  55.1 1.9 %collective-permute-start.6 = (bf16[64,512]{1,0:T(8,128)(2,1)S(1)}, bf16[64,512]{1,0:T(8,128)(2,1)S(1)}, u32[]{:S(2)}, u32[]{:S(2)}) collective-permute-start(bf16[64,512]{1,0:T(8,128)(2,1)S(1)} %get-tuple-element.14.own_ref), channel_id=1, source_target_pairs={{0,4},{4,0},{8,12},{12,8},{16,20},{20,16},{24,28},{28,24},{32,36},... | collective-permute-start | bytes 196616 | tf_op jit(solution)/shard_map/two_sides/ppermute | solution.py:208
  57.0 3.6 %collective-permute-done.7.cross_ref = bf16[64,512]{1,0:T(8,128)(2,1)S(1)} collective-permute-done((bf16[64,512]{1,0:T(8,128)(2,1)S(1)}, bf16[64,512]{1,0:T(8,128)(2,1)S(1)}, u32[]{:S(2)}, u32[]{:S(2)}) %collective-permute-start.7) | collective-permute-done | bytes 65568 | tf_op jit(solution)/shard_map/two_sides/ppermute | solution.py:207
  60.6 0.0 collective-permute-done.6.pair_ref
  60.6 3.1 %decode.1 = bf16[128,512]{1,0:T(8,128)(2,1)} custom-call(s32[2]{0:T(128)S(1)} %pad_add_fusion.where_ref, bf16[128,512]{1,0:T(8,128)(2,1)S(1)} %copy-done.1, s32[3,128]{1,0:T(4,128)S(1)} %bitcast.8, bf16[64,512]{1,0:T(8,128)(2,1)S(1)} %get-tuple-element.14.own_ref, bf16[64,512]{1,0:T(8,128)(2,1)S(1)} %collective-permute-done.6.pair_ref, ...), custom_call_target="tpu_custom_call" | custom-call | flops 4194304000 | bytes 8388608 | tf_op jit(solution)/shard_map/decode/pallas_call | solution.py:265
  (10 shorter events, 0.0 us)
Async XLA Ops:
  0.7 26.3 %copy-start = (bf16[3,3,512,512]{3,2,1,0:T(8,128)(2,1)S(1)}, bf16[3,3,512,512]{3,2,1,0:T(8,128)(2,1)}, u32[]{:S(2)}) copy-start(bf16[3,3,512,512]{3,2,1,0:T(8,128)(2,1)} %ew_ref.5) | copy-start | bytes 14155780
  17.8 30.1 %slice-start = ((s8[4718592]{0:T(1024)(128)(4,1)}), s8[4194304]{0:T(1024)(128)(4,1)S(1)}, s32[]{:S(2)}) async-start(s8[4718592]{0:T(1024)(128)(4,1)} %bitcast.6), calls=%async_computation.1 | async-start | bytes 8388608
  17.8 30.1 %slice-start.1 = ((s8[4718592]{0:T(1024)(128)(4,1)}), s8[524288]{0:T(1024)(128)(4,1)S(1)}, s32[]{:S(2)}) async-start(s8[4718592]{0:T(1024)(128)(4,1)} %bitcast.6), calls=%async_computation.2 | async-start | bytes 1048576
  17.8 9.2 %collective-permute-start.1 = (bf16[64,512]{1,0:T(8,128)(2,1)S(1)}, bf16[64,512]{1,0:T(8,128)(2,1)S(1)}, u32[]{:S(2)}, u32[]{:S(2)}) collective-permute-start(bf16[64,512]{1,0:T(8,128)(2,1)S(1)} %bitcast.9), channel_id=1, source_target_pairs={{4,8},{8,4},{12,16},{16,12},{20,24},{24,20},{28,32},{32,28},{36,40... | collective-permute-start | bytes 196616 | tf_op jit(solution)/shard_map/mesh_sides/ppermute | solution.py:207
  22.9 4.1 %collective-permute-start = (bf16[64,512]{1,0:T(8,128)(2,1)S(1)}, bf16[64,512]{1,0:T(8,128)(2,1)S(1)}, u32[]{:S(2)}, u32[]{:S(2)}) collective-permute-start(bf16[64,512]{1,0:T(8,128)(2,1)S(1)} %bitcast.10), channel_id=1, source_target_pairs={{0,4},{4,0},{8,12},{12,8},{16,20},{20,16},{24,28},{28,24},{32,36},... | collective-permute-start | bytes 196616 | tf_op jit(solution)/shard_map/mesh_sides/ppermute | solution.py:208
  30.1 17.8 %collective-permute-start.2 = (bf16[128,512]{1,0:T(8,128)(2,1)S(1)}, bf16[128,512]{1,0:T(8,128)(2,1)S(1)}, u32[]{:S(2)}, u32[]{:S(2)}) collective-permute-start(bf16[128,512]{1,0:T(8,128)(2,1)S(1)} %get-tuple-element.10), channel_id=1, source_target_pairs={{0,4},{4,0},{8,12},{12,8},{16,20},{20,16},{24,28},{28,24},{32,36},... | collective-permute-start | bytes 393224 | tf_op jit(solution)/shard_map/sum_sides/ppermute | solution.py:208
  32.0 15.9 %collective-permute-start.3 = (bf16[128,512]{1,0:T(8,128)(2,1)S(1)}, bf16[128,512]{1,0:T(8,128)(2,1)S(1)}, u32[]{:S(2)}, u32[]{:S(2)}) collective-permute-start(bf16[128,512]{1,0:T(8,128)(2,1)S(1)} %get-tuple-element.11), channel_id=1, source_target_pairs={{4,8},{8,4},{12,16},{16,12},{20,24},{24,20},{28,32},{32,28},{36,40... | collective-permute-start | bytes 393224 | tf_op jit(solution)/shard_map/sum_sides/ppermute | solution.py:207
  36.8 9.5 %collective-permute-start.4 = (bf16[64,512]{1,0:T(8,128)(2,1)S(1)}, bf16[64,512]{1,0:T(8,128)(2,1)S(1)}, u32[]{:S(2)}, u32[]{:S(2)}) collective-permute-start(bf16[64,512]{1,0:T(8,128)(2,1)S(1)} %get-tuple-element.12), channel_id=1, source_target_pairs={{0,8},{4,12},{8,16},{12,20},{16,24},{20,28},{24,32},{28,36},{32,40... | collective-permute-start | bytes 196616 | tf_op jit(solution)/shard_map/sum_sides/ppermute | solution.py:250
  38.8 9.1 %collective-permute-start.5 = (bf16[64,512]{1,0:T(8,128)(2,1)S(1)}, bf16[64,512]{1,0:T(8,128)(2,1)S(1)}, u32[]{:S(2)}, u32[]{:S(2)}) collective-permute-start(bf16[64,512]{1,0:T(8,128)(2,1)S(1)} %get-tuple-element.13), channel_id=1, source_target_pairs={{8,0},{12,4},{16,8},{20,12},{24,16},{28,20},{32,24},{36,28},{40,32... | collective-permute-start | bytes 196616 | tf_op jit(solution)/shard_map/sum_sides/ppermute | solution.py:251
  47.9 12.7 %copy-start.1 = (bf16[128,512]{1,0:T(8,128)(2,1)S(1)}, bf16[128,512]{1,0:T(8,128)(2,1)}, u32[]{:S(2)}) copy-start(bf16[128,512]{1,0:T(8,128)(2,1)} %grid_ref.3) | copy-start | bytes 393220
  47.9 12.7 %copy-start.2 = (s32[128,3]{0,1:T(4,128)S(1)}, s32[128,3]{0,1:T(4,128)}, u32[]{:S(2)}) copy-start(s32[128,3]{0,1:T(4,128)} %param.15) | copy-start | bytes 4612
  51.7 8.9 %collective-permute-start.7 = (bf16[64,512]{1,0:T(8,128)(2,1)S(1)}, bf16[64,512]{1,0:T(8,128)(2,1)S(1)}, u32[]{:S(2)}, u32[]{:S(2)}) collective-permute-start(bf16[64,512]{1,0:T(8,128)(2,1)S(1)} %get-tuple-element.14.own_ref), channel_id=1, source_target_pairs={{4,8},{8,4},{12,16},{16,12},{20,24},{24,20},{28,32},{32,28},{36,40... | collective-permute-start | bytes 196616 | tf_op jit(solution)/shard_map/two_sides/ppermute | solution.py:207
  55.1 5.5 %collective-permute-start.6 = (bf16[64,512]{1,0:T(8,128)(2,1)S(1)}, bf16[64,512]{1,0:T(8,128)(2,1)S(1)}, u32[]{:S(2)}, u32[]{:S(2)}) collective-permute-start(bf16[64,512]{1,0:T(8,128)(2,1)S(1)} %get-tuple-element.14.own_ref), channel_id=1, source_target_pairs={{0,4},{4,0},{8,12},{12,8},{16,20},{20,16},{24,28},{28,24},{32,36},... | collective-permute-start | bytes 196616 | tf_op jit(solution)/shard_map/two_sides/ppermute | solution.py:208

commit v2 on v1

v2 whole, which is shorter than its diff:
```python
import jax
import jax.numpy as jnp
from jax import lax
from jax.experimental import pallas as pl
from jax.experimental.pallas import tpu as pltpu
from jax.sharding import PartitionSpec as P

BF = jnp.bfloat16
F32 = jnp.float32
NONE = 384


def mm(a, b):
    return jnp.dot(a, b, preferred_element_type=F32)


def silu(x):
    half = 0.5 * x
    return half + half * jnp.tanh(half)


def layer_norm(values):
    average = jnp.mean(values, axis=-1, keepdims=True)
    centred = values - average
    spread = jnp.mean(centred * centred, axis=-1, keepdims=True)
    return centred * lax.rsqrt(spread + 1e-05)


def update(state, inner, aggregate, w1, w2):
    inner = inner + mm(aggregate.astype(BF), w1)
    outer = layer_norm(mm(silu(inner).astype(BF), w2))
    return (state.astype(F32) + outer).astype(BF)


def slot_of(target_band, band):
    step = jnp.where(band % 2 == 0, target_band - band, band - target_band)
    return jnp.where(step < 0, 2, step)


def one_hot(index, rows, dtype=BF):
    lanes = lax.broadcasted_iota(jnp.int32, (index.shape[0], rows), 1)
    return jnp.where(lanes == index, 1.0, 0.0).astype(dtype)


def pack_kernel(grid_ref, mesh_ref, enc_ref, proc_ref, far_ref, out_ref, enc_buf, proc_buf, far_buf, rows, sems):
    small = [
        pltpu.make_async_copy(src, dst, sems.at[n])
        for n, (src, dst) in enumerate(((enc_ref, enc_buf), (proc_ref, proc_buf), (far_ref, far_buf)))
    ]
    large = []
    large.append(pltpu.make_async_copy(grid_ref, out_ref.at[0:128], sems.at[3]))
    large.append(pltpu.make_async_copy(mesh_ref, out_ref.at[128:144], sems.at[4]))
    for copy in small + large:
        copy.start()
    band = lax.axis_index("band")
    rows[...] = jnp.full(rows.shape, float(NONE), F32)
    for copy in small:
        copy.wait()
    enc = enc_buf[...]
    rows[0:2, :] = (slot_of(enc >> 6, band) * 64 + (enc & 63)).astype(F32)
    proc = proc_buf[...]
    rows[2:8, 0:16] = (slot_of(proc >> 6, band) * 64 + (proc & 63)).astype(F32)
    far = far_buf[...]
    rows[8:9, 0:6] = (slot_of(far >> 2, band) * 64 + (far & 3) * 16).astype(F32)
    index = rows[...].astype(BF)
    out_ref[176:192, 0:128] = index
    out_ref[176:192, 128:512] = jnp.zeros((16, 384), BF)
    for copy in large:
        copy.wait()


def window(all_ref):
    return jnp.concatenate(
        [all_ref[l, 128 + 16 * s : 144 + 16 * s] for s in range(3) for l in range(4)], axis=0
    )


def encode_first_kernel(all_ref, ew_ref, sent_ref, hot_ref, spread_ref):
    rows_id = lax.broadcasted_iota(jnp.int32, (192, 128), 0)
    for l in range(4):
        sent_ref[l * 128 : (l + 1) * 128] = mm(all_ref[l, 0:128], ew_ref[0, 0])
        index = all_ref[l, 176:192, 0:128].astype(F32)
        cols = index.T.astype(jnp.int32)
        flat = index.astype(jnp.int32)
        for k in range(2):
            start = l * 256 + k * 128
            spread_ref[:, start : start + 128] = jnp.where(rows_id == flat[k : k + 1, :], 1.0, 0.0).astype(BF)
            hot_ref[start : start + 128] = one_hot(cols[:, k : k + 1], 192)


def encode_kernel(all_ref, sent_ref, hot_ref, spread_ref, ew_ref, acc_ref, p1_ref, far_ref, p2_ref, msgs):
    table = window(all_ref)
    recv = mm(table, ew_ref[0, 1]).astype(BF)
    for l in range(4):
        sent = sent_ref[l * 128 : (l + 1) * 128]
        before = mm(hot_ref[l * 256 : (l + 1) * 256], recv) + jnp.concatenate([sent, sent], axis=0)
        result = layer_norm(mm(silu(before).astype(BF), ew_ref[0, 2]))
        msgs[l * 256 : (l + 1) * 256] = result.astype(BF)
    total = mm(spread_ref[...], msgs[...])
    acc_ref[...] = total
    p1_ref[...] = total[0:128].astype(BF)
    cross = total[128:192].astype(BF)
    far_ref[...] = cross
    p2_ref[0:64] = cross
    p2_ref[64:128] = cross


def process_first_kernel(all_ref, nw_ref, after_ref, inner_ref, hots):
    near_id = lax.broadcasted_iota(jnp.int32, (16, 1), 0)
    lanes = lax.broadcasted_iota(jnp.int32, (16, 256), 1)
    far = []
    for l in range(4):
        cols = all_ref[l, 176:192, 0:128].astype(F32).T.astype(jnp.int32)
        for k in range(6):
            hit = jnp.logical_or(lanes == cols[0:16, 2 + k : 3 + k], lanes == near_id + (192 + 16 * l))
            hots[l * 96 + 16 * k : l * 96 + 16 * k + 16] = jnp.where(hit, 1.0, 0.0).astype(BF)
        far.append(jnp.logical_or(lanes[0:8] == cols[0:8, 8:9], lanes[0:8] == 192 + 16 * l))
    hots[384:416] = jnp.concatenate([jnp.where(hit, 1.0, 0.0) for hit in far], axis=0).astype(BF)
    table = window(all_ref)
    inner_ref[...] = mm(table, nw_ref[0, 0])


def process_kernel(
    acc_ref, r1_ref, r2_ref, far_ref, all_ref, inner_ref, hots, ew_ref, nw_ref, after_ref, band_ref, own_ref
):
    table = window(all_ref)
    own = acc_ref[0:64] + r1_ref[64:128].astype(F32) + r2_ref[0:64].astype(F32)
    pair = acc_ref[64:128] + r1_ref[0:64].astype(F32) + far_ref[...].astype(F32)
    cross = acc_ref[128:192] + r2_ref[64:128].astype(F32)
    sums = jnp.concatenate([own, pair, cross], axis=0)
    one = update(table, inner_ref[...], sums, nw_ref[0, 1], nw_ref[0, 2])
    send = mm(one, ew_ref[1, 0]).astype(BF)
    recv = mm(one[0:64], ew_ref[1, 1]).astype(BF)
    both = jnp.concatenate([send, recv], axis=0)
    inner = mm(one[0:64], nw_ref[1, 0])
    near_id = lax.broadcasted_iota(jnp.int32, (16, 1), 0)
    far_id = lax.broadcasted_iota(jnp.int32, (8, 1), 0)
    near, far = [], []
    for start, size in ((0, 192), (192, 224)):
        before = mm(hots[start : start + size], both)
        messages = layer_norm(mm(silu(before).astype(BF), ew_ref[1, 2]))
        for m in range(2):
            total = messages[96 * m : 96 * m + 16]
            for k in range(1, 6):
                total = total + messages[96 * m + 16 * k : 96 * m + 16 * k + 16]
            near.append(total)
    for l in range(4):
        values = jnp.where(far_id < 6, messages[192 + 8 * l : 200 + 8 * l], 0.0)
        far.append(jnp.sum(values, axis=0, keepdims=True))
    parts = [a + jnp.where(near_id == 0, b, 0.0) for a, b in zip(near, far)]
    sums = jnp.concatenate(parts, axis=0)
    two = update(one[0:64], inner, sums, nw_ref[1, 1], nw_ref[1, 2])
    band_ref[...] = two
    lon = lax.axis_index("lon")
    for l in range(4):

        @pl.when(lon == l)
        def _():
            own_ref[...] = two[16 * l : 16 * l + 16]


def decode_first_kernel(grid_ref, dec_ref, ew_ref, nw_ref, after_ref, recv_ref, inner_ref, hots, rows):
    index = dec_ref[...]
    rows[...] = jnp.zeros(rows.shape, F32)
    rows[0:3, :] = (slot_of(index >> 6, lax.axis_index("band")) * 64 + (index & 63)).astype(F32)
    index = rows[...].T.astype(jnp.int32)
    for k in range(3):
        hots[k * 128 : (k + 1) * 128] = one_hot(index[:, k : k + 1], 192)
    recv_ref[...] = mm(grid_ref[...], ew_ref[2, 1])
    inner_ref[...] = mm(grid_ref[...], nw_ref[2, 0])


def decode_kernel(grid_ref, own_ref, pair_ref, cross_ref, recv_ref, inner_ref, hots, ew_ref, nw_ref, out_ref):
    table = jnp.concatenate([own_ref[...], pair_ref[...], cross_ref[...]], axis=0)
    send = mm(table, ew_ref[2, 0]).astype(BF)
    recv = recv_ref[...]
    sums = None
    for k in range(3):
        before = mm(hots[k * 128 : (k + 1) * 128], send) + recv
        messages = layer_norm(mm(silu(before).astype(BF), ew_ref[2, 2]))
        sums = messages if sums is None else sums + messages
    out_ref[...] = update(grid_ref[...], inner_ref[...], sums, nw_ref[2, 1], nw_ref[2, 2])


VMEM = pl.BlockSpec(memory_space=pltpu.VMEM)
HBM = pl.BlockSpec(memory_space=pltpu.HBM)
ANY = pl.BlockSpec(memory_space=pl.ANY)
MIB = 1024 * 1024


def kernel(body, name, operands, outs, scratch=(), limit=16, products=4000, spaces=None):
    return pl.pallas_call(
        body,
        in_specs=spaces or [VMEM] * len(operands),
        out_specs=[VMEM] * len(outs),
        out_shape=[jax.ShapeDtypeStruct(dims, kind) for dims, kind in outs],
        scratch_shapes=list(scratch),
        compiler_params=pltpu.CompilerParams(vmem_limit_bytes=limit * MIB),
        cost_estimate=pl.CostEstimate(
            flops=2 * products * 512 * 512, bytes_accessed=8 * MIB, transcendentals=0
        ),
        name=name,
    )(*operands)


def per_device(
    grid_state, mesh_state, edge_weights, node_weights, enc_recv, proc_send, long_send, dec_send
):
    width = grid_state.shape[1]
    bands = lax.axis_size("band")
    across = [(i, i + 1 if i % 2 else i - 1) for i in range(1, bands - 1)]
    within = [(i, i ^ 1) for i in range(bands)]
    beyond = [(i, i + 2) for i in range(1, bands - 2, 2)]
    beyond += [(i, i - 2) for i in range(2, bands, 2)]

    def sides(pair_block, cross_block):
        cross = lax.ppermute(cross_block, "band", across)
        pair = lax.ppermute(pair_block, "band", within)
        return pair, cross

    small = pltpu.SemaphoreType.DMA((5,)), pltpu.VMEM((16, 128), F32)
    inputs = (grid_state, mesh_state, enc_recv.T, proc_send.T, long_send)
    inputs = [pltpu.with_memory_space_constraint(x, pltpu.HBM) for x in inputs]
    buffers = [pltpu.VMEM(x.shape, jnp.int32) for x in inputs[2:]]
    (packed,) = kernel(
        pack_kernel,
        "pack",
        inputs,
        [((192, width), BF)],
        [*buffers, small[1], small[0]],
        products=8000,
        spaces=[HBM] * 5,
    )
    with jax.named_scope("mesh_sides"):
        pair_state, cross_state = sides(mesh_state, mesh_state)
        packed = packed.at[144:176].set(jnp.concatenate([pair_state, cross_state], axis=0))
    with jax.named_scope("gather_lon"):
        packed = lax.all_gather(packed, "lon", axis=0)
    sent, hot, spread = kernel(
        encode_first_kernel,
        "encode_first",
        (packed, edge_weights),
        [((512, width), F32), ((1024, 192), BF), ((192, 1024), BF)],
        products=1000,
    )
    acc, p1, far, p2 = kernel(
        encode_kernel,
        "encode",
        (packed, sent, hot, spread, edge_weights),
        [((192, width), F32), ((128, width), BF), ((64, width), BF), ((128, width), BF)],
        [pltpu.VMEM((1024, width), BF)],
        products=8000,
    )
    with jax.named_scope("sum_pair"):
        r1 = lax.ppermute(p1, "band", within)
        r_far = lax.ppermute(far, "band", beyond)
    with jax.named_scope("sum_cross"):
        chip = acc[0:64] + r1[64:128].astype(F32)
        r2 = lax.ppermute(p2.at[64:128].set(chip.astype(BF)), "band", across)
    inner_one, hot = kernel(
        process_first_kernel,
        "process_first",
        (packed, node_weights, r_far),
        [((192, width), F32), ((416, 256), BF)],
        products=1000,
        spaces=[VMEM, VMEM, ANY],
    )
    recv, inner_grid, hot_grid = kernel(
        decode_first_kernel,
        "decode_first",
        (grid_state, dec_send.T, edge_weights, node_weights, r_far),
        [((128, width), F32), ((128, width), F32), ((384, 192), BF)],
        [pltpu.VMEM((8, 128), F32)],
        products=1000,
        spaces=[VMEM] * 4 + [ANY],
    )
    band_two, mesh_two = kernel(
        process_kernel,
        "process",
        (acc, r1, r2, r_far, packed, inner_one, hot, edge_weights, node_weights, recv),
        [((64, width), BF), ((16, width), BF)],
        products=8000,
        spaces=[VMEM] * 9 + [ANY],
    )
    with jax.named_scope("two_sides"):
        pair_two, cross_two = sides(band_two, band_two)
    (grid_out,) = kernel(
        decode_kernel,
        "decode",
        (grid_state, band_two, pair_two, cross_two, recv, inner_grid, hot_grid, edge_weights, node_weights),
        [((128, width), BF)],
        products=8000,
    )
    return (grid_out, mesh_two)


def solution(mesh):
    rows = P(("band", "lon"), None)
    in_specs = (rows, rows, P(), P(), rows, rows, rows, rows)
    return jax.shard_map(
        per_device, mesh=mesh, in_specs=in_specs, out_specs=(rows, rows), check_vma=False
    )
```

time: 64.1 us -> 59 us (0.920)
  the two profiles are of different devices: /device:TPU:768 before, /device:TPU:1 now
where the time goes in v2:
time: 59 us; the launch traced here: 58.7 us
  starting transfers between devices  32.8 us (56%)
  blocking collectives  11.8 us (20%)
  Pallas kernels  10 us (17%)
  waiting for transfers between devices  3.18 us (5%)
  between operations  0.84 us (1%)
    ppermute x2, starting transfers between devices, sides(): pair = lax.ppermute(pair_block, 'band', within)  14.1 us
    all_gather x1, blocking collectives, per_device(): packed = lax.all_gather(packed, 'lon', axis=0)  11.8 us
    pallas_call x7, Pallas kernels, kernel(): pl.pallas_call(body, in_specs=spaces or [VMEM] * len(operands), out_specs...  10 us
    ppermute x2, starting transfers between devices, sides(): cross = lax.ppermute(cross_block, 'band', across)  8.22 us
    ppermute x1, starting transfers between devices, per_device(): r1 = lax.ppermute(p1, 'band', within)  5.11 us
    ppermute x1, starting transfers between devices, per_device(): r2 = lax.ppermute(p2.at[64:128].set(chip.astype(BF)), 'band', across)  4.17 us
    ppermute x1, waiting for transfers between devices, per_device(): r2 = lax.ppermute(p2.at[64:128].set(chip.astype(BF)), 'band', across)  1.95 us
    ppermute x1, starting transfers between devices, per_device(): r_far = lax.ppermute(far, 'band', beyond)  1.29 us
  transfers between devices with their start and end apart: 7, of which 2 were waited for; matrix products, arithmetic and copies ran while one was open for 0% of the time, Pallas kernels for 3%

profile of v2, /device:TPU:1, one launch (start us, length us, event | category | flops | bytes accessed | tf_op | source)
XLA Modules:
  0.0 58.7 jit_solution(8535815191059140929)
XLA Ops:
  0.6 4.6 %collective-permute-start.1 = (bf16[16,512]{1,0:T(8,128)(2,1)}, bf16[16,512]{1,0:T(8,128)(2,1)S(1)}, u32[]{:S(2)}, u32[]{:S(2)}) collective-permute-start(bf16[16,512]{1,0:T(8,128)(2,1)} %mesh_ref.1), channel_id=1, source_target_pairs={{4,8},{8,4},{12,16},{16,12},{20,24},{24,20},{28,32},{32,28},{36,40... | collective-permute-start | bytes 49160 | tf_op jit(solution)/shard_map/mesh_sides/ppermute | solution.py:217
  5.2 12.1 %collective-permute-start = (bf16[16,512]{1,0:T(8,128)(2,1)}, bf16[16,512]{1,0:T(8,128)(2,1)S(1)}, u32[]{:S(2)}, u32[]{:S(2)}) collective-permute-start(bf16[16,512]{1,0:T(8,128)(2,1)} %mesh_ref.1), channel_id=1, source_target_pairs={{0,4},{4,0},{8,12},{12,8},{16,20},{20,16},{24,28},{28,24},{32,36},... | collective-permute-start | bytes 49160 | tf_op jit(solution)/shard_map/mesh_sides/ppermute | solution.py:218
  17.4 1.1 %pack.1 = bf16[192,512]{1,0:T(8,128)(2,1)S(1)} custom-call(bf16[128,512]{1,0:T(8,128)(2,1)} %grid_ref.5, bf16[16,512]{1,0:T(8,128)(2,1)} %mesh_ref.1, s32[2,128]{1,0:T(2,128)} %bitcast.13, s32[6,16]{1,0:T(8,128)} %bitcast.12, s32[1,6]{1,0:T(1,128)} %far_ref.1), custom_call_target="tpu_custom_call" | custom-call | flops 4194304000 | bytes 8388608 | tf_op jit(solution)/shard_map/pack/pallas_call | solution.py:192
  18.5 0.0 collective-permute-done.1
  18.6 11.8 %all_gather.10.all_ref = bf16[4,192,512]{2,1,0:T(8,128)(2,1)S(1)} all-gather(bf16[1,192,512]{2,1,0:T(8,128)(2,1)S(1)} %fusion.1), channel_id=1, replica_groups=mesh['band'=256,'lon'=4] {'lon'}, dimensions={0}, use_global_device_ids=true | all-gather | bytes 983040 | tf_op jit(solution)/shard_map/gather_lon/all_gather | solution.py:238
  30.3 0.6 encode_first.1
  30.9 0.0 slice-start.1
  30.9 2.2 %encode.1 = (f32[192,512]{1,0:T(8,128)S(1)}, bf16[128,512]{1,0:T(8,128)(2,1)S(1)}, bf16[64,512]{1,0:T(8,128)(2,1)S(1)}, bf16[128,512]{1,0:T(8,128)(2,1)S(1)}) custom-call(bf16[4,192,512]{2,1,0:T(8,128)(2,1)S(1)} %all_gather.10.all_ref, f32[512,512]{1,0:T(8,128)S(1)} %get-tuple-element.40.sent_ref, bf16[1024,192]{1,0:T(8,128)(2,1)S(1)} %get-tuple-element.41.hot_ref, ...), custom_call_target="tpu_custom_call" | custom-call | flops 4194304000 | bytes 8388608 | tf_op jit(solution)/shard_map/encode/pallas_call | solution.py:192
  33.1 0.0 copy-start.1
  33.1 0.0 copy-start.2
  33.1 5.1 %collective-permute-start.2 = (bf16[128,512]{1,0:T(8,128)(2,1)S(1)}, bf16[128,512]{1,0:T(8,128)(2,1)S(1)}, u32[]{:S(2)}, u32[]{:S(2)}) collective-permute-start(bf16[128,512]{1,0:T(8,128)(2,1)S(1)} %get-tuple-element.44), channel_id=1, source_target_pairs={{0,4},{4,0},{8,12},{12,8},{16,20},{20,16},{24,28},{28,24},{32,36},... | collective-permute-start | bytes 393224 | tf_op jit(solution)/shard_map/sum_pair/ppermute | solution.py:255
  38.2 1.3 %collective-permute-start.4 = (bf16[64,512]{1,0:T(8,128)(2,1)S(1)}, bf16[64,512]{1,0:T(8,128)(2,1)S(1)}, u32[]{:S(2)}, u32[]{:S(2)}) collective-permute-start(bf16[64,512]{1,0:T(8,128)(2,1)S(1)} %get-tuple-element.46), channel_id=1, source_target_pairs={{4,12},{12,20},{20,28},{28,36},{36,44},{44,52},{52,60},{60,68},{68... | collective-permute-start | bytes 196616 | tf_op jit(solution)/shard_map/sum_pair/ppermute | solution.py:256
  39.5 0.0 collective-permute-done.2.r1_ref
  39.6 4.2 %collective-permute-start.3 = (bf16[128,512]{1,0:T(8,128)(2,1)S(1)}, bf16[128,512]{1,0:T(8,128)(2,1)S(1)}, u32[]{:S(2)}, u32[]{:S(2)}) collective-permute-start(bf16[128,512]{1,0:T(8,128)(2,1)S(1)} %fusion), channel_id=1, source_target_pairs={{4,8},{8,4},{12,16},{16,12},{20,24},{24,20},{28,32},{32,28},{36,40... | collective-permute-start | bytes 393224 | tf_op jit(solution)/shard_map/sum_cross/ppermute | solution.py:259
  43.8 0.0 collective-permute-done.4.after_ref.far_ref
  43.8 0.3 process_first.1
  44.1 0.3 decode_first.1
  44.4 1.9 %collective-permute-done.3.r2_ref = bf16[128,512]{1,0:T(8,128)(2,1)S(1)} collective-permute-done((bf16[128,512]{1,0:T(8,128)(2,1)S(1)}, bf16[128,512]{1,0:T(8,128)(2,1)S(1)}, u32[]{:S(2)}, u32[]{:S(2)}) %collective-permute-start.3) | collective-permute-done | bytes 131104 | tf_op jit(solution)/shard_map/sum_cross/ppermute | solution.py:259
  46.4 3.0 %process.1 = (bf16[64,512]{1,0:T(8,128)(2,1)S(1)}, bf16[16,512]{1,0:T(8,128)(2,1)}) custom-call(f32[192,512]{1,0:T(8,128)S(1)} %get-tuple-element.43.acc_ref, bf16[128,512]{1,0:T(8,128)(2,1)S(1)} %collective-permute-done.2.r1_ref, bf16[128,512]{1,0:T(8,128)(2,1)S(1)} %collective-permute-done.3.r2_ref, ...), custom_call_target="tpu_custom_call" | custom-call | flops 4194304000 | bytes 8388608 | tf_op jit(solution)/shard_map/process/pallas_call | solution.py:192
  49.4 3.6 %collective-permute-start.6 = (bf16[64,512]{1,0:T(8,128)(2,1)S(1)}, bf16[64,512]{1,0:T(8,128)(2,1)S(1)}, u32[]{:S(2)}, u32[]{:S(2)}) collective-permute-start(bf16[64,512]{1,0:T(8,128)(2,1)S(1)} %get-tuple-element.50.own_ref), channel_id=1, source_target_pairs={{4,8},{8,4},{12,16},{16,12},{20,24},{24,20},{28,32},{32,28},{36,40... | collective-permute-start | bytes 196616 | tf_op jit(solution)/shard_map/two_sides/ppermute | solution.py:217
  53.0 1.9 %collective-permute-start.5 = (bf16[64,512]{1,0:T(8,128)(2,1)S(1)}, bf16[64,512]{1,0:T(8,128)(2,1)S(1)}, u32[]{:S(2)}, u32[]{:S(2)}) collective-permute-start(bf16[64,512]{1,0:T(8,128)(2,1)S(1)} %get-tuple-element.50.own_ref), channel_id=1, source_target_pairs={{0,4},{4,0},{8,12},{12,8},{16,20},{20,16},{24,28},{28,24},{32,36},... | collective-permute-start | bytes 196616 | tf_op jit(solution)/shard_map/two_sides/ppermute | solution.py:218
  55.0 0.0 collective-permute-done.6.cross_ref
  55.0 1.2 %collective-permute-done.5.pair_ref = bf16[64,512]{1,0:T(8,128)(2,1)S(1)} collective-permute-done((bf16[64,512]{1,0:T(8,128)(2,1)S(1)}, bf16[64,512]{1,0:T(8,128)(2,1)S(1)}, u32[]{:S(2)}, u32[]{:S(2)}) %collective-permute-start.5) | collective-permute-done | bytes 65568 | tf_op jit(solution)/shard_map/two_sides/ppermute | solution.py:218
  56.2 2.5 %decode.1 = bf16[128,512]{1,0:T(8,128)(2,1)} custom-call(bf16[128,512]{1,0:T(8,128)(2,1)S(1)} %copy-done.1, bf16[64,512]{1,0:T(8,128)(2,1)S(1)} %get-tuple-element.50.own_ref, bf16[64,512]{1,0:T(8,128)(2,1)S(1)} %collective-permute-done.5.pair_ref, bf16[64,512]{1,0:T(8,128)(2,1)S(1)} %collective-permute-done.6.cross_ref, ...), custom_call_target="tpu_custom_call" | custom-call | flops 4194304000 | bytes 8388608 | tf_op jit(solution)/shard_map/decode/pallas_call | solution.py:192
  (11 shorter events, 0.0 us)
Async XLA Ops:
  0.6 17.9 %collective-permute-start.1 = (bf16[16,512]{1,0:T(8,128)(2,1)}, bf16[16,512]{1,0:T(8,128)(2,1)S(1)}, u32[]{:S(2)}, u32[]{:S(2)}) collective-permute-start(bf16[16,512]{1,0:T(8,128)(2,1)} %mesh_ref.1), channel_id=1, source_target_pairs={{4,8},{8,4},{12,16},{16,12},{20,24},{24,20},{28,32},{32,28},{36,40... | collective-permute-start | bytes 49160 | tf_op jit(solution)/shard_map/mesh_sides/ppermute | solution.py:217
  5.2 13.3 %collective-permute-start = (bf16[16,512]{1,0:T(8,128)(2,1)}, bf16[16,512]{1,0:T(8,128)(2,1)S(1)}, u32[]{:S(2)}, u32[]{:S(2)}) collective-permute-start(bf16[16,512]{1,0:T(8,128)(2,1)} %mesh_ref.1), channel_id=1, source_target_pairs={{0,4},{4,0},{8,12},{12,8},{16,20},{20,16},{24,28},{28,24},{32,36},... | collective-permute-start | bytes 49160 | tf_op jit(solution)/shard_map/mesh_sides/ppermute | solution.py:218
  17.4 13.0 %copy-start = (bf16[3,3,512,512]{3,2,1,0:T(8,128)(2,1)S(1)}, bf16[3,3,512,512]{3,2,1,0:T(8,128)(2,1)}, u32[]{:S(2)}) copy-start(bf16[3,3,512,512]{3,2,1,0:T(8,128)(2,1)} %ew_ref.9) | copy-start | bytes 14155780
  30.3 13.4 %slice-start = ((s8[4718592]{0:T(1024)(128)(4,1)}), s8[4194304]{0:T(1024)(128)(4,1)S(1)}, s32[]{:S(2)}) async-start(s8[4718592]{0:T(1024)(128)(4,1)} %bitcast.8), calls=%async_computation | async-start | bytes 8388608
  30.9 12.9 %slice-start.1 = ((s8[4718592]{0:T(1024)(128)(4,1)}), s8[524288]{0:T(1024)(128)(4,1)S(1)}, s32[]{:S(2)}) async-start(s8[4718592]{0:T(1024)(128)(4,1)} %bitcast.8), calls=%async_computation.1 | async-start | bytes 1048576
  33.1 11.0 %copy-start.1 = (bf16[128,512]{1,0:T(8,128)(2,1)S(1)}, bf16[128,512]{1,0:T(8,128)(2,1)}, u32[]{:S(2)}) copy-start(bf16[128,512]{1,0:T(8,128)(2,1)} %grid_ref.5) | copy-start | bytes 393220
  33.1 11.0 %copy-start.2 = (s32[128,3]{0,1:T(4,128)S(1)}, s32[128,3]{0,1:T(4,128)}, u32[]{:S(2)}) copy-start(s32[128,3]{0,1:T(4,128)} %param.19) | copy-start | bytes 4612
  33.1 6.4 %collective-permute-start.2 = (bf16[128,512]{1,0:T(8,128)(2,1)S(1)}, bf16[128,512]{1,0:T(8,128)(2,1)S(1)}, u32[]{:S(2)}, u32[]{:S(2)}) collective-permute-start(bf16[128,512]{1,0:T(8,128)(2,1)S(1)} %get-tuple-element.44), channel_id=1, source_target_pairs={{0,4},{4,0},{8,12},{12,8},{16,20},{20,16},{24,28},{28,24},{32,36},... | collective-permute-start | bytes 393224 | tf_op jit(solution)/shard_map/sum_pair/ppermute | solution.py:255
  38.2 5.5 %collective-permute-start.4 = (bf16[64,512]{1,0:T(8,128)(2,1)S(1)}, bf16[64,512]{1,0:T(8,128)(2,1)S(1)}, u32[]{:S(2)}, u32[]{:S(2)}) collective-permute-start(bf16[64,512]{1,0:T(8,128)(2,1)S(1)} %get-tuple-element.46), channel_id=1, source_target_pairs={{4,12},{12,20},{20,28},{28,36},{36,44},{44,52},{52,60},{60,68},{68... | collective-permute-start | bytes 196616 | tf_op jit(solution)/shard_map/sum_pair/ppermute | solution.py:256
  39.6 6.8 %collective-permute-start.3 = (bf16[128,512]{1,0:T(8,128)(2,1)S(1)}, bf16[128,512]{1,0:T(8,128)(2,1)S(1)}, u32[]{:S(2)}, u32[]{:S(2)}) collective-permute-start(bf16[128,512]{1,0:T(8,128)(2,1)S(1)} %fusion), channel_id=1, source_target_pairs={{4,8},{8,4},{12,16},{16,12},{20,24},{24,20},{28,32},{32,28},{36,40... | collective-permute-start | bytes 393224 | tf_op jit(solution)/shard_map/sum_cross/ppermute | solution.py:259
  49.4 5.6 %collective-permute-start.6 = (bf16[64,512]{1,0:T(8,128)(2,1)S(1)}, bf16[64,512]{1,0:T(8,128)(2,1)S(1)}, u32[]{:S(2)}, u32[]{:S(2)}) collective-permute-start(bf16[64,512]{1,0:T(8,128)(2,1)S(1)} %get-tuple-element.50.own_ref), channel_id=1, source_target_pairs={{4,8},{8,4},{12,16},{16,12},{20,24},{24,20},{28,32},{32,28},{36,40... | collective-permute-start | bytes 196616 | tf_op jit(solution)/shard_map/two_sides/ppermute | solution.py:217
  53.0 3.1 %collective-permute-start.5 = (bf16[64,512]{1,0:T(8,128)(2,1)S(1)}, bf16[64,512]{1,0:T(8,128)(2,1)S(1)}, u32[]{:S(2)}, u32[]{:S(2)}) collective-permute-start(bf16[64,512]{1,0:T(8,128)(2,1)S(1)} %get-tuple-element.50.own_ref), channel_id=1, source_target_pairs={{0,4},{4,0},{8,12},{12,8},{16,20},{20,16},{24,28},{28,24},{32,36},... | collective-permute-start | bytes 196616 | tf_op jit(solution)/shard_map/two_sides/ppermute | solution.py:218

commit v3 on v2

--- a/solution.py
+++ b/solution.py
@@ -14,8 +14,7 @@
     return jnp.dot(a, b, preferred_element_type=F32)
 
 
-def silu(x):
-    half = 0.5 * x
+def silu_of_half(half):
     return half + half * jnp.tanh(half)
 
 
@@ -28,7 +27,7 @@
 
 def update(state, inner, aggregate, w1, w2):
     inner = inner + mm(aggregate.astype(BF), w1)
-    outer = layer_norm(mm(silu(inner).astype(BF), w2))
+    outer = layer_norm(mm(silu_of_half(0.5 * inner).astype(BF), w2))
     return (state.astype(F32) + outer).astype(BF)
 
 
@@ -78,7 +77,7 @@
 def encode_first_kernel(all_ref, ew_ref, sent_ref, hot_ref, spread_ref):
     rows_id = lax.broadcasted_iota(jnp.int32, (192, 128), 0)
     for l in range(4):
-        sent_ref[l * 128 : (l + 1) * 128] = mm(all_ref[l, 0:128], ew_ref[0, 0])
+        sent_ref[l * 128 : (l + 1) * 128] = 0.5 * mm(all_ref[l, 0:128], ew_ref[0, 0])
         index = all_ref[l, 176:192, 0:128].astype(F32)
         cols = index.T.astype(jnp.int32)
         flat = index.astype(jnp.int32)
@@ -88,15 +87,15 @@
             hot_ref[start : start + 128] = one_hot(cols[:, k : k + 1], 192)
 
 
-def encode_kernel(all_ref, sent_ref, hot_ref, spread_ref, ew_ref, acc_ref, p1_ref, far_ref, p2_ref, msgs):
+def encode_kernel(all_ref, sent_ref, hot_ref, spread_ref, ew_ref, acc_ref, p1_ref, far_ref, p2_ref):
     table = window(all_ref)
-    recv = mm(table, ew_ref[0, 1]).astype(BF)
+    recv = (0.5 * mm(table, ew_ref[0, 1])).astype(BF)
     for l in range(4):
         sent = sent_ref[l * 128 : (l + 1) * 128]
         before = mm(hot_ref[l * 256 : (l + 1) * 256], recv) + jnp.concatenate([sent, sent], axis=0)
-        result = layer_norm(mm(silu(before).astype(BF), ew_ref[0, 2]))
-        msgs[l * 256 : (l + 1) * 256] = result.astype(BF)
-    total = mm(spread_ref[...], msgs[...])
+        result = layer_norm(mm(silu_of_half(before).astype(BF), ew_ref[0, 2]))
+        part = mm(spread_ref[:, l * 256 : (l + 1) * 256], result.astype(BF))
+        total = part if l == 0 else total + part
     acc_ref[...] = total
     p1_ref[...] = total[0:128].astype(BF)
     cross = total[128:192].astype(BF)
@@ -105,7 +104,7 @@
     p2_ref[64:128] = cross
 
 
-def process_first_kernel(all_ref, nw_ref, after_ref, inner_ref, hots):
+def process_first_kernel(all_ref, acc_ref, r1_ref, far_ref, ew_ref, nw_ref, inner_ref, send_ref, hots):
     near_id = lax.broadcasted_iota(jnp.int32, (16, 1), 0)
     lanes = lax.broadcasted_iota(jnp.int32, (16, 256), 1)
     far = []
@@ -117,28 +116,32 @@
         far.append(jnp.logical_or(lanes[0:8] == cols[0:8, 8:9], lanes[0:8] == 192 + 16 * l))
     hots[384:416] = jnp.concatenate([jnp.where(hit, 1.0, 0.0) for hit in far], axis=0).astype(BF)
     table = window(all_ref)
-    inner_ref[...] = mm(table, nw_ref[0, 0])
+    inner = mm(table, nw_ref[0, 0])
+    inner_ref[...] = jnp.concatenate([inner[0:64], inner[128:192]], axis=0)
+    sums = acc_ref[64:128] + r1_ref[0:64].astype(F32) + far_ref[...].astype(F32)
+    one = update(table[64:128], inner[64:128], sums, nw_ref[0, 1], nw_ref[0, 2])
+    send_ref[...] = (0.5 * mm(one, ew_ref[1, 0])).astype(BF)
 
 
 def process_kernel(
-    acc_ref, r1_ref, r2_ref, far_ref, all_ref, inner_ref, hots, ew_ref, nw_ref, after_ref, band_ref, own_ref
+    acc_ref, r1_ref, r2_ref, send_ref, all_ref, inner_ref, hots, ew_ref, nw_ref, after_ref, band_ref, own_ref
 ):
     table = window(all_ref)
+    table = jnp.concatenate([table[0:64], table[128:192]], axis=0)
     own = acc_ref[0:64] + r1_ref[64:128].astype(F32) + r2_ref[0:64].astype(F32)
-    pair = acc_ref[64:128] + r1_ref[0:64].astype(F32) + far_ref[...].astype(F32)
     cross = acc_ref[128:192] + r2_ref[64:128].astype(F32)
-    sums = jnp.concatenate([own, pair, cross], axis=0)
+    sums = jnp.concatenate([own, cross], axis=0)
     one = update(table, inner_ref[...], sums, nw_ref[0, 1], nw_ref[0, 2])
-    send = mm(one, ew_ref[1, 0]).astype(BF)
-    recv = mm(one[0:64], ew_ref[1, 1]).astype(BF)
-    both = jnp.concatenate([send, recv], axis=0)
+    send = (0.5 * mm(one, ew_ref[1, 0])).astype(BF)
+    recv = (0.5 * mm(one[0:64], ew_ref[1, 1])).astype(BF)
+    both = jnp.concatenate([send[0:64], send_ref[...], send[64:128], recv], axis=0)
     inner = mm(one[0:64], nw_ref[1, 0])
     near_id = lax.broadcasted_iota(jnp.int32, (16, 1), 0)
     far_id = lax.broadcasted_iota(jnp.int32, (8, 1), 0)
     near, far = [], []
     for start, size in ((0, 192), (192, 224)):
         before = mm(hots[start : start + size], both)
-        messages = layer_norm(mm(silu(before).astype(BF), ew_ref[1, 2]))
+        messages = layer_norm(mm(silu_of_half(before).astype(BF), ew_ref[1, 2]))
         for m in range(2):
             total = messages[96 * m : 96 * m + 16]
             for k in range(1, 6):
@@ -166,18 +169,18 @@
     index = rows[...].T.astype(jnp.int32)
     for k in range(3):
         hots[k * 128 : (k + 1) * 128] = one_hot(index[:, k : k + 1], 192)
-    recv_ref[...] = mm(grid_ref[...], ew_ref[2, 1])
+    recv_ref[...] = 0.5 * mm(grid_ref[...], ew_ref[2, 1])
     inner_ref[...] = mm(grid_ref[...], nw_ref[2, 0])
 
 
 def decode_kernel(grid_ref, own_ref, pair_ref, cross_ref, recv_ref, inner_ref, hots, ew_ref, nw_ref, out_ref):
     table = jnp.concatenate([own_ref[...], pair_ref[...], cross_ref[...]], axis=0)
-    send = mm(table, ew_ref[2, 0]).astype(BF)
+    send = (0.5 * mm(table, ew_ref[2, 0])).astype(BF)
     recv = recv_ref[...]
     sums = None
     for k in range(3):
         before = mm(hots[k * 128 : (k + 1) * 128], send) + recv
-        messages = layer_norm(mm(silu(before).astype(BF), ew_ref[2, 2]))
+        messages = layer_norm(mm(silu_of_half(before).astype(BF), ew_ref[2, 2]))
         sums = messages if sums is None else sums + messages
     out_ref[...] = update(grid_ref[...], inner_ref[...], sums, nw_ref[2, 1], nw_ref[2, 2])
 
@@ -248,7 +251,6 @@
         "encode",
         (packed, sent, hot, spread, edge_weights),
         [((192, width), F32), ((128, width), BF), ((64, width), BF), ((128, width), BF)],
-        [pltpu.VMEM((1024, width), BF)],
         products=8000,
     )
     with jax.named_scope("sum_pair"):
@@ -257,13 +259,12 @@
     with jax.named_scope("sum_cross"):
         chip = acc[0:64] + r1[64:128].astype(F32)
         r2 = lax.ppermute(p2.at[64:128].set(chip.astype(BF)), "band", across)
-    inner_one, hot = kernel(
+    inner_one, send_pair, hot = kernel(
         process_first_kernel,
         "process_first",
-        (packed, node_weights, r_far),
-        [((192, width), F32), ((416, 256), BF)],
+        (packed, acc, r1, r_far, edge_weights, node_weights),
+        [((128, width), F32), ((64, width), BF), ((416, 256), BF)],
         products=1000,
-        spaces=[VMEM, VMEM, ANY],
     )
     recv, inner_grid, hot_grid = kernel(
         decode_first_kernel,
@@ -277,7 +278,7 @@
     band_two, mesh_two = kernel(
         process_kernel,
         "process",
-        (acc, r1, r2, r_far, packed, inner_one, hot, edge_weights, node_weights, recv),
+        (acc, r1, r2, send_pair, packed, inner_one, hot, edge_weights, node_weights, recv),
         [((64, width), BF), ((16, width), BF)],
         products=8000,
         spaces=[VMEM] * 9 + [ANY],

time: 59 us -> 59.2 us (level)
  Pallas kernels: 10 us -> 10.9 us
    pallas_call x7, Pallas kernels: 10 us -> 10.9 us  [kernel(): pl.pallas_call(body, in_specs=spaces or [VMEM] * len(operands), out_specs...]
  transfers between devices with their start and end apart: 7 -> 7, of which waited for: 2 -> 2; matrix products, arithmetic and copies ran while one was open for 0% -> 0% of each run, Pallas kernels for 3% -> 4%
where the time goes in v3:
time: 59.2 us; the launch traced here: 58.9 us
  starting transfers between devices  32.7 us (55%)
  blocking collectives  11.8 us (20%)
  Pallas kernels  10.9 us (18%)
  waiting for transfers between devices  2.6 us (4%)
  between operations  0.85 us (1%)
    ppermute x2, starting transfers between devices, sides(): pair = lax.ppermute(pair_block, 'band', within)  14.1 us
    all_gather x1, blocking collectives, per_device(): packed = lax.all_gather(packed, 'lon', axis=0)  11.8 us
    pallas_call x7, Pallas kernels, kernel(): pl.pallas_call(body, in_specs=spaces or [VMEM] * len(operands), out_specs...  10.9 us
    ppermute x2, starting transfers between devices, sides(): cross = lax.ppermute(cross_block, 'band', across)  8.23 us
    ppermute x1, starting transfers between devices, per_device(): r1 = lax.ppermute(p1, 'band', within)  4.99 us
    ppermute x1, starting transfers between devices, per_device(): r2 = lax.ppermute(p2.at[64:128].set(chip.astype(BF)), 'band', across)  4.17 us
    ppermute x1, waiting for transfers between devices, per_device(): r2 = lax.ppermute(p2.at[64:128].set(chip.astype(BF)), 'band', across)  1.38 us
    ppermute x1, starting transfers between devices, per_device(): r_far = lax.ppermute(far, 'band', beyond)  1.29 us
  transfers between devices with their start and end apart: 7, of which 2 were waited for; matrix products, arithmetic and copies ran while one was open for 0% of the time, Pallas kernels for 4%

profile of v3, /device:TPU:1, one launch (start us, length us, event | category | flops | bytes accessed | tf_op | source)
XLA Modules:
  0.0 58.9 jit_solution(5461943086194842631)
XLA Ops:
  0.6 4.6 %collective-permute-start.1 = (bf16[16,512]{1,0:T(8,128)(2,1)}, bf16[16,512]{1,0:T(8,128)(2,1)S(1)}, u32[]{:S(2)}, u32[]{:S(2)}) collective-permute-start(bf16[16,512]{1,0:T(8,128)(2,1)} %mesh_ref.1), channel_id=1, source_target_pairs={{4,8},{8,4},{12,16},{16,12},{20,24},{24,20},{28,32},{32,28},{36,40... | collective-permute-start | bytes 49160 | tf_op jit(solution)/shard_map/mesh_sides/ppermute | solution.py:220
  5.2 12.1 %collective-permute-start = (bf16[16,512]{1,0:T(8,128)(2,1)}, bf16[16,512]{1,0:T(8,128)(2,1)S(1)}, u32[]{:S(2)}, u32[]{:S(2)}) collective-permute-start(bf16[16,512]{1,0:T(8,128)(2,1)} %mesh_ref.1), channel_id=1, source_target_pairs={{0,4},{4,0},{8,12},{12,8},{16,20},{20,16},{24,28},{28,24},{32,36},... | collective-permute-start | bytes 49160 | tf_op jit(solution)/shard_map/mesh_sides/ppermute | solution.py:221
  17.4 1.1 %pack.1 = bf16[192,512]{1,0:T(8,128)(2,1)S(1)} custom-call(bf16[128,512]{1,0:T(8,128)(2,1)} %grid_ref.5, bf16[16,512]{1,0:T(8,128)(2,1)} %mesh_ref.1, s32[2,128]{1,0:T(2,128)} %bitcast.13, s32[6,16]{1,0:T(8,128)} %bitcast.12, s32[1,6]{1,0:T(1,128)} %far_ref.1), custom_call_target="tpu_custom_call" | custom-call | flops 4194304000 | bytes 8388608 | tf_op jit(solution)/shard_map/pack/pallas_call | solution.py:195
  18.5 0.0 collective-permute-done.1
  18.6 11.8 %all_gather.10.all_ref = bf16[4,192,512]{2,1,0:T(8,128)(2,1)S(1)} all-gather(bf16[1,192,512]{2,1,0:T(8,128)(2,1)S(1)} %fusion.1), channel_id=1, replica_groups=mesh['band'=256,'lon'=4] {'lon'}, dimensions={0}, use_global_device_ids=true | all-gather | bytes 983040 | tf_op jit(solution)/shard_map/gather_lon/all_gather | solution.py:241
  30.3 0.6 encode_first.1
  30.9 0.0 slice-start.1
  30.9 0.0 copy-start.1
  30.9 0.0 copy-start.2
  30.9 2.7 %encode.1 = (f32[192,512]{1,0:T(8,128)S(1)}, bf16[128,512]{1,0:T(8,128)(2,1)S(1)}, bf16[64,512]{1,0:T(8,128)(2,1)S(1)}, bf16[128,512]{1,0:T(8,128)(2,1)S(1)}) custom-call(bf16[4,192,512]{2,1,0:T(8,128)(2,1)S(1)} %all_gather.10.all_ref, f32[512,512]{1,0:T(8,128)S(1)} %get-tuple-element.41.sent_ref, bf16[1024,192]{1,0:T(8,128)(2,1)S(1)} %get-tuple-element.42.hot_ref, ...), custom_call_target="tpu_custom_call" | custom-call | flops 4194304000 | bytes 8388608 | tf_op jit(solution)/shard_map/encode/pallas_call | solution.py:195
  33.7 5.0 %collective-permute-start.2 = (bf16[128,512]{1,0:T(8,128)(2,1)S(1)}, bf16[128,512]{1,0:T(8,128)(2,1)S(1)}, u32[]{:S(2)}, u32[]{:S(2)}) collective-permute-start(bf16[128,512]{1,0:T(8,128)(2,1)S(1)} %get-tuple-element.45), channel_id=1, source_target_pairs={{0,4},{4,0},{8,12},{12,8},{16,20},{20,16},{24,28},{28,24},{32,36},... | collective-permute-start | bytes 393224 | tf_op jit(solution)/shard_map/sum_pair/ppermute | solution.py:257
  38.7 1.3 %collective-permute-start.4 = (bf16[64,512]{1,0:T(8,128)(2,1)S(1)}, bf16[64,512]{1,0:T(8,128)(2,1)S(1)}, u32[]{:S(2)}, u32[]{:S(2)}) collective-permute-start(bf16[64,512]{1,0:T(8,128)(2,1)S(1)} %get-tuple-element.47), channel_id=1, source_target_pairs={{4,12},{12,20},{20,28},{28,36},{36,44},{44,52},{52,60},{60,68},{68... | collective-permute-start | bytes 196616 | tf_op jit(solution)/shard_map/sum_pair/ppermute | solution.py:258
  40.0 0.0 collective-permute-done.2.r1_ref
  40.0 4.2 %collective-permute-start.3 = (bf16[128,512]{1,0:T(8,128)(2,1)S(1)}, bf16[128,512]{1,0:T(8,128)(2,1)S(1)}, u32[]{:S(2)}, u32[]{:S(2)}) collective-permute-start(bf16[128,512]{1,0:T(8,128)(2,1)S(1)} %fusion), channel_id=1, source_target_pairs={{4,8},{8,4},{12,16},{16,12},{20,24},{24,20},{28,32},{32,28},{36,40... | collective-permute-start | bytes 393224 | tf_op jit(solution)/shard_map/sum_cross/ppermute | solution.py:261
  44.2 0.0 collective-permute-done.4.far_ref.after_ref
  44.2 0.3 decode_first.1
  44.6 0.8 %process_first.1 = (f32[128,512]{1,0:T(8,128)S(1)}, bf16[64,512]{1,0:T(8,128)(2,1)S(1)}, bf16[416,256]{1,0:T(8,128)(2,1)S(1)}) custom-call(bf16[4,192,512]{2,1,0:T(8,128)(2,1)S(1)} %all_gather.10.all_ref, f32[192,512]{1,0:T(8,128)S(1)} %get-tuple-element.44.acc_ref, bf16[128,512]{1,0:T(8,128)(2,1)S(1)} %collective-permute-done.2.r1_ref, ...), custom_call_target="tpu_custom_call" | custom-call | flops 524288000 | bytes 8388608 | tf_op jit(solution)/shard_map/process_first/pallas_call | solution.py:195
  45.4 1.4 %collective-permute-done.3.r2_ref = bf16[128,512]{1,0:T(8,128)(2,1)S(1)} collective-permute-done((bf16[128,512]{1,0:T(8,128)(2,1)S(1)}, bf16[128,512]{1,0:T(8,128)(2,1)S(1)}, u32[]{:S(2)}, u32[]{:S(2)}) %collective-permute-start.3) | collective-permute-done | bytes 131104 | tf_op jit(solution)/shard_map/sum_cross/ppermute | solution.py:261
  46.8 2.9 %process.1 = (bf16[64,512]{1,0:T(8,128)(2,1)S(1)}, bf16[16,512]{1,0:T(8,128)(2,1)}) custom-call(f32[192,512]{1,0:T(8,128)S(1)} %get-tuple-element.44.acc_ref, bf16[128,512]{1,0:T(8,128)(2,1)S(1)} %collective-permute-done.2.r1_ref, bf16[128,512]{1,0:T(8,128)(2,1)S(1)} %collective-permute-done.3.r2_ref, bf16[64,512]{1,0:T(8,128)(2,1)S(1)} %get-tuple-element.48.send_ref, ...), custom_call_target="tpu_custom_call" | custom-call | flops 4194304000 | bytes 8388608 | tf_op jit(solution)/shard_map/process/pallas_call | solution.py:195
  49.7 3.6 %collective-permute-start.6 = (bf16[64,512]{1,0:T(8,128)(2,1)S(1)}, bf16[64,512]{1,0:T(8,128)(2,1)S(1)}, u32[]{:S(2)}, u32[]{:S(2)}) collective-permute-start(bf16[64,512]{1,0:T(8,128)(2,1)S(1)} %get-tuple-element.52.own_ref), channel_id=1, source_target_pairs={{4,8},{8,4},{12,16},{16,12},{20,24},{24,20},{28,32},{32,28},{36,40... | collective-permute-start | bytes 196616 | tf_op jit(solution)/shard_map/two_sides/ppermute | solution.py:220
  53.3 1.9 %collective-permute-start.5 = (bf16[64,512]{1,0:T(8,128)(2,1)S(1)}, bf16[64,512]{1,0:T(8,128)(2,1)S(1)}, u32[]{:S(2)}, u32[]{:S(2)}) collective-permute-start(bf16[64,512]{1,0:T(8,128)(2,1)S(1)} %get-tuple-element.52.own_ref), channel_id=1, source_target_pairs={{0,4},{4,0},{8,12},{12,8},{16,20},{20,16},{24,28},{28,24},{32,36},... | collective-permute-start | bytes 196616 | tf_op jit(solution)/shard_map/two_sides/ppermute | solution.py:221
  55.3 0.0 collective-permute-done.6.cross_ref
  55.3 1.2 %collective-permute-done.5.pair_ref = bf16[64,512]{1,0:T(8,128)(2,1)S(1)} collective-permute-done((bf16[64,512]{1,0:T(8,128)(2,1)S(1)}, bf16[64,512]{1,0:T(8,128)(2,1)S(1)}, u32[]{:S(2)}, u32[]{:S(2)}) %collective-permute-start.5) | collective-permute-done | bytes 65568 | tf_op jit(solution)/shard_map/two_sides/ppermute | solution.py:221
  56.5 2.4 %decode.1 = bf16[128,512]{1,0:T(8,128)(2,1)} custom-call(bf16[128,512]{1,0:T(8,128)(2,1)S(1)} %copy-done.1, bf16[64,512]{1,0:T(8,128)(2,1)S(1)} %get-tuple-element.52.own_ref, bf16[64,512]{1,0:T(8,128)(2,1)S(1)} %collective-permute-done.5.pair_ref, bf16[64,512]{1,0:T(8,128)(2,1)S(1)} %collective-permute-done.6.cross_ref, ...), custom_call_target="tpu_custom_call" | custom-call | flops 4194304000 | bytes 8388608 | tf_op jit(solution)/shard_map/decode/pallas_call | solution.py:195
  (11 shorter events, 0.0 us)
Async XLA Ops:
  0.6 17.9 %collective-permute-start.1 = (bf16[16,512]{1,0:T(8,128)(2,1)}, bf16[16,512]{1,0:T(8,128)(2,1)S(1)}, u32[]{:S(2)}, u32[]{:S(2)}) collective-permute-start(bf16[16,512]{1,0:T(8,128)(2,1)} %mesh_ref.1), channel_id=1, source_target_pairs={{4,8},{8,4},{12,16},{16,12},{20,24},{24,20},{28,32},{32,28},{36,40... | collective-permute-start | bytes 49160 | tf_op jit(solution)/shard_map/mesh_sides/ppermute | solution.py:220
  5.2 13.3 %collective-permute-start = (bf16[16,512]{1,0:T(8,128)(2,1)}, bf16[16,512]{1,0:T(8,128)(2,1)S(1)}, u32[]{:S(2)}, u32[]{:S(2)}) collective-permute-start(bf16[16,512]{1,0:T(8,128)(2,1)} %mesh_ref.1), channel_id=1, source_target_pairs={{0,4},{4,0},{8,12},{12,8},{16,20},{20,16},{24,28},{28,24},{32,36},... | collective-permute-start | bytes 49160 | tf_op jit(solution)/shard_map/mesh_sides/ppermute | solution.py:221
  17.4 13.0 %copy-start = (bf16[3,3,512,512]{3,2,1,0:T(8,128)(2,1)S(1)}, bf16[3,3,512,512]{3,2,1,0:T(8,128)(2,1)}, u32[]{:S(2)}) copy-start(bf16[3,3,512,512]{3,2,1,0:T(8,128)(2,1)} %ew_ref.11) | copy-start | bytes 14155780
  30.3 13.9 %slice-start = ((s8[4718592]{0:T(1024)(128)(4,1)}), s8[4194304]{0:T(1024)(128)(4,1)S(1)}, s32[]{:S(2)}) async-start(s8[4718592]{0:T(1024)(128)(4,1)} %bitcast.8), calls=%async_computation | async-start | bytes 8388608
  30.9 13.3 %slice-start.1 = ((s8[4718592]{0:T(1024)(128)(4,1)}), s8[524288]{0:T(1024)(128)(4,1)S(1)}, s32[]{:S(2)}) async-start(s8[4718592]{0:T(1024)(128)(4,1)} %bitcast.8), calls=%async_computation.1 | async-start | bytes 1048576
  30.9 13.3 %copy-start.1 = (bf16[128,512]{1,0:T(8,128)(2,1)S(1)}, bf16[128,512]{1,0:T(8,128)(2,1)}, u32[]{:S(2)}) copy-start(bf16[128,512]{1,0:T(8,128)(2,1)} %grid_ref.5) | copy-start | bytes 393220
  30.9 13.3 %copy-start.2 = (s32[128,3]{0,1:T(4,128)S(1)}, s32[128,3]{0,1:T(4,128)}, u32[]{:S(2)}) copy-start(s32[128,3]{0,1:T(4,128)} %param.19) | copy-start | bytes 4612
  33.7 6.3 %collective-permute-start.2 = (bf16[128,512]{1,0:T(8,128)(2,1)S(1)}, bf16[128,512]{1,0:T(8,128)(2,1)S(1)}, u32[]{:S(2)}, u32[]{:S(2)}) collective-permute-start(bf16[128,512]{1,0:T(8,128)(2,1)S(1)} %get-tuple-element.45), channel_id=1, source_target_pairs={{0,4},{4,0},{8,12},{12,8},{16,20},{20,16},{24,28},{28,24},{32,36},... | collective-permute-start | bytes 393224 | tf_op jit(solution)/shard_map/sum_pair/ppermute | solution.py:257
  38.7 5.5 %collective-permute-start.4 = (bf16[64,512]{1,0:T(8,128)(2,1)S(1)}, bf16[64,512]{1,0:T(8,128)(2,1)S(1)}, u32[]{:S(2)}, u32[]{:S(2)}) collective-permute-start(bf16[64,512]{1,0:T(8,128)(2,1)S(1)} %get-tuple-element.47), channel_id=1, source_target_pairs={{4,12},{12,20},{20,28},{28,36},{36,44},{44,52},{52,60},{60,68},{68... | collective-permute-start | bytes 196616 | tf_op jit(solution)/shard_map/sum_pair/ppermute | solution.py:258
  40.0 6.8 %collective-permute-start.3 = (bf16[128,512]{1,0:T(8,128)(2,1)S(1)}, bf16[128,512]{1,0:T(8,128)(2,1)S(1)}, u32[]{:S(2)}, u32[]{:S(2)}) collective-permute-start(bf16[128,512]{1,0:T(8,128)(2,1)S(1)} %fusion), channel_id=1, source_target_pairs={{4,8},{8,4},{12,16},{16,12},{20,24},{24,20},{28,32},{32,28},{36,40... | collective-permute-start | bytes 393224 | tf_op jit(solution)/shard_map/sum_cross/ppermute | solution.py:261
  49.7 5.6 %collective-permute-start.6 = (bf16[64,512]{1,0:T(8,128)(2,1)S(1)}, bf16[64,512]{1,0:T(8,128)(2,1)S(1)}, u32[]{:S(2)}, u32[]{:S(2)}) collective-permute-start(bf16[64,512]{1,0:T(8,128)(2,1)S(1)} %get-tuple-element.52.own_ref), channel_id=1, source_target_pairs={{4,8},{8,4},{12,16},{16,12},{20,24},{24,20},{28,32},{32,28},{36,40... | collective-permute-start | bytes 196616 | tf_op jit(solution)/shard_map/two_sides/ppermute | solution.py:220
  53.3 3.1 %collective-permute-start.5 = (bf16[64,512]{1,0:T(8,128)(2,1)S(1)}, bf16[64,512]{1,0:T(8,128)(2,1)S(1)}, u32[]{:S(2)}, u32[]{:S(2)}) collective-permute-start(bf16[64,512]{1,0:T(8,128)(2,1)S(1)} %get-tuple-element.52.own_ref), channel_id=1, source_target_pairs={{0,4},{4,0},{8,12},{12,8},{16,20},{20,16},{24,28},{28,24},{32,36},... | collective-permute-start | bytes 196616 | tf_op jit(solution)/shard_map/two_sides/ppermute | solution.py:221

commit v4 on v3

--- a/solution.py
+++ b/solution.py
@@ -76,8 +76,9 @@
 
 def encode_first_kernel(all_ref, ew_ref, sent_ref, hot_ref, spread_ref):
     rows_id = lax.broadcasted_iota(jnp.int32, (192, 128), 0)
-    for l in range(4):
-        sent_ref[l * 128 : (l + 1) * 128] = 0.5 * mm(all_ref[l, 0:128], ew_ref[0, 0])
+    grid_rows = jnp.concatenate([all_ref[l, 0:128] for l in range(4)], axis=0)
+    sent_ref[...] = 0.5 * mm(grid_rows, ew_ref[0, 0])
+    for l in range(4):
         index = all_ref[l, 176:192, 0:128].astype(F32)
         cols = index.T.astype(jnp.int32)
         flat = index.astype(jnp.int32)
@@ -87,15 +88,15 @@
             hot_ref[start : start + 128] = one_hot(cols[:, k : k + 1], 192)
 
 
-def encode_kernel(all_ref, sent_ref, hot_ref, spread_ref, ew_ref, acc_ref, p1_ref, far_ref, p2_ref):
+def encode_kernel(all_ref, sent_ref, hot_ref, spread_ref, ew_ref, acc_ref, p1_ref, far_ref, p2_ref, msgs):
     table = window(all_ref)
     recv = (0.5 * mm(table, ew_ref[0, 1])).astype(BF)
-    for l in range(4):
-        sent = sent_ref[l * 128 : (l + 1) * 128]
-        before = mm(hot_ref[l * 256 : (l + 1) * 256], recv) + jnp.concatenate([sent, sent], axis=0)
+    for n in range(2):
+        sent = [sent_ref[l * 128 : (l + 1) * 128] for l in (2 * n, 2 * n, 2 * n + 1, 2 * n + 1)]
+        before = mm(hot_ref[n * 512 : (n + 1) * 512], recv) + jnp.concatenate(sent, axis=0)
         result = layer_norm(mm(silu_of_half(before).astype(BF), ew_ref[0, 2]))
-        part = mm(spread_ref[:, l * 256 : (l + 1) * 256], result.astype(BF))
-        total = part if l == 0 else total + part
+        msgs[n * 512 : (n + 1) * 512] = result.astype(BF)
+    total = mm(spread_ref[...], msgs[...])
     acc_ref[...] = total
     p1_ref[...] = total[0:128].astype(BF)
     cross = total[128:192].astype(BF)
@@ -139,16 +140,15 @@
     near_id = lax.broadcasted_iota(jnp.int32, (16, 1), 0)
     far_id = lax.broadcasted_iota(jnp.int32, (8, 1), 0)
     near, far = [], []
-    for start, size in ((0, 192), (192, 224)):
-        before = mm(hots[start : start + size], both)
-        messages = layer_norm(mm(silu_of_half(before).astype(BF), ew_ref[1, 2]))
-        for m in range(2):
-            total = messages[96 * m : 96 * m + 16]
-            for k in range(1, 6):
-                total = total + messages[96 * m + 16 * k : 96 * m + 16 * k + 16]
-            near.append(total)
-    for l in range(4):
-        values = jnp.where(far_id < 6, messages[192 + 8 * l : 200 + 8 * l], 0.0)
+    before = mm(hots[...], both)
+    messages = layer_norm(mm(silu_of_half(before).astype(BF), ew_ref[1, 2]))
+    for l in range(4):
+        total = messages[96 * l : 96 * l + 16]
+        for k in range(1, 6):
+            total = total + messages[96 * l + 16 * k : 96 * l + 16 * k + 16]
+        near.append(total)
+    for l in range(4):
+        values = jnp.where(far_id < 6, messages[384 + 8 * l : 392 + 8 * l], 0.0)
         far.append(jnp.sum(values, axis=0, keepdims=True))
     parts = [a + jnp.where(near_id == 0, b, 0.0) for a, b in zip(near, far)]
     sums = jnp.concatenate(parts, axis=0)
@@ -177,11 +177,9 @@
     table = jnp.concatenate([own_ref[...], pair_ref[...], cross_ref[...]], axis=0)
     send = (0.5 * mm(table, ew_ref[2, 0])).astype(BF)
     recv = recv_ref[...]
-    sums = None
-    for k in range(3):
-        before = mm(hots[k * 128 : (k + 1) * 128], send) + recv
-        messages = layer_norm(mm(silu_of_half(before).astype(BF), ew_ref[2, 2]))
-        sums = messages if sums is None else sums + messages
+    before = mm(hots[...], send) + jnp.concatenate([recv, recv, recv], axis=0)
+    messages = layer_norm(mm(silu_of_half(before).astype(BF), ew_ref[2, 2]))
+    sums = messages[0:128] + messages[128:256] + messages[256:384]
     out_ref[...] = update(grid_ref[...], inner_ref[...], sums, nw_ref[2, 1], nw_ref[2, 2])
 
 
@@ -251,6 +249,7 @@
         "encode",
         (packed, sent, hot, spread, edge_weights),
         [((192, width), F32), ((128, width), BF), ((64, width), BF), ((128, width), BF)],
+        [pltpu.VMEM((1024, width), BF)],
         products=8000,
     )
     with jax.named_scope("sum_pair"):

time: 59.2 us -> 57.7 us (0.975)
  Pallas kernels: 10.9 us -> 9.49 us
    pallas_call x7, Pallas kernels: 10.9 us -> 9.49 us  [kernel(): pl.pallas_call(body, in_specs=spaces or [VMEM] * len(operands), out_specs...]
where the time goes in v4:
time: 57.7 us; the launch traced here: 57.5 us
  starting transfers between devices  32.7 us (57%)
  blocking collectives  11.8 us (20%)
  Pallas kernels  9.49 us (16%)
  waiting for transfers between devices  2.61 us (5%)
  between operations  0.85 us (1%)
    ppermute x2, starting transfers between devices, sides(): pair = lax.ppermute(pair_block, 'band', within)  14.1 us
    all_gather x1, blocking collectives, per_device(): packed = lax.all_gather(packed, 'lon', axis=0)  11.8 us
    pallas_call x7, Pallas kernels, kernel(): pl.pallas_call(body, in_specs=spaces or [VMEM] * len(operands), out_specs...  9.49 us
    ppermute x2, starting transfers between devices, sides(): cross = lax.ppermute(cross_block, 'band', across)  8.22 us
    ppermute x1, starting transfers between devices, per_device(): r1 = lax.ppermute(p1, 'band', within)  4.97 us
    ppermute x1, starting transfers between devices, per_device(): r2 = lax.ppermute(p2.at[64:128].set(chip.astype(BF)), 'band', across)  4.17 us
    ppermute x1, waiting for transfers between devices, per_device(): r2 = lax.ppermute(p2.at[64:128].set(chip.astype(BF)), 'band', across)  1.38 us
    ppermute x1, starting transfers between devices, per_device(): r_far = lax.ppermute(far, 'band', beyond)  1.29 us
  transfers between devices with their start and end apart: 7, of which 2 were waited for; matrix products, arithmetic and copies ran while one was open for 0% of the time, Pallas kernels for 4%

profile of v4, /device:TPU:1, one launch (start us, length us, event | category | flops | bytes accessed | tf_op | source)
XLA Modules:
  0.0 57.5 jit_solution(665577804689831175)
XLA Ops:
  0.6 4.6 %collective-permute-start.1 = (bf16[16,512]{1,0:T(8,128)(2,1)}, bf16[16,512]{1,0:T(8,128)(2,1)S(1)}, u32[]{:S(2)}, u32[]{:S(2)}) collective-permute-start(bf16[16,512]{1,0:T(8,128)(2,1)} %mesh_ref.1), channel_id=1, source_target_pairs={{4,8},{8,4},{12,16},{16,12},{20,24},{24,20},{28,32},{32,28},{36,40... | collective-permute-start | bytes 49160 | tf_op jit(solution)/shard_map/mesh_sides/ppermute | solution.py:218
  5.2 12.1 %collective-permute-start = (bf16[16,512]{1,0:T(8,128)(2,1)}, bf16[16,512]{1,0:T(8,128)(2,1)S(1)}, u32[]{:S(2)}, u32[]{:S(2)}) collective-permute-start(bf16[16,512]{1,0:T(8,128)(2,1)} %mesh_ref.1), channel_id=1, source_target_pairs={{0,4},{4,0},{8,12},{12,8},{16,20},{20,16},{24,28},{28,24},{32,36},... | collective-permute-start | bytes 49160 | tf_op jit(solution)/shard_map/mesh_sides/ppermute | solution.py:219
  17.4 1.1 %pack.1 = bf16[192,512]{1,0:T(8,128)(2,1)S(1)} custom-call(bf16[128,512]{1,0:T(8,128)(2,1)} %grid_ref.5, bf16[16,512]{1,0:T(8,128)(2,1)} %mesh_ref.1, s32[2,128]{1,0:T(2,128)} %bitcast.13, s32[6,16]{1,0:T(8,128)} %bitcast.12, s32[1,6]{1,0:T(1,128)} %far_ref.1), custom_call_target="tpu_custom_call" | custom-call | flops 4194304000 | bytes 8388608 | tf_op jit(solution)/shard_map/pack/pallas_call | solution.py:193
  18.5 0.0 collective-permute-done.1
  18.5 0.0 collective-permute-done
  18.6 11.8 %all_gather.10.all_ref = bf16[4,192,512]{2,1,0:T(8,128)(2,1)S(1)} all-gather(bf16[1,192,512]{2,1,0:T(8,128)(2,1)S(1)} %fusion.1), channel_id=1, replica_groups=mesh['band'=256,'lon'=4] {'lon'}, dimensions={0}, use_global_device_ids=true | all-gather | bytes 983040 | tf_op jit(solution)/shard_map/gather_lon/all_gather | solution.py:239
  30.3 0.5 encode_first.1
  30.9 0.0 slice-start.1
  30.9 0.0 copy-start.1
  30.9 0.0 copy-start.2
  30.9 1.8 %encode.1 = (f32[192,512]{1,0:T(8,128)S(1)}, bf16[128,512]{1,0:T(8,128)(2,1)S(1)}, bf16[64,512]{1,0:T(8,128)(2,1)S(1)}, bf16[128,512]{1,0:T(8,128)(2,1)S(1)}) custom-call(bf16[4,192,512]{2,1,0:T(8,128)(2,1)S(1)} %all_gather.10.all_ref, f32[512,512]{1,0:T(8,128)S(1)} %get-tuple-element.41.sent_ref, bf16[1024,192]{1,0:T(8,128)(2,1)S(1)} %get-tuple-element.42.hot_ref, ...), custom_call_target="tpu_custom_call" | custom-call | flops 4194304000 | bytes 8388608 | tf_op jit(solution)/shard_map/encode/pallas_call | solution.py:193
  32.7 5.0 %collective-permute-start.2 = (bf16[128,512]{1,0:T(8,128)(2,1)S(1)}, bf16[128,512]{1,0:T(8,128)(2,1)S(1)}, u32[]{:S(2)}, u32[]{:S(2)}) collective-permute-start(bf16[128,512]{1,0:T(8,128)(2,1)S(1)} %get-tuple-element.45), channel_id=1, source_target_pairs={{0,4},{4,0},{8,12},{12,8},{16,20},{20,16},{24,28},{28,24},{32,36},... | collective-permute-start | bytes 393224 | tf_op jit(solution)/shard_map/sum_pair/ppermute | solution.py:256
  37.7 1.3 %collective-permute-start.4 = (bf16[64,512]{1,0:T(8,128)(2,1)S(1)}, bf16[64,512]{1,0:T(8,128)(2,1)S(1)}, u32[]{:S(2)}, u32[]{:S(2)}) collective-permute-start(bf16[64,512]{1,0:T(8,128)(2,1)S(1)} %get-tuple-element.47), channel_id=1, source_target_pairs={{4,12},{12,20},{20,28},{28,36},{36,44},{44,52},{52,60},{60,68},{68... | collective-permute-start | bytes 196616 | tf_op jit(solution)/shard_map/sum_pair/ppermute | solution.py:257
  39.0 0.0 collective-permute-done.2.r1_ref
  39.0 4.2 %collective-permute-start.3 = (bf16[128,512]{1,0:T(8,128)(2,1)S(1)}, bf16[128,512]{1,0:T(8,128)(2,1)S(1)}, u32[]{:S(2)}, u32[]{:S(2)}) collective-permute-start(bf16[128,512]{1,0:T(8,128)(2,1)S(1)} %fusion), channel_id=1, source_target_pairs={{4,8},{8,4},{12,16},{16,12},{20,24},{24,20},{28,32},{32,28},{36,40... | collective-permute-start | bytes 393224 | tf_op jit(solution)/shard_map/sum_cross/ppermute | solution.py:260
  43.3 0.3 decode_first.1
  43.6 0.8 %process_first.1 = (f32[128,512]{1,0:T(8,128)S(1)}, bf16[64,512]{1,0:T(8,128)(2,1)S(1)}, bf16[416,256]{1,0:T(8,128)(2,1)S(1)}) custom-call(bf16[4,192,512]{2,1,0:T(8,128)(2,1)S(1)} %all_gather.10.all_ref, f32[192,512]{1,0:T(8,128)S(1)} %get-tuple-element.44.acc_ref, bf16[128,512]{1,0:T(8,128)(2,1)S(1)} %collective-permute-done.2.r1_ref, ...), custom_call_target="tpu_custom_call" | custom-call | flops 524288000 | bytes 8388608 | tf_op jit(solution)/shard_map/process_first/pallas_call | solution.py:193
  44.5 1.4 %collective-permute-done.3.r2_ref = bf16[128,512]{1,0:T(8,128)(2,1)S(1)} collective-permute-done((bf16[128,512]{1,0:T(8,128)(2,1)S(1)}, bf16[128,512]{1,0:T(8,128)(2,1)S(1)}, u32[]{:S(2)}, u32[]{:S(2)}) %collective-permute-start.3) | collective-permute-done | bytes 131104 | tf_op jit(solution)/shard_map/sum_cross/ppermute | solution.py:260
  45.8 2.7 %process.1 = (bf16[64,512]{1,0:T(8,128)(2,1)S(1)}, bf16[16,512]{1,0:T(8,128)(2,1)}) custom-call(f32[192,512]{1,0:T(8,128)S(1)} %get-tuple-element.44.acc_ref, bf16[128,512]{1,0:T(8,128)(2,1)S(1)} %collective-permute-done.2.r1_ref, bf16[128,512]{1,0:T(8,128)(2,1)S(1)} %collective-permute-done.3.r2_ref, bf16[64,512]{1,0:T(8,128)(2,1)S(1)} %get-tuple-element.48.send_ref, ...), custom_call_target="tpu_custom_call" | custom-call | flops 4194304000 | bytes 8388608 | tf_op jit(solution)/shard_map/process/pallas_call | solution.py:193
  48.5 3.6 %collective-permute-start.6 = (bf16[64,512]{1,0:T(8,128)(2,1)S(1)}, bf16[64,512]{1,0:T(8,128)(2,1)S(1)}, u32[]{:S(2)}, u32[]{:S(2)}) collective-permute-start(bf16[64,512]{1,0:T(8,128)(2,1)S(1)} %get-tuple-element.52.own_ref), channel_id=1, source_target_pairs={{4,8},{8,4},{12,16},{16,12},{20,24},{24,20},{28,32},{32,28},{36,40... | collective-permute-start | bytes 196616 | tf_op jit(solution)/shard_map/two_sides/ppermute | solution.py:218
  52.2 1.9 %collective-permute-start.5 = (bf16[64,512]{1,0:T(8,128)(2,1)S(1)}, bf16[64,512]{1,0:T(8,128)(2,1)S(1)}, u32[]{:S(2)}, u32[]{:S(2)}) collective-permute-start(bf16[64,512]{1,0:T(8,128)(2,1)S(1)} %get-tuple-element.52.own_ref), channel_id=1, source_target_pairs={{0,4},{4,0},{8,12},{12,8},{16,20},{20,16},{24,28},{28,24},{32,36},... | collective-permute-start | bytes 196616 | tf_op jit(solution)/shard_map/two_sides/ppermute | solution.py:219
  54.1 0.0 collective-permute-done.6.cross_ref
  54.1 1.2 %collective-permute-done.5.pair_ref = bf16[64,512]{1,0:T(8,128)(2,1)S(1)} collective-permute-done((bf16[64,512]{1,0:T(8,128)(2,1)S(1)}, bf16[64,512]{1,0:T(8,128)(2,1)S(1)}, u32[]{:S(2)}, u32[]{:S(2)}) %collective-permute-start.5) | collective-permute-done | bytes 65568 | tf_op jit(solution)/shard_map/two_sides/ppermute | solution.py:219
  55.3 2.1 %decode.1 = bf16[128,512]{1,0:T(8,128)(2,1)} custom-call(bf16[128,512]{1,0:T(8,128)(2,1)S(1)} %copy-done.1, bf16[64,512]{1,0:T(8,128)(2,1)S(1)} %get-tuple-element.52.own_ref, bf16[64,512]{1,0:T(8,128)(2,1)S(1)} %collective-permute-done.5.pair_ref, bf16[64,512]{1,0:T(8,128)(2,1)S(1)} %collective-permute-done.6.cross_ref, ...), custom_call_target="tpu_custom_call" | custom-call | flops 4194304000 | bytes 8388608 | tf_op jit(solution)/shard_map/decode/pallas_call | solution.py:193
  (11 shorter events, 0.0 us)
Async XLA Ops:
  0.6 17.9 %collective-permute-start.1 = (bf16[16,512]{1,0:T(8,128)(2,1)}, bf16[16,512]{1,0:T(8,128)(2,1)S(1)}, u32[]{:S(2)}, u32[]{:S(2)}) collective-permute-start(bf16[16,512]{1,0:T(8,128)(2,1)} %mesh_ref.1), channel_id=1, source_target_pairs={{4,8},{8,4},{12,16},{16,12},{20,24},{24,20},{28,32},{32,28},{36,40... | collective-permute-start | bytes 49160 | tf_op jit(solution)/shard_map/mesh_sides/ppermute | solution.py:218
  5.2 13.3 %collective-permute-start = (bf16[16,512]{1,0:T(8,128)(2,1)}, bf16[16,512]{1,0:T(8,128)(2,1)S(1)}, u32[]{:S(2)}, u32[]{:S(2)}) collective-permute-start(bf16[16,512]{1,0:T(8,128)(2,1)} %mesh_ref.1), channel_id=1, source_target_pairs={{0,4},{4,0},{8,12},{12,8},{16,20},{20,16},{24,28},{28,24},{32,36},... | collective-permute-start | bytes 49160 | tf_op jit(solution)/shard_map/mesh_sides/ppermute | solution.py:219
  17.4 13.0 %copy-start = (bf16[3,3,512,512]{3,2,1,0:T(8,128)(2,1)S(1)}, bf16[3,3,512,512]{3,2,1,0:T(8,128)(2,1)}, u32[]{:S(2)}) copy-start(bf16[3,3,512,512]{3,2,1,0:T(8,128)(2,1)} %ew_ref.11) | copy-start | bytes 14155780
  30.3 12.9 %slice-start = ((s8[4718592]{0:T(1024)(128)(4,1)}), s8[4194304]{0:T(1024)(128)(4,1)S(1)}, s32[]{:S(2)}) async-start(s8[4718592]{0:T(1024)(128)(4,1)} %bitcast.8), calls=%async_computation | async-start | bytes 8388608
  30.9 12.3 %slice-start.1 = ((s8[4718592]{0:T(1024)(128)(4,1)}), s8[524288]{0:T(1024)(128)(4,1)S(1)}, s32[]{:S(2)}) async-start(s8[4718592]{0:T(1024)(128)(4,1)} %bitcast.8), calls=%async_computation.1 | async-start | bytes 1048576
  30.9 12.3 %copy-start.1 = (bf16[128,512]{1,0:T(8,128)(2,1)S(1)}, bf16[128,512]{1,0:T(8,128)(2,1)}, u32[]{:S(2)}) copy-start(bf16[128,512]{1,0:T(8,128)(2,1)} %grid_ref.5) | copy-start | bytes 393220
  30.9 12.3 %copy-start.2 = (s32[128,3]{0,1:T(4,128)S(1)}, s32[128,3]{0,1:T(4,128)}, u32[]{:S(2)}) copy-start(s32[128,3]{0,1:T(4,128)} %param.19) | copy-start | bytes 4612
  32.7 6.3 %collective-permute-start.2 = (bf16[128,512]{1,0:T(8,128)(2,1)S(1)}, bf16[128,512]{1,0:T(8,128)(2,1)S(1)}, u32[]{:S(2)}, u32[]{:S(2)}) collective-permute-start(bf16[128,512]{1,0:T(8,128)(2,1)S(1)} %get-tuple-element.45), channel_id=1, source_target_pairs={{0,4},{4,0},{8,12},{12,8},{16,20},{20,16},{24,28},{28,24},{32,36},... | collective-permute-start | bytes 393224 | tf_op jit(solution)/shard_map/sum_pair/ppermute | solution.py:256
  37.7 5.5 %collective-permute-start.4 = (bf16[64,512]{1,0:T(8,128)(2,1)S(1)}, bf16[64,512]{1,0:T(8,128)(2,1)S(1)}, u32[]{:S(2)}, u32[]{:S(2)}) collective-permute-start(bf16[64,512]{1,0:T(8,128)(2,1)S(1)} %get-tuple-element.47), channel_id=1, source_target_pairs={{4,12},{12,20},{20,28},{28,36},{36,44},{44,52},{52,60},{60,68},{68... | collective-permute-start | bytes 196616 | tf_op jit(solution)/shard_map/sum_pair/ppermute | solution.py:257
  39.0 6.8 %collective-permute-start.3 = (bf16[128,512]{1,0:T(8,128)(2,1)S(1)}, bf16[128,512]{1,0:T(8,128)(2,1)S(1)}, u32[]{:S(2)}, u32[]{:S(2)}) collective-permute-start(bf16[128,512]{1,0:T(8,128)(2,1)S(1)} %fusion), channel_id=1, source_target_pairs={{4,8},{8,4},{12,16},{16,12},{20,24},{24,20},{28,32},{32,28},{36,40... | collective-permute-start | bytes 393224 | tf_op jit(solution)/shard_map/sum_cross/ppermute | solution.py:260
  48.5 5.6 %collective-permute-start.6 = (bf16[64,512]{1,0:T(8,128)(2,1)S(1)}, bf16[64,512]{1,0:T(8,128)(2,1)S(1)}, u32[]{:S(2)}, u32[]{:S(2)}) collective-permute-start(bf16[64,512]{1,0:T(8,128)(2,1)S(1)} %get-tuple-element.52.own_ref), channel_id=1, source_target_pairs={{4,8},{8,4},{12,16},{16,12},{20,24},{24,20},{28,32},{32,28},{36,40... | collective-permute-start | bytes 196616 | tf_op jit(solution)/shard_map/two_sides/ppermute | solution.py:218
  52.2 3.1 %collective-permute-start.5 = (bf16[64,512]{1,0:T(8,128)(2,1)S(1)}, bf16[64,512]{1,0:T(8,128)(2,1)S(1)}, u32[]{:S(2)}, u32[]{:S(2)}) collective-permute-start(bf16[64,512]{1,0:T(8,128)(2,1)S(1)} %get-tuple-element.52.own_ref), channel_id=1, source_target_pairs={{0,4},{4,0},{8,12},{12,8},{16,20},{20,16},{24,28},{28,24},{32,36},... | collective-permute-start | bytes 196616 | tf_op jit(solution)/shard_map/two_sides/ppermute | solution.py:219

commit v5 on v4

--- a/solution.py
+++ b/solution.py
@@ -62,16 +62,18 @@
     far = far_buf[...]
     rows[8:9, 0:6] = (slot_of(far >> 2, band) * 64 + (far & 3) * 16).astype(F32)
     index = rows[...].astype(BF)
-    out_ref[176:192, 0:128] = index
-    out_ref[176:192, 128:512] = jnp.zeros((16, 384), BF)
+    out_ref[160:176, 0:128] = index
+    out_ref[160:176, 128:512] = jnp.zeros((16, 384), BF)
     for copy in large:
         copy.wait()
 
 
-def window(all_ref):
-    return jnp.concatenate(
-        [all_ref[l, 128 + 16 * s : 144 + 16 * s] for s in range(3) for l in range(4)], axis=0
-    )
+def mesh_rows(all_ref, start):
+    return jnp.concatenate([all_ref[l, start : start + 16] for l in range(4)], axis=0)
+
+
+def window(all_ref, pair_ref):
+    return jnp.concatenate([mesh_rows(all_ref, 128), pair_ref[...], mesh_rows(all_ref, 144)], axis=0)
 
 
 def encode_first_kernel(all_ref, ew_ref, sent_ref, hot_ref, spread_ref):
@@ -79,7 +81,7 @@
     grid_rows = jnp.concatenate([all_ref[l, 0:128] for l in range(4)], axis=0)
     sent_ref[...] = 0.5 * mm(grid_rows, ew_ref[0, 0])
     for l in range(4):
-        index = all_ref[l, 176:192, 0:128].astype(F32)
+        index = all_ref[l, 160:176, 0:128].astype(F32)
         cols = index.T.astype(jnp.int32)
         flat = index.astype(jnp.int32)
         for k in range(2):
@@ -88,8 +90,8 @@
             hot_ref[start : start + 128] = one_hot(cols[:, k : k + 1], 192)
 
 
-def encode_kernel(all_ref, sent_ref, hot_ref, spread_ref, ew_ref, acc_ref, p1_ref, far_ref, p2_ref, msgs):
-    table = window(all_ref)
+def encode_kernel(all_ref, pair_ref, sent_ref, hot_ref, spread_ref, ew_ref, acc_ref, p1_ref, far_ref, p2_ref, msgs):
+    table = window(all_ref, pair_ref)
     recv = (0.5 * mm(table, ew_ref[0, 1])).astype(BF)
     for n in range(2):
         sent = [sent_ref[l * 128 : (l + 1) * 128] for l in (2 * n, 2 * n, 2 * n + 1, 2 * n + 1)]
@@ -105,18 +107,18 @@
     p2_ref[64:128] = cross
 
 
-def process_first_kernel(all_ref, acc_ref, r1_ref, far_ref, ew_ref, nw_ref, inner_ref, send_ref, hots):
+def process_first_kernel(all_ref, pair_ref, acc_ref, r1_ref, far_ref, ew_ref, nw_ref, inner_ref, send_ref, hots):
     near_id = lax.broadcasted_iota(jnp.int32, (16, 1), 0)
     lanes = lax.broadcasted_iota(jnp.int32, (16, 256), 1)
     far = []
     for l in range(4):
-        cols = all_ref[l, 176:192, 0:128].astype(F32).T.astype(jnp.int32)
+        cols = all_ref[l, 160:176, 0:128].astype(F32).T.astype(jnp.int32)
         for k in range(6):
             hit = jnp.logical_or(lanes == cols[0:16, 2 + k : 3 + k], lanes == near_id + (192 + 16 * l))
             hots[l * 96 + 16 * k : l * 96 + 16 * k + 16] = jnp.where(hit, 1.0, 0.0).astype(BF)
         far.append(jnp.logical_or(lanes[0:8] == cols[0:8, 8:9], lanes[0:8] == 192 + 16 * l))
     hots[384:416] = jnp.concatenate([jnp.where(hit, 1.0, 0.0) for hit in far], axis=0).astype(BF)
-    table = window(all_ref)
+    table = window(all_ref, pair_ref)
     inner = mm(table, nw_ref[0, 0])
     inner_ref[...] = jnp.concatenate([inner[0:64], inner[128:192]], axis=0)
     sums = acc_ref[64:128] + r1_ref[0:64].astype(F32) + far_ref[...].astype(F32)
@@ -127,8 +129,7 @@
 def process_kernel(
     acc_ref, r1_ref, r2_ref, send_ref, all_ref, inner_ref, hots, ew_ref, nw_ref, after_ref, band_ref, own_ref
 ):
-    table = window(all_ref)
-    table = jnp.concatenate([table[0:64], table[128:192]], axis=0)
+    table = jnp.concatenate([mesh_rows(all_ref, 128), mesh_rows(all_ref, 144)], axis=0)
     own = acc_ref[0:64] + r1_ref[64:128].astype(F32) + r2_ref[0:64].astype(F32)
     cross = acc_ref[128:192] + r2_ref[64:128].astype(F32)
     sums = jnp.concatenate([own, cross], axis=0)
@@ -227,16 +228,17 @@
         pack_kernel,
         "pack",
         inputs,
-        [((192, width), BF)],
+        [((176, width), BF)],
         [*buffers, small[1], small[0]],
         products=8000,
         spaces=[HBM] * 5,
     )
-    with jax.named_scope("mesh_sides"):
-        pair_state, cross_state = sides(mesh_state, mesh_state)
-        packed = packed.at[144:176].set(jnp.concatenate([pair_state, cross_state], axis=0))
+    with jax.named_scope("mesh_cross"):
+        packed = packed.at[144:160].set(lax.ppermute(mesh_state, "band", across))
     with jax.named_scope("gather_lon"):
         packed = lax.all_gather(packed, "lon", axis=0)
+    with jax.named_scope("mesh_pair"):
+        pair_state = lax.ppermute(packed[:, 128:144].reshape(64, width), "band", within)
     sent, hot, spread = kernel(
         encode_first_kernel,
         "encode_first",
@@ -247,7 +249,7 @@
     acc, p1, far, p2 = kernel(
         encode_kernel,
         "encode",
-        (packed, sent, hot, spread, edge_weights),
+        (packed, pair_state, sent, hot, spread, edge_weights),
         [((192, width), F32), ((128, width), BF), ((64, width), BF), ((128, width), BF)],
         [pltpu.VMEM((1024, width), BF)],
         products=8000,
@@ -261,7 +263,7 @@
     inner_one, send_pair, hot = kernel(
         process_first_kernel,
         "process_first",
-        (packed, acc, r1, r_far, edge_weights, node_weights),
+        (packed, pair_state, acc, r1, r_far, edge_weights, node_weights),
         [((128, width), F32), ((64, width), BF), ((416, 256), BF)],
         products=1000,
     )

time: 57.7 us -> 58.7 us (1.017)
  the two profiles are of different devices: /device:TPU:1 before, /device:TPU:505 now
where the time goes in v5:
time: 58.7 us; the launch traced here: 58.4 us
  starting transfers between devices  22.3 us (38%)
  waiting for transfers between devices  14.1 us (24%)
  blocking collectives  11.5 us (20%)
  Pallas kernels  9.55 us (16%)
  between operations  0.81 us (1%)
    all_gather x1, blocking collectives, per_device(): packed = lax.all_gather(packed, 'lon', axis=0)  11.5 us
    pallas_call x7, Pallas kernels, kernel(): pl.pallas_call(body, in_specs=spaces or [VMEM] * len(operands), out_specs...  9.55 us
    ppermute x1, starting transfers between devices, per_device(): r_far = lax.ppermute(far, 'band', beyond)  6.98 us
    ppermute x1, waiting for transfers between devices, per_device(): r2 = lax.ppermute(p2.at[64:128].set(chip.astype(BF)), 'band', across)  6.37 us
    ppermute x1, waiting for transfers between devices, sides(): cross = lax.ppermute(cross_block, 'band', across)  5.02 us
    ppermute x1, starting transfers between devices, per_device(): packed = packed.at[144:160].set(lax.ppermute(mesh_state, 'band', across))  4.98 us
    ppermute x1, waiting for transfers between devices, per_device(): packed = packed.at[144:160].set(lax.ppermute(mesh_state, 'band', across))  2.44 us
    ppermute x1, starting transfers between devices, per_device(): r1 = lax.ppermute(p1, 'band', within)  2.27 us
  transfers between devices with their start and end apart: 7, of which 4 were waited for; matrix products, arithmetic and copies ran while one was open for 0% of the time, Pallas kernels for 5%

profile of v5, /device:TPU:505, one launch (start us, length us, event | category | flops | bytes accessed | tf_op | source)
XLA Modules:
  0.0 58.4 jit_solution(4082905346383013566)
XLA Ops:
  0.6 5.0 %collective-permute-start = (bf16[16,512]{1,0:T(8,128)(2,1)}, bf16[16,512]{1,0:T(8,128)(2,1)S(1)}, u32[]{:S(2)}, u32[]{:S(2)}) collective-permute-start(bf16[16,512]{1,0:T(8,128)(2,1)} %mesh_ref.1), channel_id=1, source_target_pairs={{4,8},{8,4},{12,16},{16,12},{20,24},{24,20},{28,32},{32,28},{36,40... | collective-permute-start | bytes 49160 | tf_op jit(solution)/shard_map/mesh_cross/ppermute | solution.py:237
  5.6 0.0 copy-start
  5.6 1.1 %pack.1 = bf16[176,512]{1,0:T(8,128)(2,1)S(1)} custom-call(bf16[128,512]{1,0:T(8,128)(2,1)} %grid_ref.5, bf16[16,512]{1,0:T(8,128)(2,1)} %mesh_ref.1, s32[2,128]{1,0:T(2,128)} %bitcast.13, s32[6,16]{1,0:T(8,128)} %bitcast.12, s32[1,6]{1,0:T(1,128)} %far_ref.1), custom_call_target="tpu_custom_call" | custom-call | flops 4194304000 | bytes 8388608 | tf_op jit(solution)/shard_map/pack/pallas_call | solution.py:194
  6.8 2.4 %collective-permute-done = bf16[16,512]{1,0:T(8,128)(2,1)S(1)} collective-permute-done((bf16[16,512]{1,0:T(8,128)(2,1)}, bf16[16,512]{1,0:T(8,128)(2,1)S(1)}, u32[]{:S(2)}, u32[]{:S(2)}) %collective-permute-start) | collective-permute-done | bytes 16416 | tf_op jit(solution)/shard_map/mesh_cross/ppermute | solution.py:237
  9.2 11.5 %all_gather.10.all_ref = bf16[4,176,512]{2,1,0:T(8,128)(2,1)S(1)} all-gather(bf16[1,176,512]{2,1,0:T(8,128)(2,1)S(1)} %bitcast_dynamic-update-slice_fusion), channel_id=1, replica_groups=mesh['band'=256,'lon'=4] {'lon'}, dimensions={0}, use_global_device_ids=true | all-gather | bytes 901120 | tf_op jit(solution)/shard_map/gather_lon/all_gather | solution.py:239
  20.8 2.2 %collective-permute-start.1 = (bf16[64,512]{1,0:T(8,128)(2,1)S(1)}, bf16[64,512]{1,0:T(8,128)(2,1)S(1)}, u32[]{:S(2)}, u32[]{:S(2)}) collective-permute-start(bf16[64,512]{1,0:T(8,128)(2,1)S(1)} %bitcast.11), channel_id=1, source_target_pairs={{0,4},{4,0},{8,12},{12,8},{16,20},{20,16},{24,28},{28,24},{32,36},... | collective-permute-start | bytes 196616 | tf_op jit(solution)/shard_map/mesh_pair/ppermute | solution.py:241
  23.0 0.0 slice-start
  23.1 0.5 encode_first.1
  23.6 0.3 collective-permute-done.1.pair_ref
  23.9 1.8 %encode.1 = (f32[192,512]{1,0:T(8,128)S(1)}, bf16[128,512]{1,0:T(8,128)(2,1)S(1)}, bf16[64,512]{1,0:T(8,128)(2,1)S(1)}, bf16[128,512]{1,0:T(8,128)(2,1)S(1)}) custom-call(bf16[4,176,512]{2,1,0:T(8,128)(2,1)S(1)} %all_gather.10.all_ref, bf16[64,512]{1,0:T(8,128)(2,1)S(1)} %collective-permute-done.1.pair_ref, f32[512,512]{1,0:T(8,128)S(1)} %get-tuple-element.41.sent_ref, ...), custom_call_target="tpu_custom_call" | custom-call | flops 4194304000 | bytes 8388608 | tf_op jit(solution)/shard_map/encode/pallas_call | solution.py:194
  25.7 2.3 %collective-permute-start.2 = (bf16[128,512]{1,0:T(8,128)(2,1)S(1)}, bf16[128,512]{1,0:T(8,128)(2,1)S(1)}, u32[]{:S(2)}, u32[]{:S(2)}) collective-permute-start(bf16[128,512]{1,0:T(8,128)(2,1)S(1)} %get-tuple-element.45), channel_id=1, source_target_pairs={{0,4},{4,0},{8,12},{12,8},{16,20},{20,16},{24,28},{28,24},{32,36},... | collective-permute-start | bytes 393224 | tf_op jit(solution)/shard_map/sum_pair/ppermute | solution.py:258
  28.0 7.0 %collective-permute-start.4 = (bf16[64,512]{1,0:T(8,128)(2,1)S(1)}, bf16[64,512]{1,0:T(8,128)(2,1)S(1)}, u32[]{:S(2)}, u32[]{:S(2)}) collective-permute-start(bf16[64,512]{1,0:T(8,128)(2,1)S(1)} %get-tuple-element.47), channel_id=1, source_target_pairs={{4,12},{12,20},{20,28},{28,36},{36,44},{44,52},{52,60},{60,68},{68... | collective-permute-start | bytes 196616 | tf_op jit(solution)/shard_map/sum_pair/ppermute | solution.py:259
  35.0 0.0 collective-permute-done.2.r1_ref
  35.0 2.0 %collective-permute-start.3 = (bf16[128,512]{1,0:T(8,128)(2,1)S(1)}, bf16[128,512]{1,0:T(8,128)(2,1)S(1)}, u32[]{:S(2)}, u32[]{:S(2)}) collective-permute-start(bf16[128,512]{1,0:T(8,128)(2,1)S(1)} %fusion), channel_id=1, source_target_pairs={{4,8},{8,4},{12,16},{16,12},{20,24},{24,20},{28,32},{32,28},{36,40... | collective-permute-start | bytes 393224 | tf_op jit(solution)/shard_map/sum_cross/ppermute | solution.py:262
  37.0 0.0 collective-permute-done.4.far_ref.after_ref
  37.1 0.3 decode_first.1
  37.4 0.9 %process_first.1 = (f32[128,512]{1,0:T(8,128)S(1)}, bf16[64,512]{1,0:T(8,128)(2,1)S(1)}, bf16[416,256]{1,0:T(8,128)(2,1)S(1)}) custom-call(bf16[4,176,512]{2,1,0:T(8,128)(2,1)S(1)} %all_gather.10.all_ref, bf16[64,512]{1,0:T(8,128)(2,1)S(1)} %collective-permute-done.1.pair_ref, f32[192,512]{1,0:T(8,128)S(1)} %get-tuple-element.44.acc_ref, ...), custom_call_target="tpu_custom_call" | custom-call | flops 524288000 | bytes 8388608 | tf_op jit(solution)/shard_map/process_first/pallas_call | solution.py:194
  38.3 6.4 %collective-permute-done.3.r2_ref = bf16[128,512]{1,0:T(8,128)(2,1)S(1)} collective-permute-done((bf16[128,512]{1,0:T(8,128)(2,1)S(1)}, bf16[128,512]{1,0:T(8,128)(2,1)S(1)}, u32[]{:S(2)}, u32[]{:S(2)}) %collective-permute-start.3) | collective-permute-done | bytes 131104 | tf_op jit(solution)/shard_map/sum_cross/ppermute | solution.py:262
  44.6 2.7 %process.1 = (bf16[64,512]{1,0:T(8,128)(2,1)S(1)}, bf16[16,512]{1,0:T(8,128)(2,1)}) custom-call(f32[192,512]{1,0:T(8,128)S(1)} %get-tuple-element.44.acc_ref, bf16[128,512]{1,0:T(8,128)(2,1)S(1)} %collective-permute-done.2.r1_ref, bf16[128,512]{1,0:T(8,128)(2,1)S(1)} %collective-permute-done.3.r2_ref, bf16[64,512]{1,0:T(8,128)(2,1)S(1)} %get-tuple-element.48.send_ref, ...), custom_call_target="tpu_custom_call" | custom-call | flops 4194304000 | bytes 8388608 | tf_op jit(solution)/shard_map/process/pallas_call | solution.py:194
  47.4 1.9 %collective-permute-start.6 = (bf16[64,512]{1,0:T(8,128)(2,1)S(1)}, bf16[64,512]{1,0:T(8,128)(2,1)S(1)}, u32[]{:S(2)}, u32[]{:S(2)}) collective-permute-start(bf16[64,512]{1,0:T(8,128)(2,1)S(1)} %get-tuple-element.52.own_ref), channel_id=1, source_target_pairs={{4,8},{8,4},{12,16},{16,12},{20,24},{24,20},{28,32},{32,28},{36,40... | collective-permute-start | bytes 196616 | tf_op jit(solution)/shard_map/two_sides/ppermute | solution.py:219
  49.3 1.9 %collective-permute-start.5 = (bf16[64,512]{1,0:T(8,128)(2,1)S(1)}, bf16[64,512]{1,0:T(8,128)(2,1)S(1)}, u32[]{:S(2)}, u32[]{:S(2)}) collective-permute-start(bf16[64,512]{1,0:T(8,128)(2,1)S(1)} %get-tuple-element.52.own_ref), channel_id=1, source_target_pairs={{0,4},{4,0},{8,12},{12,8},{16,20},{20,16},{24,28},{28,24},{32,36},... | collective-permute-start | bytes 196616 | tf_op jit(solution)/shard_map/two_sides/ppermute | solution.py:220
  51.2 5.0 %collective-permute-done.6.cross_ref = bf16[64,512]{1,0:T(8,128)(2,1)S(1)} collective-permute-done((bf16[64,512]{1,0:T(8,128)(2,1)S(1)}, bf16[64,512]{1,0:T(8,128)(2,1)S(1)}, u32[]{:S(2)}, u32[]{:S(2)}) %collective-permute-start.6) | collective-permute-done | bytes 65568 | tf_op jit(solution)/shard_map/two_sides/ppermute | solution.py:219
  56.2 0.0 collective-permute-done.5.pair_ref
  56.3 2.1 %decode.1 = bf16[128,512]{1,0:T(8,128)(2,1)} custom-call(bf16[128,512]{1,0:T(8,128)(2,1)S(1)} %copy-done.1, bf16[64,512]{1,0:T(8,128)(2,1)S(1)} %get-tuple-element.52.own_ref, bf16[64,512]{1,0:T(8,128)(2,1)S(1)} %collective-permute-done.5.pair_ref, bf16[64,512]{1,0:T(8,128)(2,1)S(1)} %collective-permute-done.6.cross_ref, ...), custom_call_target="tpu_custom_call" | custom-call | flops 4194304000 | bytes 8388608 | tf_op jit(solution)/shard_map/decode/pallas_call | solution.py:194
  (12 shorter events, 0.0 us)
Async XLA Ops:
  0.6 8.6 %collective-permute-start = (bf16[16,512]{1,0:T(8,128)(2,1)}, bf16[16,512]{1,0:T(8,128)(2,1)S(1)}, u32[]{:S(2)}, u32[]{:S(2)}) collective-permute-start(bf16[16,512]{1,0:T(8,128)(2,1)} %mesh_ref.1), channel_id=1, source_target_pairs={{4,8},{8,4},{12,16},{16,12},{20,24},{24,20},{28,32},{32,28},{36,40... | collective-permute-start | bytes 49160 | tf_op jit(solution)/shard_map/mesh_cross/ppermute | solution.py:237
  5.6 17.4 %copy-start = (bf16[3,3,512,512]{3,2,1,0:T(8,128)(2,1)S(1)}, bf16[3,3,512,512]{3,2,1,0:T(8,128)(2,1)}, u32[]{:S(2)}) copy-start(bf16[3,3,512,512]{3,2,1,0:T(8,128)(2,1)} %ew_ref.11) | copy-start | bytes 14155780
  20.8 3.1 %collective-permute-start.1 = (bf16[64,512]{1,0:T(8,128)(2,1)S(1)}, bf16[64,512]{1,0:T(8,128)(2,1)S(1)}, u32[]{:S(2)}, u32[]{:S(2)}) collective-permute-start(bf16[64,512]{1,0:T(8,128)(2,1)S(1)} %bitcast.11), channel_id=1, source_target_pairs={{0,4},{4,0},{8,12},{12,8},{16,20},{20,16},{24,28},{28,24},{32,36},... | collective-permute-start | bytes 196616 | tf_op jit(solution)/shard_map/mesh_pair/ppermute | solution.py:241
  23.0 14.0 %slice-start = ((s8[4718592]{0:T(1024)(128)(4,1)}), s8[4194304]{0:T(1024)(128)(4,1)S(1)}, s32[]{:S(2)}) async-start(s8[4718592]{0:T(1024)(128)(4,1)} %bitcast.7), calls=%async_computation | async-start | bytes 8388608
  23.9 13.1 %slice-start.1 = ((s8[4718592]{0:T(1024)(128)(4,1)}), s8[524288]{0:T(1024)(128)(4,1)S(1)}, s32[]{:S(2)}) async-start(s8[4718592]{0:T(1024)(128)(4,1)} %bitcast.7), calls=%async_computation.1 | async-start | bytes 1048576
  23.9 13.1 %copy-start.1 = (bf16[128,512]{1,0:T(8,128)(2,1)S(1)}, bf16[128,512]{1,0:T(8,128)(2,1)}, u32[]{:S(2)}) copy-start(bf16[128,512]{1,0:T(8,128)(2,1)} %grid_ref.5) | copy-start | bytes 393220
  23.9 13.1 %copy-start.2 = (s32[128,3]{0,1:T(4,128)S(1)}, s32[128,3]{0,1:T(4,128)}, u32[]{:S(2)}) copy-start(s32[128,3]{0,1:T(4,128)} %param.19) | copy-start | bytes 4612
  25.7 9.3 %collective-permute-start.2 = (bf16[128,512]{1,0:T(8,128)(2,1)S(1)}, bf16[128,512]{1,0:T(8,128)(2,1)S(1)}, u32[]{:S(2)}, u32[]{:S(2)}) collective-permute-start(bf16[128,512]{1,0:T(8,128)(2,1)S(1)} %get-tuple-element.45), channel_id=1, source_target_pairs={{0,4},{4,0},{8,12},{12,8},{16,20},{20,16},{24,28},{28,24},{32,36},... | collective-permute-start | bytes 393224 | tf_op jit(solution)/shard_map/sum_pair/ppermute | solution.py:258
  28.0 9.0 %collective-permute-start.4 = (bf16[64,512]{1,0:T(8,128)(2,1)S(1)}, bf16[64,512]{1,0:T(8,128)(2,1)S(1)}, u32[]{:S(2)}, u32[]{:S(2)}) collective-permute-start(bf16[64,512]{1,0:T(8,128)(2,1)S(1)} %get-tuple-element.47), channel_id=1, source_target_pairs={{4,12},{12,20},{20,28},{28,36},{36,44},{44,52},{52,60},{60,68},{68... | collective-permute-start | bytes 196616 | tf_op jit(solution)/shard_map/sum_pair/ppermute | solution.py:259
  35.0 9.6 %collective-permute-start.3 = (bf16[128,512]{1,0:T(8,128)(2,1)S(1)}, bf16[128,512]{1,0:T(8,128)(2,1)S(1)}, u32[]{:S(2)}, u32[]{:S(2)}) collective-permute-start(bf16[128,512]{1,0:T(8,128)(2,1)S(1)} %fusion), channel_id=1, source_target_pairs={{4,8},{8,4},{12,16},{16,12},{20,24},{24,20},{28,32},{32,28},{36,40... | collective-permute-start | bytes 393224 | tf_op jit(solution)/shard_map/sum_cross/ppermute | solution.py:262
  47.4 8.9 %collective-permute-start.6 = (bf16[64,512]{1,0:T(8,128)(2,1)S(1)}, bf16[64,512]{1,0:T(8,128)(2,1)S(1)}, u32[]{:S(2)}, u32[]{:S(2)}) collective-permute-start(bf16[64,512]{1,0:T(8,128)(2,1)S(1)} %get-tuple-element.52.own_ref), channel_id=1, source_target_pairs={{4,8},{8,4},{12,16},{16,12},{20,24},{24,20},{28,32},{32,28},{36,40... | collective-permute-start | bytes 196616 | tf_op jit(solution)/shard_map/two_sides/ppermute | solution.py:219
  49.3 6.9 %collective-permute-start.5 = (bf16[64,512]{1,0:T(8,128)(2,1)S(1)}, bf16[64,512]{1,0:T(8,128)(2,1)S(1)}, u32[]{:S(2)}, u32[]{:S(2)}) collective-permute-start(bf16[64,512]{1,0:T(8,128)(2,1)S(1)} %get-tuple-element.52.own_ref), channel_id=1, source_target_pairs={{0,4},{4,0},{8,12},{12,8},{16,20},{20,16},{24,28},{28,24},{32,36},... | collective-permute-start | bytes 196616 | tf_op jit(solution)/shard_map/two_sides/ppermute | solution.py:220

commit v6 on v4

--- a/solution.py
+++ b/solution.py
@@ -74,7 +74,7 @@
     )
 
 
-def encode_first_kernel(all_ref, ew_ref, sent_ref, hot_ref, spread_ref):
+def encode_first(all_ref, ew_ref, sent_ref, hot_ref, spread_ref):
     rows_id = lax.broadcasted_iota(jnp.int32, (192, 128), 0)
     grid_rows = jnp.concatenate([all_ref[l, 0:128] for l in range(4)], axis=0)
     sent_ref[...] = 0.5 * mm(grid_rows, ew_ref[0, 0])
@@ -88,7 +88,8 @@
             hot_ref[start : start + 128] = one_hot(cols[:, k : k + 1], 192)
 
 
-def encode_kernel(all_ref, sent_ref, hot_ref, spread_ref, ew_ref, acc_ref, p1_ref, far_ref, p2_ref, msgs):
+def encode_kernel(all_ref, ew_ref, acc_ref, p1_ref, far_ref, p2_ref, msgs, sent_ref, hot_ref, spread_ref):
+    encode_first(all_ref, ew_ref, sent_ref, hot_ref, spread_ref)
     table = window(all_ref)
     recv = (0.5 * mm(table, ew_ref[0, 1])).astype(BF)
     for n in range(2):
@@ -237,19 +238,17 @@
         packed = packed.at[144:176].set(jnp.concatenate([pair_state, cross_state], axis=0))
     with jax.named_scope("gather_lon"):
         packed = lax.all_gather(packed, "lon", axis=0)
-    sent, hot, spread = kernel(
-        encode_first_kernel,
-        "encode_first",
-        (packed, edge_weights),
-        [((512, width), F32), ((1024, 192), BF), ((192, 1024), BF)],
-        products=1000,
-    )
     acc, p1, far, p2 = kernel(
         encode_kernel,
         "encode",
-        (packed, sent, hot, spread, edge_weights),
+        (packed, edge_weights),
         [((192, width), F32), ((128, width), BF), ((64, width), BF), ((128, width), BF)],
-        [pltpu.VMEM((1024, width), BF)],
+        [
+            pltpu.VMEM((1024, width), BF),
+            pltpu.VMEM((512, width), F32),
+            pltpu.VMEM((1024, 192), BF),
+            pltpu.VMEM((192, 1024), BF),
+        ],
         products=8000,
     )
     with jax.named_scope("sum_pair"):

time: 57.7 us -> 57.6 us (level)
    pallas_call x7 -> x6, Pallas kernels: 9.49 us -> 9.4 us  [kernel(): pl.pallas_call(body, in_specs=spaces or [VMEM] * len(operands), out_specs...]
where the time goes in v6:
time: 57.6 us; the launch traced here: 57.3 us
  starting transfers between devices  32.7 us (57%)
  blocking collectives  11.7 us (20%)
  Pallas kernels  9.4 us (16%)
  waiting for transfers between devices  2.61 us (5%)
  between operations  0.83 us (1%)
    ppermute x2, starting transfers between devices, sides(): pair = lax.ppermute(pair_block, 'band', within)  14.1 us
    all_gather x1, blocking collectives, per_device(): packed = lax.all_gather(packed, 'lon', axis=0)  11.7 us
    pallas_call x6, Pallas kernels, kernel(): pl.pallas_call(body, in_specs=spaces or [VMEM] * len(operands), out_specs...  9.4 us
    ppermute x2, starting transfers between devices, sides(): cross = lax.ppermute(cross_block, 'band', across)  8.21 us
    ppermute x1, starting transfers between devices, per_device(): r1 = lax.ppermute(p1, 'band', within)  4.97 us
    ppermute x1, starting transfers between devices, per_device(): r2 = lax.ppermute(p2.at[64:128].set(chip.astype(BF)), 'band', across)  4.17 us
    ppermute x1, waiting for transfers between devices, per_device(): r2 = lax.ppermute(p2.at[64:128].set(chip.astype(BF)), 'band', across)  1.38 us
    ppermute x1, starting transfers between devices, per_device(): r_far = lax.ppermute(far, 'band', beyond)  1.29 us
  transfers between devices with their start and end apart: 7, of which 2 were waited for; matrix products, arithmetic and copies ran while one was open for 0% of the time, Pallas kernels for 4%

profile of v6, /device:TPU:1, one launch (start us, length us, event | category | flops | bytes accessed | tf_op | source)
XLA Modules:
  0.0 57.3 jit_solution(1223793644953740350)
XLA Ops:
  0.6 4.6 %collective-permute-start.1 = (bf16[16,512]{1,0:T(8,128)(2,1)}, bf16[16,512]{1,0:T(8,128)(2,1)S(1)}, u32[]{:S(2)}, u32[]{:S(2)}) collective-permute-start(bf16[16,512]{1,0:T(8,128)(2,1)} %mesh_ref.1), channel_id=1, source_target_pairs={{4,8},{8,4},{12,16},{16,12},{20,24},{24,20},{28,32},{32,28},{36,40... | collective-permute-start | bytes 49160 | tf_op jit(solution)/shard_map/mesh_sides/ppermute | solution.py:219
  5.2 12.1 %collective-permute-start = (bf16[16,512]{1,0:T(8,128)(2,1)}, bf16[16,512]{1,0:T(8,128)(2,1)S(1)}, u32[]{:S(2)}, u32[]{:S(2)}) collective-permute-start(bf16[16,512]{1,0:T(8,128)(2,1)} %mesh_ref.1), channel_id=1, source_target_pairs={{0,4},{4,0},{8,12},{12,8},{16,20},{20,16},{24,28},{28,24},{32,36},... | collective-permute-start | bytes 49160 | tf_op jit(solution)/shard_map/mesh_sides/ppermute | solution.py:220
  17.4 0.0 copy-start
  17.4 1.1 %pack.1 = bf16[192,512]{1,0:T(8,128)(2,1)S(1)} custom-call(bf16[128,512]{1,0:T(8,128)(2,1)} %grid_ref.5, bf16[16,512]{1,0:T(8,128)(2,1)} %mesh_ref.1, s32[2,128]{1,0:T(2,128)} %bitcast.13, s32[6,16]{1,0:T(8,128)} %bitcast.12, s32[1,6]{1,0:T(1,128)} %far_ref.1), custom_call_target="tpu_custom_call" | custom-call | flops 4194304000 | bytes 8388608 | tf_op jit(solution)/shard_map/pack/pallas_call | solution.py:194
  18.5 0.0 collective-permute-done.1
  18.5 0.0 collective-permute-done
  18.6 0.0 slice-start
  18.6 11.7 %all_gather.10.all_ref = bf16[4,192,512]{2,1,0:T(8,128)(2,1)S(1)} all-gather(bf16[1,192,512]{2,1,0:T(8,128)(2,1)S(1)} %fusion.1), channel_id=1, replica_groups=mesh['band'=256,'lon'=4] {'lon'}, dimensions={0}, use_global_device_ids=true | all-gather | bytes 983040 | tf_op jit(solution)/shard_map/gather_lon/all_gather | solution.py:240
  30.3 0.0 copy-start.2
  30.4 2.2 %encode.1 = (f32[192,512]{1,0:T(8,128)S(1)}, bf16[128,512]{1,0:T(8,128)(2,1)S(1)}, bf16[64,512]{1,0:T(8,128)(2,1)S(1)}, bf16[128,512]{1,0:T(8,128)(2,1)S(1)}) custom-call(bf16[4,192,512]{2,1,0:T(8,128)(2,1)S(1)} %all_gather.10.all_ref, bf16[3,3,512,512]{3,2,1,0:T(8,128)(2,1)S(1)} %copy-done), custom_call_target="tpu_custom_call" | custom-call | flops 4194304000 | bytes 8388608 | tf_op jit(solution)/shard_map/encode/pallas_call | solution.py:194
  32.6 5.0 %collective-permute-start.2 = (bf16[128,512]{1,0:T(8,128)(2,1)S(1)}, bf16[128,512]{1,0:T(8,128)(2,1)S(1)}, u32[]{:S(2)}, u32[]{:S(2)}) collective-permute-start(bf16[128,512]{1,0:T(8,128)(2,1)S(1)} %get-tuple-element.39), channel_id=1, source_target_pairs={{0,4},{4,0},{8,12},{12,8},{16,20},{20,16},{24,28},{28,24},{32,36},... | collective-permute-start | bytes 393224 | tf_op jit(solution)/shard_map/sum_pair/ppermute | solution.py:255
  37.6 1.3 %collective-permute-start.4 = (bf16[64,512]{1,0:T(8,128)(2,1)S(1)}, bf16[64,512]{1,0:T(8,128)(2,1)S(1)}, u32[]{:S(2)}, u32[]{:S(2)}) collective-permute-start(bf16[64,512]{1,0:T(8,128)(2,1)S(1)} %get-tuple-element.41), channel_id=1, source_target_pairs={{4,12},{12,20},{20,28},{28,36},{36,44},{44,52},{52,60},{60,68},{68... | collective-permute-start | bytes 196616 | tf_op jit(solution)/shard_map/sum_pair/ppermute | solution.py:256
  38.9 0.0 collective-permute-done.2.r1_ref
  38.9 4.2 %collective-permute-start.3 = (bf16[128,512]{1,0:T(8,128)(2,1)S(1)}, bf16[128,512]{1,0:T(8,128)(2,1)S(1)}, u32[]{:S(2)}, u32[]{:S(2)}) collective-permute-start(bf16[128,512]{1,0:T(8,128)(2,1)S(1)} %fusion), channel_id=1, source_target_pairs={{4,8},{8,4},{12,16},{16,12},{20,24},{24,20},{28,32},{32,28},{36,40... | collective-permute-start | bytes 393224 | tf_op jit(solution)/shard_map/sum_cross/ppermute | solution.py:259
  43.1 0.0 collective-permute-done.4.far_ref.after_ref
  43.1 0.3 decode_first.1
  43.5 0.8 %process_first.1 = (f32[128,512]{1,0:T(8,128)S(1)}, bf16[64,512]{1,0:T(8,128)(2,1)S(1)}, bf16[416,256]{1,0:T(8,128)(2,1)S(1)}) custom-call(bf16[4,192,512]{2,1,0:T(8,128)(2,1)S(1)} %all_gather.10.all_ref, f32[192,512]{1,0:T(8,128)S(1)} %get-tuple-element.38.acc_ref, bf16[128,512]{1,0:T(8,128)(2,1)S(1)} %collective-permute-done.2.r1_ref, ...), custom_call_target="tpu_custom_call" | custom-call | flops 524288000 | bytes 8388608 | tf_op jit(solution)/shard_map/process_first/pallas_call | solution.py:194
  44.3 1.4 %collective-permute-done.3.r2_ref = bf16[128,512]{1,0:T(8,128)(2,1)S(1)} collective-permute-done((bf16[128,512]{1,0:T(8,128)(2,1)S(1)}, bf16[128,512]{1,0:T(8,128)(2,1)S(1)}, u32[]{:S(2)}, u32[]{:S(2)}) %collective-permute-start.3) | collective-permute-done | bytes 131104 | tf_op jit(solution)/shard_map/sum_cross/ppermute | solution.py:259
  45.7 2.7 %process.1 = (bf16[64,512]{1,0:T(8,128)(2,1)S(1)}, bf16[16,512]{1,0:T(8,128)(2,1)}) custom-call(f32[192,512]{1,0:T(8,128)S(1)} %get-tuple-element.38.acc_ref, bf16[128,512]{1,0:T(8,128)(2,1)S(1)} %collective-permute-done.2.r1_ref, bf16[128,512]{1,0:T(8,128)(2,1)S(1)} %collective-permute-done.3.r2_ref, bf16[64,512]{1,0:T(8,128)(2,1)S(1)} %get-tuple-element.42.send_ref, ...), custom_call_target="tpu_custom_call" | custom-call | flops 4194304000 | bytes 8388608 | tf_op jit(solution)/shard_map/process/pallas_call | solution.py:194
  48.4 3.6 %collective-permute-start.6 = (bf16[64,512]{1,0:T(8,128)(2,1)S(1)}, bf16[64,512]{1,0:T(8,128)(2,1)S(1)}, u32[]{:S(2)}, u32[]{:S(2)}) collective-permute-start(bf16[64,512]{1,0:T(8,128)(2,1)S(1)} %get-tuple-element.46.own_ref), channel_id=1, source_target_pairs={{4,8},{8,4},{12,16},{16,12},{20,24},{24,20},{28,32},{32,28},{36,40... | collective-permute-start | bytes 196616 | tf_op jit(solution)/shard_map/two_sides/ppermute | solution.py:219
  52.0 1.9 %collective-permute-start.5 = (bf16[64,512]{1,0:T(8,128)(2,1)S(1)}, bf16[64,512]{1,0:T(8,128)(2,1)S(1)}, u32[]{:S(2)}, u32[]{:S(2)}) collective-permute-start(bf16[64,512]{1,0:T(8,128)(2,1)S(1)} %get-tuple-element.46.own_ref), channel_id=1, source_target_pairs={{0,4},{4,0},{8,12},{12,8},{16,20},{20,16},{24,28},{28,24},{32,36},... | collective-permute-start | bytes 196616 | tf_op jit(solution)/shard_map/two_sides/ppermute | solution.py:220
  54.0 0.0 collective-permute-done.6.cross_ref
  54.0 1.2 %collective-permute-done.5.pair_ref = bf16[64,512]{1,0:T(8,128)(2,1)S(1)} collective-permute-done((bf16[64,512]{1,0:T(8,128)(2,1)S(1)}, bf16[64,512]{1,0:T(8,128)(2,1)S(1)}, u32[]{:S(2)}, u32[]{:S(2)}) %collective-permute-start.5) | collective-permute-done | bytes 65568 | tf_op jit(solution)/shard_map/two_sides/ppermute | solution.py:220
  55.2 2.1 %decode.1 = bf16[128,512]{1,0:T(8,128)(2,1)} custom-call(bf16[128,512]{1,0:T(8,128)(2,1)S(1)} %copy-done.1, bf16[64,512]{1,0:T(8,128)(2,1)S(1)} %get-tuple-element.46.own_ref, bf16[64,512]{1,0:T(8,128)(2,1)S(1)} %collective-permute-done.5.pair_ref, bf16[64,512]{1,0:T(8,128)(2,1)S(1)} %collective-permute-done.6.cross_ref, ...), custom_call_target="tpu_custom_call" | custom-call | flops 4194304000 | bytes 8388608 | tf_op jit(solution)/shard_map/decode/pallas_call | solution.py:194
  (10 shorter events, 0.0 us)
Async XLA Ops:
  0.6 17.9 %collective-permute-start.1 = (bf16[16,512]{1,0:T(8,128)(2,1)}, bf16[16,512]{1,0:T(8,128)(2,1)S(1)}, u32[]{:S(2)}, u32[]{:S(2)}) collective-permute-start(bf16[16,512]{1,0:T(8,128)(2,1)} %mesh_ref.1), channel_id=1, source_target_pairs={{4,8},{8,4},{12,16},{16,12},{20,24},{24,20},{28,32},{32,28},{36,40... | collective-permute-start | bytes 49160 | tf_op jit(solution)/shard_map/mesh_sides/ppermute | solution.py:219
  5.2 13.3 %collective-permute-start = (bf16[16,512]{1,0:T(8,128)(2,1)}, bf16[16,512]{1,0:T(8,128)(2,1)S(1)}, u32[]{:S(2)}, u32[]{:S(2)}) collective-permute-start(bf16[16,512]{1,0:T(8,128)(2,1)} %mesh_ref.1), channel_id=1, source_target_pairs={{0,4},{4,0},{8,12},{12,8},{16,20},{20,16},{24,28},{28,24},{32,36},... | collective-permute-start | bytes 49160 | tf_op jit(solution)/shard_map/mesh_sides/ppermute | solution.py:220
  17.4 13.0 %copy-start = (bf16[3,3,512,512]{3,2,1,0:T(8,128)(2,1)S(1)}, bf16[3,3,512,512]{3,2,1,0:T(8,128)(2,1)}, u32[]{:S(2)}) copy-start(bf16[3,3,512,512]{3,2,1,0:T(8,128)(2,1)} %ew_ref.9) | copy-start | bytes 14155780
  18.6 24.5 %slice-start = ((s8[4718592]{0:T(1024)(128)(4,1)}), s8[4194304]{0:T(1024)(128)(4,1)S(1)}, s32[]{:S(2)}) async-start(s8[4718592]{0:T(1024)(128)(4,1)} %bitcast.8), calls=%async_computation | async-start | bytes 8388608
  30.3 12.8 %slice-start.1 = ((s8[4718592]{0:T(1024)(128)(4,1)}), s8[524288]{0:T(1024)(128)(4,1)S(1)}, s32[]{:S(2)}) async-start(s8[4718592]{0:T(1024)(128)(4,1)} %bitcast.8), calls=%async_computation.1 | async-start | bytes 1048576
  30.3 12.8 %copy-start.1 = (bf16[128,512]{1,0:T(8,128)(2,1)S(1)}, bf16[128,512]{1,0:T(8,128)(2,1)}, u32[]{:S(2)}) copy-start(bf16[128,512]{1,0:T(8,128)(2,1)} %grid_ref.5) | copy-start | bytes 393220
  30.3 12.8 %copy-start.2 = (s32[128,3]{0,1:T(4,128)S(1)}, s32[128,3]{0,1:T(4,128)}, u32[]{:S(2)}) copy-start(s32[128,3]{0,1:T(4,128)} %param.19) | copy-start | bytes 4612
  32.6 6.3 %collective-permute-start.2 = (bf16[128,512]{1,0:T(8,128)(2,1)S(1)}, bf16[128,512]{1,0:T(8,128)(2,1)S(1)}, u32[]{:S(2)}, u32[]{:S(2)}) collective-permute-start(bf16[128,512]{1,0:T(8,128)(2,1)S(1)} %get-tuple-element.39), channel_id=1, source_target_pairs={{0,4},{4,0},{8,12},{12,8},{16,20},{20,16},{24,28},{28,24},{32,36},... | collective-permute-start | bytes 393224 | tf_op jit(solution)/shard_map/sum_pair/ppermute | solution.py:255
  37.6 5.5 %collective-permute-start.4 = (bf16[64,512]{1,0:T(8,128)(2,1)S(1)}, bf16[64,512]{1,0:T(8,128)(2,1)S(1)}, u32[]{:S(2)}, u32[]{:S(2)}) collective-permute-start(bf16[64,512]{1,0:T(8,128)(2,1)S(1)} %get-tuple-element.41), channel_id=1, source_target_pairs={{4,12},{12,20},{20,28},{28,36},{36,44},{44,52},{52,60},{60,68},{68... | collective-permute-start | bytes 196616 | tf_op jit(solution)/shard_map/sum_pair/ppermute | solution.py:256
  38.9 6.8 %collective-permute-start.3 = (bf16[128,512]{1,0:T(8,128)(2,1)S(1)}, bf16[128,512]{1,0:T(8,128)(2,1)S(1)}, u32[]{:S(2)}, u32[]{:S(2)}) collective-permute-start(bf16[128,512]{1,0:T(8,128)(2,1)S(1)} %fusion), channel_id=1, source_target_pairs={{4,8},{8,4},{12,16},{16,12},{20,24},{24,20},{28,32},{32,28},{36,40... | collective-permute-start | bytes 393224 | tf_op jit(solution)/shard_map/sum_cross/ppermute | solution.py:259
  48.4 5.6 %collective-permute-start.6 = (bf16[64,512]{1,0:T(8,128)(2,1)S(1)}, bf16[64,512]{1,0:T(8,128)(2,1)S(1)}, u32[]{:S(2)}, u32[]{:S(2)}) collective-permute-start(bf16[64,512]{1,0:T(8,128)(2,1)S(1)} %get-tuple-element.46.own_ref), channel_id=1, source_target_pairs={{4,8},{8,4},{12,16},{16,12},{20,24},{24,20},{28,32},{32,28},{36,40... | collective-permute-start | bytes 196616 | tf_op jit(solution)/shard_map/two_sides/ppermute | solution.py:219
  52.0 3.1 %collective-permute-start.5 = (bf16[64,512]{1,0:T(8,128)(2,1)S(1)}, bf16[64,512]{1,0:T(8,128)(2,1)S(1)}, u32[]{:S(2)}, u32[]{:S(2)}) collective-permute-start(bf16[64,512]{1,0:T(8,128)(2,1)S(1)} %get-tuple-element.46.own_ref), channel_id=1, source_target_pairs={{0,4},{4,0},{8,12},{12,8},{16,20},{20,16},{24,28},{28,24},{32,36},... | collective-permute-start | bytes 196616 | tf_op jit(solution)/shard_map/two_sides/ppermute | solution.py:220

commit v7 on v6

--- a/solution.py
+++ b/solution.py
@@ -74,10 +74,8 @@
     )
 
 
-def encode_first(all_ref, ew_ref, sent_ref, hot_ref, spread_ref):
+def encode_first(all_ref, hot_ref, spread_ref):
     rows_id = lax.broadcasted_iota(jnp.int32, (192, 128), 0)
-    grid_rows = jnp.concatenate([all_ref[l, 0:128] for l in range(4)], axis=0)
-    sent_ref[...] = 0.5 * mm(grid_rows, ew_ref[0, 0])
     for l in range(4):
         index = all_ref[l, 176:192, 0:128].astype(F32)
         cols = index.T.astype(jnp.int32)
@@ -88,12 +86,14 @@
             hot_ref[start : start + 128] = one_hot(cols[:, k : k + 1], 192)
 
 
-def encode_kernel(all_ref, ew_ref, acc_ref, p1_ref, far_ref, p2_ref, msgs, sent_ref, hot_ref, spread_ref):
-    encode_first(all_ref, ew_ref, sent_ref, hot_ref, spread_ref)
+def encode_kernel(all_ref, ew_ref, acc_ref, p1_ref, far_ref, p2_ref, msgs, hot_ref, spread_ref):
+    encode_first(all_ref, hot_ref, spread_ref)
     table = window(all_ref)
     recv = (0.5 * mm(table, ew_ref[0, 1])).astype(BF)
     for n in range(2):
-        sent = [sent_ref[l * 128 : (l + 1) * 128] for l in (2 * n, 2 * n, 2 * n + 1, 2 * n + 1)]
+        grid_rows = jnp.concatenate([all_ref[2 * n, 0:128], all_ref[2 * n + 1, 0:128]], axis=0)
+        sent = 0.5 * mm(grid_rows, ew_ref[0, 0])
+        sent = [sent[0:128], sent[0:128], sent[128:256], sent[128:256]]
         before = mm(hot_ref[n * 512 : (n + 1) * 512], recv) + jnp.concatenate(sent, axis=0)
         result = layer_norm(mm(silu_of_half(before).astype(BF), ew_ref[0, 2]))
         msgs[n * 512 : (n + 1) * 512] = result.astype(BF)
@@ -245,7 +245,6 @@
         [((192, width), F32), ((128, width), BF), ((64, width), BF), ((128, width), BF)],
         [
             pltpu.VMEM((1024, width), BF),
-            pltpu.VMEM((512, width), F32),
             pltpu.VMEM((1024, 192), BF),
             pltpu.VMEM((192, 1024), BF),
         ],

time: 57.6 us -> 57.6 us (level)
  no operation moved by 1% of the time
where the time goes in v7:
time: 57.6 us; the launch traced here: 57.3 us
  starting transfers between devices  32.7 us (57%)
  blocking collectives  11.7 us (20%)
  Pallas kernels  9.32 us (16%)
  waiting for transfers between devices  2.6 us (5%)
  between operations  0.84 us (1%)
    ppermute x2, starting transfers between devices, sides(): pair = lax.ppermute(pair_block, 'band', within)  14.1 us
    all_gather x1, blocking collectives, per_device(): packed = lax.all_gather(packed, 'lon', axis=0)  11.7 us
    pallas_call x6, Pallas kernels, kernel(): pl.pallas_call(body, in_specs=spaces or [VMEM] * len(operands), out_specs...  9.32 us
    ppermute x2, starting transfers between devices, sides(): cross = lax.ppermute(cross_block, 'band', across)  8.23 us
    ppermute x1, starting transfers between devices, per_device(): r1 = lax.ppermute(p1, 'band', within)  4.97 us
    ppermute x1, starting transfers between devices, per_device(): r2 = lax.ppermute(p2.at[64:128].set(chip.astype(BF)), 'band', across)  4.17 us
    ppermute x1, waiting for transfers between devices, per_device(): r2 = lax.ppermute(p2.at[64:128].set(chip.astype(BF)), 'band', across)  1.38 us
    ppermute x1, starting transfers between devices, per_device(): r_far = lax.ppermute(far, 'band', beyond)  1.29 us
  transfers between devices with their start and end apart: 7, of which 2 were waited for; matrix products, arithmetic and copies ran while one was open for 0% of the time, Pallas kernels for 4%

profile of v7, /device:TPU:1, one launch (start us, length us, event | category | flops | bytes accessed | tf_op | source)
XLA Modules:
  0.0 57.3 jit_solution(1081319328594806470)
XLA Ops:
  0.6 4.6 %collective-permute-start.1 = (bf16[16,512]{1,0:T(8,128)(2,1)}, bf16[16,512]{1,0:T(8,128)(2,1)S(1)}, u32[]{:S(2)}, u32[]{:S(2)}) collective-permute-start(bf16[16,512]{1,0:T(8,128)(2,1)} %mesh_ref.1), channel_id=1, source_target_pairs={{4,8},{8,4},{12,16},{16,12},{20,24},{24,20},{28,32},{32,28},{36,40... | collective-permute-start | bytes 49160 | tf_op jit(solution)/shard_map/mesh_sides/ppermute | solution.py:219
  5.2 12.1 %collective-permute-start = (bf16[16,512]{1,0:T(8,128)(2,1)}, bf16[16,512]{1,0:T(8,128)(2,1)S(1)}, u32[]{:S(2)}, u32[]{:S(2)}) collective-permute-start(bf16[16,512]{1,0:T(8,128)(2,1)} %mesh_ref.1), channel_id=1, source_target_pairs={{0,4},{4,0},{8,12},{12,8},{16,20},{20,16},{24,28},{28,24},{32,36},... | collective-permute-start | bytes 49160 | tf_op jit(solution)/shard_map/mesh_sides/ppermute | solution.py:220
  17.4 1.1 %pack.1 = bf16[192,512]{1,0:T(8,128)(2,1)S(1)} custom-call(bf16[128,512]{1,0:T(8,128)(2,1)} %grid_ref.5, bf16[16,512]{1,0:T(8,128)(2,1)} %mesh_ref.1, s32[2,128]{1,0:T(2,128)} %bitcast.13, s32[6,16]{1,0:T(8,128)} %bitcast.12, s32[1,6]{1,0:T(1,128)} %far_ref.1), custom_call_target="tpu_custom_call" | custom-call | flops 4194304000 | bytes 8388608 | tf_op jit(solution)/shard_map/pack/pallas_call | solution.py:194
  18.5 0.0 collective-permute-done.1
  18.5 0.0 collective-permute-done
  18.6 0.0 slice-start
  18.6 11.7 %all_gather.10.all_ref = bf16[4,192,512]{2,1,0:T(8,128)(2,1)S(1)} all-gather(bf16[1,192,512]{2,1,0:T(8,128)(2,1)S(1)} %fusion.1), channel_id=1, replica_groups=mesh['band'=256,'lon'=4] {'lon'}, dimensions={0}, use_global_device_ids=true | all-gather | bytes 983040 | tf_op jit(solution)/shard_map/gather_lon/all_gather | solution.py:240
  30.3 0.0 copy-done
  30.3 0.0 copy-start.2
  30.4 2.2 %encode.1 = (f32[192,512]{1,0:T(8,128)S(1)}, bf16[128,512]{1,0:T(8,128)(2,1)S(1)}, bf16[64,512]{1,0:T(8,128)(2,1)S(1)}, bf16[128,512]{1,0:T(8,128)(2,1)S(1)}) custom-call(bf16[4,192,512]{2,1,0:T(8,128)(2,1)S(1)} %all_gather.10.all_ref, bf16[3,3,512,512]{3,2,1,0:T(8,128)(2,1)S(1)} %copy-done), custom_call_target="tpu_custom_call" | custom-call | flops 4194304000 | bytes 8388608 | tf_op jit(solution)/shard_map/encode/pallas_call | solution.py:194
  32.5 5.0 %collective-permute-start.2 = (bf16[128,512]{1,0:T(8,128)(2,1)S(1)}, bf16[128,512]{1,0:T(8,128)(2,1)S(1)}, u32[]{:S(2)}, u32[]{:S(2)}) collective-permute-start(bf16[128,512]{1,0:T(8,128)(2,1)S(1)} %get-tuple-element.39), channel_id=1, source_target_pairs={{0,4},{4,0},{8,12},{12,8},{16,20},{20,16},{24,28},{28,24},{32,36},... | collective-permute-start | bytes 393224 | tf_op jit(solution)/shard_map/sum_pair/ppermute | solution.py:254
  37.5 1.3 %collective-permute-start.4 = (bf16[64,512]{1,0:T(8,128)(2,1)S(1)}, bf16[64,512]{1,0:T(8,128)(2,1)S(1)}, u32[]{:S(2)}, u32[]{:S(2)}) collective-permute-start(bf16[64,512]{1,0:T(8,128)(2,1)S(1)} %get-tuple-element.41), channel_id=1, source_target_pairs={{4,12},{12,20},{20,28},{28,36},{36,44},{44,52},{52,60},{60,68},{68... | collective-permute-start | bytes 196616 | tf_op jit(solution)/shard_map/sum_pair/ppermute | solution.py:255
  38.8 0.0 collective-permute-done.2.r1_ref
  38.8 4.2 %collective-permute-start.3 = (bf16[128,512]{1,0:T(8,128)(2,1)S(1)}, bf16[128,512]{1,0:T(8,128)(2,1)S(1)}, u32[]{:S(2)}, u32[]{:S(2)}) collective-permute-start(bf16[128,512]{1,0:T(8,128)(2,1)S(1)} %fusion), channel_id=1, source_target_pairs={{4,8},{8,4},{12,16},{16,12},{20,24},{24,20},{28,32},{32,28},{36,40... | collective-permute-start | bytes 393224 | tf_op jit(solution)/shard_map/sum_cross/ppermute | solution.py:258
  43.0 0.0 collective-permute-done.4.far_ref.after_ref
  43.1 0.3 decode_first.1
  43.4 0.8 %process_first.1 = (f32[128,512]{1,0:T(8,128)S(1)}, bf16[64,512]{1,0:T(8,128)(2,1)S(1)}, bf16[416,256]{1,0:T(8,128)(2,1)S(1)}) custom-call(bf16[4,192,512]{2,1,0:T(8,128)(2,1)S(1)} %all_gather.10.all_ref, f32[192,512]{1,0:T(8,128)S(1)} %get-tuple-element.38.acc_ref, bf16[128,512]{1,0:T(8,128)(2,1)S(1)} %collective-permute-done.2.r1_ref, ...), custom_call_target="tpu_custom_call" | custom-call | flops 524288000 | bytes 8388608 | tf_op jit(solution)/shard_map/process_first/pallas_call | solution.py:194
  44.3 1.4 %collective-permute-done.3.r2_ref = bf16[128,512]{1,0:T(8,128)(2,1)S(1)} collective-permute-done((bf16[128,512]{1,0:T(8,128)(2,1)S(1)}, bf16[128,512]{1,0:T(8,128)(2,1)S(1)}, u32[]{:S(2)}, u32[]{:S(2)}) %collective-permute-start.3) | collective-permute-done | bytes 131104 | tf_op jit(solution)/shard_map/sum_cross/ppermute | solution.py:258
  45.6 2.7 %process.1 = (bf16[64,512]{1,0:T(8,128)(2,1)S(1)}, bf16[16,512]{1,0:T(8,128)(2,1)}) custom-call(f32[192,512]{1,0:T(8,128)S(1)} %get-tuple-element.38.acc_ref, bf16[128,512]{1,0:T(8,128)(2,1)S(1)} %collective-permute-done.2.r1_ref, bf16[128,512]{1,0:T(8,128)(2,1)S(1)} %collective-permute-done.3.r2_ref, bf16[64,512]{1,0:T(8,128)(2,1)S(1)} %get-tuple-element.42.send_ref, ...), custom_call_target="tpu_custom_call" | custom-call | flops 4194304000 | bytes 8388608 | tf_op jit(solution)/shard_map/process/pallas_call | solution.py:194
  48.3 3.6 %collective-permute-start.6 = (bf16[64,512]{1,0:T(8,128)(2,1)S(1)}, bf16[64,512]{1,0:T(8,128)(2,1)S(1)}, u32[]{:S(2)}, u32[]{:S(2)}) collective-permute-start(bf16[64,512]{1,0:T(8,128)(2,1)S(1)} %get-tuple-element.46.own_ref), channel_id=1, source_target_pairs={{4,8},{8,4},{12,16},{16,12},{20,24},{24,20},{28,32},{32,28},{36,40... | collective-permute-start | bytes 196616 | tf_op jit(solution)/shard_map/two_sides/ppermute | solution.py:219
  52.0 1.9 %collective-permute-start.5 = (bf16[64,512]{1,0:T(8,128)(2,1)S(1)}, bf16[64,512]{1,0:T(8,128)(2,1)S(1)}, u32[]{:S(2)}, u32[]{:S(2)}) collective-permute-start(bf16[64,512]{1,0:T(8,128)(2,1)S(1)} %get-tuple-element.46.own_ref), channel_id=1, source_target_pairs={{0,4},{4,0},{8,12},{12,8},{16,20},{20,16},{24,28},{28,24},{32,36},... | collective-permute-start | bytes 196616 | tf_op jit(solution)/shard_map/two_sides/ppermute | solution.py:220
  53.9 0.0 collective-permute-done.6.cross_ref
  53.9 1.2 %collective-permute-done.5.pair_ref = bf16[64,512]{1,0:T(8,128)(2,1)S(1)} collective-permute-done((bf16[64,512]{1,0:T(8,128)(2,1)S(1)}, bf16[64,512]{1,0:T(8,128)(2,1)S(1)}, u32[]{:S(2)}, u32[]{:S(2)}) %collective-permute-start.5) | collective-permute-done | bytes 65568 | tf_op jit(solution)/shard_map/two_sides/ppermute | solution.py:220
  55.1 2.1 %decode.1 = bf16[128,512]{1,0:T(8,128)(2,1)} custom-call(bf16[128,512]{1,0:T(8,128)(2,1)S(1)} %copy-done.1, bf16[64,512]{1,0:T(8,128)(2,1)S(1)} %get-tuple-element.46.own_ref, bf16[64,512]{1,0:T(8,128)(2,1)S(1)} %collective-permute-done.5.pair_ref, bf16[64,512]{1,0:T(8,128)(2,1)S(1)} %collective-permute-done.6.cross_ref, ...), custom_call_target="tpu_custom_call" | custom-call | flops 4194304000 | bytes 8388608 | tf_op jit(solution)/shard_map/decode/pallas_call | solution.py:194
  (10 shorter events, 0.0 us)
Async XLA Ops:
  0.6 17.9 %collective-permute-start.1 = (bf16[16,512]{1,0:T(8,128)(2,1)}, bf16[16,512]{1,0:T(8,128)(2,1)S(1)}, u32[]{:S(2)}, u32[]{:S(2)}) collective-permute-start(bf16[16,512]{1,0:T(8,128)(2,1)} %mesh_ref.1), channel_id=1, source_target_pairs={{4,8},{8,4},{12,16},{16,12},{20,24},{24,20},{28,32},{32,28},{36,40... | collective-permute-start | bytes 49160 | tf_op jit(solution)/shard_map/mesh_sides/ppermute | solution.py:219
  5.2 13.3 %collective-permute-start = (bf16[16,512]{1,0:T(8,128)(2,1)}, bf16[16,512]{1,0:T(8,128)(2,1)S(1)}, u32[]{:S(2)}, u32[]{:S(2)}) collective-permute-start(bf16[16,512]{1,0:T(8,128)(2,1)} %mesh_ref.1), channel_id=1, source_target_pairs={{0,4},{4,0},{8,12},{12,8},{16,20},{20,16},{24,28},{28,24},{32,36},... | collective-permute-start | bytes 49160 | tf_op jit(solution)/shard_map/mesh_sides/ppermute | solution.py:220
  17.4 13.0 %copy-start = (bf16[3,3,512,512]{3,2,1,0:T(8,128)(2,1)S(1)}, bf16[3,3,512,512]{3,2,1,0:T(8,128)(2,1)}, u32[]{:S(2)}) copy-start(bf16[3,3,512,512]{3,2,1,0:T(8,128)(2,1)} %ew_ref.9) | copy-start | bytes 14155780
  18.6 24.5 %slice-start = ((s8[4718592]{0:T(1024)(128)(4,1)}), s8[4194304]{0:T(1024)(128)(4,1)S(1)}, s32[]{:S(2)}) async-start(s8[4718592]{0:T(1024)(128)(4,1)} %bitcast.8), calls=%async_computation | async-start | bytes 8388608
  30.3 12.7 %slice-start.1 = ((s8[4718592]{0:T(1024)(128)(4,1)}), s8[524288]{0:T(1024)(128)(4,1)S(1)}, s32[]{:S(2)}) async-start(s8[4718592]{0:T(1024)(128)(4,1)} %bitcast.8), calls=%async_computation.1 | async-start | bytes 1048576
  30.3 12.7 %copy-start.1 = (bf16[128,512]{1,0:T(8,128)(2,1)S(1)}, bf16[128,512]{1,0:T(8,128)(2,1)}, u32[]{:S(2)}) copy-start(bf16[128,512]{1,0:T(8,128)(2,1)} %grid_ref.5) | copy-start | bytes 393220
  30.3 12.7 %copy-start.2 = (s32[128,3]{0,1:T(4,128)S(1)}, s32[128,3]{0,1:T(4,128)}, u32[]{:S(2)}) copy-start(s32[128,3]{0,1:T(4,128)} %param.19) | copy-start | bytes 4612
  32.5 6.3 %collective-permute-start.2 = (bf16[128,512]{1,0:T(8,128)(2,1)S(1)}, bf16[128,512]{1,0:T(8,128)(2,1)S(1)}, u32[]{:S(2)}, u32[]{:S(2)}) collective-permute-start(bf16[128,512]{1,0:T(8,128)(2,1)S(1)} %get-tuple-element.39), channel_id=1, source_target_pairs={{0,4},{4,0},{8,12},{12,8},{16,20},{20,16},{24,28},{28,24},{32,36},... | collective-permute-start | bytes 393224 | tf_op jit(solution)/shard_map/sum_pair/ppermute | solution.py:254
  37.5 5.5 %collective-permute-start.4 = (bf16[64,512]{1,0:T(8,128)(2,1)S(1)}, bf16[64,512]{1,0:T(8,128)(2,1)S(1)}, u32[]{:S(2)}, u32[]{:S(2)}) collective-permute-start(bf16[64,512]{1,0:T(8,128)(2,1)S(1)} %get-tuple-element.41), channel_id=1, source_target_pairs={{4,12},{12,20},{20,28},{28,36},{36,44},{44,52},{52,60},{60,68},{68... | collective-permute-start | bytes 196616 | tf_op jit(solution)/shard_map/sum_pair/ppermute | solution.py:255
  38.8 6.8 %collective-permute-start.3 = (bf16[128,512]{1,0:T(8,128)(2,1)S(1)}, bf16[128,512]{1,0:T(8,128)(2,1)S(1)}, u32[]{:S(2)}, u32[]{:S(2)}) collective-permute-start(bf16[128,512]{1,0:T(8,128)(2,1)S(1)} %fusion), channel_id=1, source_target_pairs={{4,8},{8,4},{12,16},{16,12},{20,24},{24,20},{28,32},{32,28},{36,40... | collective-permute-start | bytes 393224 | tf_op jit(solution)/shard_map/sum_cross/ppermute | solution.py:258
  48.3 5.6 %collective-permute-start.6 = (bf16[64,512]{1,0:T(8,128)(2,1)S(1)}, bf16[64,512]{1,0:T(8,128)(2,1)S(1)}, u32[]{:S(2)}, u32[]{:S(2)}) collective-permute-start(bf16[64,512]{1,0:T(8,128)(2,1)S(1)} %get-tuple-element.46.own_ref), channel_id=1, source_target_pairs={{4,8},{8,4},{12,16},{16,12},{20,24},{24,20},{28,32},{32,28},{36,40... | collective-permute-start | bytes 196616 | tf_op jit(solution)/shard_map/two_sides/ppermute | solution.py:219
  52.0 3.1 %collective-permute-start.5 = (bf16[64,512]{1,0:T(8,128)(2,1)S(1)}, bf16[64,512]{1,0:T(8,128)(2,1)S(1)}, u32[]{:S(2)}, u32[]{:S(2)}) collective-permute-start(bf16[64,512]{1,0:T(8,128)(2,1)S(1)} %get-tuple-element.46.own_ref), channel_id=1, source_target_pairs={{0,4},{4,0},{8,12},{12,8},{16,20},{20,16},{24,28},{28,24},{32,36},... | collective-permute-start | bytes 196616 | tf_op jit(solution)/shard_map/two_sides/ppermute | solution.py:220
